TPU v7x, 32 devices: a whole 2x2x4 slice. The times are simulated.
32 devices in a mesh: groups: 2 (over x), dp: 2 (over core), mp: 8 (over z, y).
Axes of the slice: x: 2, y: 2, z: 4, core: 2. Of those that a mesh axis runs over, the one named last changes fastest.
Arguments:
- tokens: bfloat16 [16384, 8192], P(('groups', 'dp'), 'mp'), parts along dimension 0, may hold values from -6 to 6
- frozen_weight: bfloat16 [8192, 1024], P('mp'), may hold values from -0.09375 to 0.09375
- cotangent: bfloat16 [16384, 1024], P(('groups', 'dp'), 'mp'), parts along dimension 0, may hold values from -6 to 6
- adapter_down: bfloat16 [32, 8192, 64], P(('groups', 'dp', 'mp')), parts along dimension 0, may hold values from -0.0625 to 0.0625
- adapter_up: bfloat16 [32, 64, 1024], P(('groups', 'dp', 'mp')), parts along dimension 0, may hold values from -0.75 to 0.75
- seg_tiles: int32 [4, 24], P(('groups', 'dp')), parts along dimension 0, may hold values from 1 to 4, 32 in all within a row
- seg_adapter: int32 [96, 1], P(('groups', 'dp')), parts along dimension 0, may hold values from 0 to 15
- owner_slot: int32 [32], P('groups'), parts along dimension 0, may hold values from 0 to 15, each once
Outputs:
- output: bfloat16 [16384, 1024], P(('groups', 'dp'), 'mp'), parts along dimension 0
- token_gradient: bfloat16 [16384, 8192], P(('groups', 'dp'), 'mp'), parts along dimension 0
- down_gradient: float32 [32, 8192, 64], P(('groups', 'dp', 'mp')), parts along dimension 0
- up_gradient: float32 [32, 64, 1024], P(('groups', 'dp', 'mp')), parts along dimension 0
There are 2 independent parts, one for each index of `groups`. A program takes and returns all parts, laid end to end along the dimension named above; an argument that names none is the same for every part. Nothing has to cross between parts.
Inputs may be any that keep to these rules, and one draw needn't show every extreme that they name: `seg_tiles`: each row sums to 32; some segment has exactly 4 tiles. `seg_adapter`: every adapter is named by some segment. `owner_slot`: A permutation: each slot holds one adapter.
All inputs are finite; a program needn't handle non-finite values.
Results may differ from a plain program's by a relative error of at most 0.001.
Values may be sent and summed in bfloat16 or wider, within the bound.
No kernel may reach another device: no remote copies, remote signals or barrier semaphores. Data moves between devices by JAX's collectives and lax.ppermute only.
A program may use at most 192 MiB of HBM per device.

v0:
```python
import jax
import jax.numpy as jnp
from jax import lax
from jax.sharding import PartitionSpec as P

TILE = 128


ADAPTER_SCALE = 2.0
HIGH_ACCURACY = lax.Precision.HIGHEST


def body(
    tokens, frozen_weight, cotangent, adapter_down, adapter_up, seg_tiles, seg_adapter, owner_slot
):
    token_rows, width_local = tokens.shape
    output_local = cotangent.shape[1]
    n_model = lax.axis_size("mp")
    n_data = lax.axis_size("dp")
    slots_local, entire_width, adapter_rank = adapter_down.shape
    output_width = adapter_up.shape[2]
    slot_count = slots_local * n_data * n_model
    tile_count = token_rows // TILE
    ends = jnp.cumsum(seg_tiles[0])
    positions = jnp.arange(tile_count, dtype=jnp.int32)
    segment = jnp.sum((positions[:, None] >= ends[None, :]).astype(jnp.int32), axis=1)
    seg_pick = (segment[:, None] == jnp.arange(ends.shape[0], dtype=jnp.int32)[None, :]).astype(
        jnp.int32
    )
    tile_adapter = jnp.sum(seg_pick * seg_adapter[:, 0][None, :], axis=1)
    adapt_pick = (tile_adapter[:, None] == jnp.arange(slot_count, dtype=jnp.int32)[None, :]).astype(
        jnp.int32
    )
    tile_slot_index = jnp.sum(adapt_pick * owner_slot[None, :], axis=1)
    slot_pick = (
        tile_slot_index[:, None] == jnp.arange(slot_count, dtype=jnp.int32)[None, :]
    ).astype(jnp.float32)
    down_parts = jnp.transpose(
        adapter_down.reshape(slots_local, n_model, width_local * adapter_rank), (1, 0, 2)
    )
    up_parts = jnp.transpose(
        adapter_up.reshape(slots_local, adapter_rank, n_model, output_local), (2, 0, 1, 3)
    )
    up_parts = up_parts.reshape(n_model, slots_local, adapter_rank * output_local)
    got_down, got_up = (
        lax.all_to_all(down_parts, "mp", split_axis=0, concat_axis=0, tiled=True),
        lax.all_to_all(up_parts, "mp", split_axis=0, concat_axis=0, tiled=True),
    )
    got_down, got_up = (
        lax.all_gather(got_down, "dp", axis=0, tiled=True),
        lax.all_gather(got_up, "dp", axis=0, tiled=True),
    )
    down_slots = got_down.reshape(slot_count, width_local, adapter_rank)
    up_slots = got_up.reshape(slot_count, adapter_rank, output_local)
    down_weight_tiles = jnp.take(down_slots, tile_slot_index, axis=0)
    up_tiles = jnp.take(up_slots, tile_slot_index, axis=0)
    x_tiles = tokens.reshape(tile_count, TILE, width_local)
    g_tiles = cotangent.reshape(tile_count, TILE, output_local)
    shrink_part = jnp.einsum(
        "tkd,tdr->tkr", x_tiles, down_weight_tiles, preferred_element_type=jnp.float32
    )
    back_part = jnp.einsum("tko,tro->tkr", g_tiles, up_tiles, preferred_element_type=jnp.float32)
    shrink, backward_result = lax.psum((shrink_part, back_part), "mp")
    base_part = jnp.dot(tokens, frozen_weight, preferred_element_type=jnp.float32)
    base_output = lax.psum_scatter(base_part, "mp", scatter_dimension=1, tiled=True)
    raised_rows = jnp.einsum(
        "tkr,tro->tko", shrink, up_tiles.astype(jnp.float32), precision=HIGH_ACCURACY
    )
    output = (base_output + ADAPTER_SCALE * raised_rows.reshape(token_rows, output_local)).astype(
        jnp.bfloat16
    )
    base_gradient = lax.dot_general(
        lax.all_gather(cotangent, "mp", axis=1, tiled=True),
        frozen_weight,
        (((1,), (1,)), ((), ())),
        preferred_element_type=jnp.float32,
    )
    adapter_gradient = jnp.einsum(
        "lcu,lwu->lcw",
        backward_result,
        down_weight_tiles.astype(jnp.float32),
        precision=HIGH_ACCURACY,
    )
    token_gradient = (
        base_gradient + ADAPTER_SCALE * adapter_gradient.reshape(token_rows, width_local)
    ).astype(jnp.bfloat16)
    tile_down_weight = jnp.einsum(
        "tkd,tkr->tdr", x_tiles.astype(jnp.float32), backward_result, precision=HIGH_ACCURACY
    )
    tile_up_weight = jnp.einsum(
        "tkr,tko->tro", shrink, g_tiles.astype(jnp.float32), precision=HIGH_ACCURACY
    )
    grad_down_part = jnp.dot(
        slot_pick.T,
        tile_down_weight.reshape(tile_count, width_local * adapter_rank),
        precision=HIGH_ACCURACY,
    )
    grad_up_part = jnp.dot(
        slot_pick.T,
        tile_up_weight.reshape(tile_count, adapter_rank * output_local),
        precision=HIGH_ACCURACY,
    )
    send_down = grad_down_part.reshape(n_data * n_model, slots_local, width_local * adapter_rank)
    send_up = grad_up_part.reshape(n_data * n_model, slots_local, adapter_rank * output_local)
    got_down, got_up = (
        lax.all_to_all(send_down, ("dp", "mp"), split_axis=0, concat_axis=0, tiled=True),
        lax.all_to_all(send_up, ("dp", "mp"), split_axis=0, concat_axis=0, tiled=True),
    )
    got_down = jnp.sum(
        got_down.reshape(n_data, n_model, slots_local, width_local * adapter_rank), axis=0
    )
    got_up = jnp.sum(
        got_up.reshape(n_data, n_model, slots_local, adapter_rank * output_local), axis=0
    )
    down_gradient = jnp.transpose(
        got_down.reshape(n_model, slots_local, width_local, adapter_rank), (1, 0, 2, 3)
    )
    down_gradient = ADAPTER_SCALE * down_gradient.reshape(slots_local, entire_width, adapter_rank)
    up_gradient = jnp.transpose(
        got_up.reshape(n_model, slots_local, adapter_rank, output_local), (1, 2, 0, 3)
    )
    up_gradient = ADAPTER_SCALE * up_gradient.reshape(slots_local, adapter_rank, output_width)
    return (output, token_gradient, down_gradient, up_gradient)


def solution(mesh):
    placed = (
        P(("groups", "dp"), "mp"),
        P("mp", None),
        P(("groups", "dp"), "mp"),
        P(("groups", "dp", "mp"), None, None),
        P(("groups", "dp", "mp"), None, None),
        P(("groups", "dp"), None),
        P(("groups", "dp"), None),
        P("groups"),
    )
    return jax.shard_map(
        body,
        mesh=mesh,
        in_specs=placed,
        out_specs=(
            P(("groups", "dp"), "mp"),
            P(("groups", "dp"), "mp"),
            P(("groups", "dp", "mp"), None, None),
            P(("groups", "dp", "mp"), None, None),
        ),
        check_vma=False,
    )
```

profile of v0, /device:TPU:0, one launch (start us, length us, event | category | flops | bytes accessed | tf_op | source)
XLA Modules:
  0.0 717.3 jit_solution(130594045415051993)
XLA Ops:
  7.2 2.9 copy.42
  10.1 6.2 transpose_reshape.4
  16.8 8.4 %reduce.3 = bf16[8,65536]{1,0:T(8,128)(2,1)S(1)} reduce(bf16[8,1,65536]{2,1,0:T(2,128)(2,1)} %transpose_reshape.4, bf16[]{:T(256)} %broadcast.73), dimensions={1}, to_apply=%transpose_reshape.4.reduce_sub_computation | reduce | bytes 2097154 | tf_op jit(solution)/shard_map/transpose;reshape | solution.py:38
  27.0 33.0 %all_to_all.20 = bf16[8,2,32768]{2,1,0:T(2,128)(2,1)S(1)} all-to-all(bf16[8,2,32768]{2,1,0:T(2,128)(2,1)} %reshape.165), channel_id=1, replica_groups=mesh['groups'=2,'dp'=2,'mp'=8] {'mp'}, dimensions={0} | all-to-all | bytes 2097152 | tf_op jit(solution)/shard_map/all_to_all | solution.py:46
  60.1 3.4 reshape.166
  63.5 3.8 copy.44
  69.6 3.6 all-to-all-start.1
  73.8 6.7 all-to-all-done.1
  80.8 2.5 all_gather.10
  84.8 2.9 convolution_bitcast_fusion.3
  87.7 6.4 reshape.135
  94.1 4.8 copy.45
  98.8 4.3 gather_fusion
  103.1 8.7 %fusion.3 = f32[32,128,64]{1,2,0:T(8,128)} fusion(bf16[32,128,1024]{2,1,0:T(8,128)(2,1)} %bitcast.70, bf16[32,1024,64]{1,2,0:T(8,128)(2,1)} %gather_fusion, pred[32]{0:T(512)(128)(4,1)S(1)} %compare_and_fusion), kind=kOutput, calls=%fused_computation.14 | convolution fusion | flops 538968064 | bytes 13631520 | tf_op jit(solution)/shard_map/tkd,tdr->tkr/dot_general | solution.py:59
  112.7 14.5 %fusion.13 = f32[4096,1024]{1,0:T(8,128)} fusion(bf16[4096,1024]{1,0:T(8,128)(2,1)} %param.8, bf16[1024,1024]{1,0:T(8,128)(2,1)S(1)} %copy-done), kind=kOutput, calls=%fused_computation.41 | convolution fusion | flops 8589934592 | bytes 27262976 | tf_op jit(solution)/shard_map/dot_general | solution.py:64
  127.2 84.7 %all-reduce.3.cloned.1.call-done = (f32[32,128,64]{1,2,0:T(8,128)}, f32[32,128,64]{1,2,0:T(8,128)}) async-done(((f32[32,128,64]{1,2,0:T(8,128)}, f32[32,128,64]{1,2,0:T(8,128)}), (f32[32,128,64]{1,2,0:T(8,128)}, f32[32,128,64]{1,2,0:T(8,128)})) %all-reduce.3.cloned.1.call-update) | async-done | bytes 2097168 | tf_op jit(solution)/shard_map/psum | solution.py:63
  216.6 4.7 all-to-all-start.3
  221.3 8.3 %convolution_bitcast_fusion.2 = f32[32,1024,64]{1,2,0:T(8,128)} fusion(f32[32,128,64]{1,2,0:T(8,128)S(1)} %copy-done.3, bf16[32,128,1024]{2,1,0:T(8,128)(2,1)} %bitcast.71), kind=kOutput, calls=%fused_computation.9 | convolution fusion | flops 3221225472 | bytes 17825792 | tf_op jit(solution)/shard_map/tkd,tkr->tdr/dot_general | solution.py:87
  229.5 12.2 %copy.49 = f32[32,1024,64]{2,1,0:T(8,128)} copy(f32[32,1024,64]{1,2,0:T(8,128)} %convolution_bitcast_fusion.2) | data formatting | bytes 16777216 | tf_op jit(solution)/shard_map/tkd,tkr->tdr/dot_general | solution.py:87
  241.7 10.9 %reshape.141 = f32[32,65536]{1,0:T(8,128)} reshape(f32[32,1024,64]{2,1,0:T(8,128)} %copy.49) | data formatting | bytes 16777216 | tf_op jit(solution)/shard_map/reshape | solution.py:95
  252.7 5.6 convolution_bitcast_fusion
  258.3 6.3 copy.50
  264.6 6.5 all-to-all-start.2
  271.2 4.6 convolution_multiply_fusion.1
  275.8 12.0 %convolution_multiply_fusion = f32[32,128,1024]{2,1,0:T(8,128)} fusion(f32[32,128,64]{1,2,0:T(8,128)S(1)} %copy-done.4, bf16[32,1024,64]{1,2,0:T(8,128)(2,1)} %gather_fusion, pred[32]{0:T(512)(128)(4,1)S(1)} %compare_and_fusion), kind=kOutput, calls=%fused_computation.5 | convolution fusion | flops 3227516928 | bytes 22020128 | tf_op jit(solution)/shard_map/lcu,lwu->lcw/dot_general | solution.py:78
  289.9 138.3 %all-to-all-done.2 = f32[16,1,65536]{2,1,0:T(1,128)} async-done(((f32[16,1,65536]{2,1,0:T(1,128)}), f32[16,1,65536]{2,1,0:T(1,128)}, u32[]{:S(2)}, u32[]{:S(2)}) %all-to-all-start.2) | async-done | bytes 4194336 | tf_op jit(solution)/shard_map/all_to_all | solution.py:106
  428.3 4.7 bitcast_reduce_fusion
  434.4 5.3 mul.89
  439.7 3.8 copy.52
  443.5 17.3 %fusion = bf16[4096,1024]{1,0:T(8,128)(2,1)} fusion(f32[32,128,1024]{2,1,0:T(8,128)} %convolution_multiply_fusion, bf16[4096,1024]{1,0:T(8,128)(2,1)} %all-gather.5.cloned.1.call-done, bf16[1024,1024]{1,0:T(8,128)(2,1)S(1)} %copy-done), kind=kOutput, calls=%fused_computation.4 | convolution fusion | flops 8598323200 | bytes 35651584 | tf_op jit(solution)/shard_map/dot_general | solution.py:72
  460.8 246.2 %reduce-scatter.2.cloned.1.call-done = f32[4096,128]{1,0:T(8,128)} async-done(((f32[4096,1024]{1,0:T(8,128)}), f32[4096,128]{1,0:T(8,128)}) %reduce-scatter.2.cloned.1.call-update) | async-done | bytes 2097168 | tf_op jit(solution)/shard_map/reduce_scatter | solution.py:65
  706.9 3.4 fusion.1
  (55 shorter events, 16.0 us)
Async XLA Ops:
  7.2 105.5 %copy-start = (bf16[1024,1024]{1,0:T(8,128)(2,1)S(1)}, bf16[1024,1024]{1,0:T(8,128)(2,1)}, u32[]{:S(2)}) copy-start(bf16[1024,1024]{1,0:T(8,128)(2,1)} %param.9) | copy-start | bytes 6291460
  7.2 80.5 %all-gather.3.cloned.1.call-start = ((), (), s32[]{:S(2)}) async-start(), calls=%async_computation.6 | async-start | bytes 3145728 | tf_op jit(solution)/shard_map/all_gather | solution.py:50
  60.1 7.3 %copy-start.5 = (bf16[1,64,1024]{2,1,0:T(8,128)(2,1)S(1)}, bf16[1,64,1024]{2,1,0:T(8,128)(2,1)}, u32[]{:S(2)}) copy-start(bf16[1,64,1024]{2,1,0:T(8,128)(2,1)} %param.12) | copy-start | bytes 393220
  60.1 13.2 %copy-start.6 = (s32[1,24]{1,0:T(1,128)S(1)}, s32[1,24]{1,0:T(1,128)}, u32[]{:S(2)}) copy-start(s32[1,24]{1,0:T(1,128)} %param.13) | copy-start | bytes 292
  60.1 13.5 %copy-start.7 = (s32[24,1]{0,1:T(1,128)S(1)}, s32[24,1]{0,1:T(1,128)}, u32[]{:S(2)}) copy-start(s32[24,1]{0,1:T(1,128)} %param.14) | copy-start | bytes 292
  60.1 13.6 %copy-start.8 = (s32[16]{0:T(128)S(1)}, s32[16]{0:T(128)}, u32[]{:S(2)}) copy-start(s32[16]{0:T(128)} %param.15) | copy-start | bytes 196
  63.5 21.2 %copy-start.1 = (bf16[4096,128]{1,0:T(8,128)(2,1)S(1)}, bf16[4096,128]{1,0:T(8,128)(2,1)}, u32[]{:S(2)}) copy-start(bf16[4096,128]{1,0:T(8,128)(2,1)} %param.10) | copy-start | bytes 3145732
  69.6 10.9 %all-to-all-start.1 = ((bf16[8,2,4096]{2,1,0:T(2,128)(2,1)}), bf16[8,2,4096]{2,1,0:T(2,128)(2,1)S(1)}, u32[]{:S(2)}, u32[]{:S(2)}) async-start(bf16[8,2,4096]{2,1,0:T(2,128)(2,1)} %reshape.167), calls=%async_computation.2 | async-start | bytes 262144 | tf_op jit(solution)/shard_map/all_to_all | solution.py:47
  73.2 138.7 %all-reduce.3.cloned.1.call-start = ((), (), s32[]{:S(2)}) async-start(), calls=%async_computation.8 | async-start | bytes 4194304 | tf_op jit(solution)/shard_map/psum | solution.py:63
  111.9 331.6 %all-gather.5.cloned.1.call-start = ((), (), s32[]{:S(2)}) async-start(), calls=%async_computation.7 | async-start | bytes 9437184 | tf_op jit(solution)/shard_map/all_gather | solution.py:73
  112.6 594.3 %reduce-scatter.2.cloned.1.call-start = ((), (), s32[]{:S(2)}) async-start(), calls=%async_computation.5 | async-start | bytes 18874368 | tf_op jit(solution)/shard_map/reduce_scatter | solution.py:65
  127.1 84.8 %copy-start.2 = (bf16[4096,128]{1,0:T(8,128)(2,1)S(1)}, bf16[4096,128]{1,0:T(8,128)(2,1)}, u32[]{:S(2)}) copy-start(bf16[4096,128]{1,0:T(8,128)(2,1)} %param.10) | copy-start | bytes 3145732
  214.1 7.2 copy-start.3
  216.6 48.1 %all-to-all-start.3 = ((f32[16,1,8192]{2,1,0:T(1,128)}), f32[16,1,8192]{2,1,0:T(1,128)}, u32[]{:S(2)}, u32[]{:S(2)}) async-start(f32[16,1,8192]{2,1,0:T(1,128)} %copy.51), calls=%async_computation.4 | async-start | bytes 1048576 | tf_op jit(solution)/shard_map/all_to_all | solution.py:107
  264.6 11.2 %copy-start.4 = (f32[32,128,64]{1,2,0:T(8,128)S(1)}, f32[32,128,64]{1,2,0:T(8,128)}, u32[]{:S(2)}) copy-start(f32[32,128,64]{1,2,0:T(8,128)} %get-tuple-element.21) | copy-start | bytes 3145732
  264.6 163.6 %all-to-all-start.2 = ((f32[16,1,65536]{2,1,0:T(1,128)}), f32[16,1,65536]{2,1,0:T(1,128)}, u32[]{:S(2)}, u32[]{:S(2)}) async-start(f32[16,1,65536]{2,1,0:T(1,128)} %copy.50), calls=%async_computation.3 | async-start | bytes 8388608 | tf_op jit(solution)/shard_map/all_to_all | solution.py:106
Sparse Core Ops, SparseCore 0:
  67.5 9.5 all-gather.2
  112.0 99.8 all-reduce.2
  214.0 208.4 all-gather.4
  426.1 280.7 reduce-scatter.1
where the time goes:
time: 726 us; the launch traced here: 717 us
  waiting for transfers between devices  477 us (66%)
  local copies, waits for them, and re-layouts  77.4 us (11%)
  matrix products  77.1 us (11%)
  blocking collectives  35.5 us (5%)
  other arithmetic  21.2 us (3%)
  starting transfers between devices  14.9 us (2%)
  between operations  14.4 us (2%)
    reduce_scatter x1, waiting for transfers between devices, body(): lax.psum_scatter(base_part, 'mp', scatter_dimension=1, tiled=True)  246 us
    all_to_all x1, waiting for transfers between devices, body(): lax.all_to_all(send_down, ('dp', 'mp'), split_axis=0, concat_axis=0, tile...  138 us
    psum x1, waiting for transfers between devices, body(): shrink, backward_result = lax.psum((shrink_part, back_part), 'mp')  84.7 us
    all_to_all x1, blocking collectives, body(): lax.all_to_all(down_parts, 'mp', split_axis=0, concat_axis=0, tiled=True)  33 us
    dot_general x1, matrix products, body(): lax.dot_general(lax.all_gather(cotangent, 'mp', axis=1, tiled=True), froz...  17.3 us
  transfers between devices with their start and end apart: 7, of which 4 were waited for; matrix products, arithmetic and copies ran while one was open for 17% of the time, Pallas kernels for 0%

commit v1 on v0

v1 whole, which is shorter than its diff:
```python
import functools

import jax
import jax.numpy as jnp
from jax import lax
from jax.experimental import pallas as pl
from jax.experimental.pallas import tpu as pltpu
from jax.sharding import PartitionSpec as P

TILE = 128
ADAPTER_SCALE = 2.0
INNER = 2
PAD = 16
TOP = 32700.0
STEPS = 64.0
TINY = 1e-30
VMEM = 60 * 1024 * 1024
F32 = jnp.float32
BF16 = jnp.bfloat16
NT = (((1,), (1,)), ((), ()))
TN = (((0,), (0,)), ((), ()))


def dot(a, b, dims=(((1,), (0,)), ((), ()))):
    return lax.dot_general(a, b, dims, preferred_element_type=F32)


def split_halves(twice, rank):
    high = twice.astype(BF16).astype(F32)
    lane = lax.broadcasted_iota(jnp.int32, twice.shape, 1)
    return jnp.where(lane < rank, high, twice - high).astype(BF16)


def encode(v):
    most = jnp.max(jnp.abs(v), axis=0, keepdims=True)
    code = jnp.ceil(jnp.log2(jnp.maximum(most, TINY)) * STEPS)
    gain = jnp.exp2(code * (-1.0 / STEPS)) * TOP
    return jnp.round(v * gain).astype(jnp.int32).astype(jnp.int16), code


def step_of(code):
    return jnp.exp2(code.astype(jnp.int32).astype(F32) * (1.0 / STEPS)) * (1.0 / TOP)


def decode(q, code):
    return q.astype(jnp.int32).astype(F32) * step_of(code)


def turn_kernel(in_ref, out_ref):
    out_ref[0] = in_ref[0].T


def forward_kernel(slot_ref, x_ref, w_ref, down_ref, up_ref, part_ref, split_ref):
    step = pl.program_id(0)
    n, rows, cols = part_ref.shape
    tiles = rows // TILE
    rank = down_ref.shape[1] // 2
    base = dot(x_ref[...], w_ref[...])
    for t in range(tiles):
        at = slice(t * TILE, (t + 1) * TILE)
        slot = slot_ref[step * tiles + t]
        pieces = split_halves(dot(x_ref[at, :], down_ref[slot], NT), rank)
        split_ref[at, :] = pieces
        total = base[at] + ADAPTER_SCALE * dot(pieces, up_ref[slot])
        for j in range(n):
            part_ref[j, at, :] = total[:, j * cols : (j + 1) * cols]


def backward_kernel(blocks, slot_ref, place_ref, *refs):
    cots = refs[:blocks]
    x_ref, w_ref, down_ref, up_ref, split_ref, tg_ref, gdown_ref, gup_ref, cot_ref = refs[blocks:]
    step = pl.program_id(0)
    rows = x_ref.shape[0]
    tiles = rows // TILE
    rank = down_ref.shape[1] // 2

    @pl.when(step == 0)
    def _():
        gdown_ref[...] = jnp.zeros_like(gdown_ref)
        gup_ref[...] = jnp.zeros_like(gup_ref)

    if blocks == 1:
        cot_ref[...] = cots[0][...]
    else:
        for j, block in enumerate(cots):
            wide = block.shape[1]
            cot_ref[:, pl.ds(pl.multiple_of(place_ref[j] * wide, wide), wide)] = block[...]
    base = dot(cot_ref[...], w_ref[...], NT)
    for t in range(tiles):
        at = slice(t * TILE, (t + 1) * TILE)
        slot = slot_ref[step * tiles + t]
        cot = cot_ref[at, :]
        pieces = split_halves(dot(cot, up_ref[slot], NT), rank)
        tg_ref[at, :] = (base[at] + ADAPTER_SCALE * dot(pieces, down_ref[slot])).astype(BF16)
        grad = dot(pieces, x_ref[at, :], TN)
        gdown_ref[slot] += grad[:rank] + grad[rank:]
        grad = dot(split_ref[at, :], cot, TN)
        gup_ref[slot] += grad[:rank] + grad[rank:]


def sum_kernel(coded, block_rows, pick_ref, *refs):
    total = refs[0][0]
    for ref in refs[1 : 1 + coded]:
        total = total + decode(ref[0, 0, :block_rows, :], ref[0, 0, block_rows : block_rows + 1, :])
    out_ref = refs[-1]
    if out_ref.dtype == BF16:
        out_ref[...] = total.astype(BF16)
    else:
        q, code = encode(total)
        out_ref[0, 0, :block_rows, :] = q
        out_ref[0, 0, block_rows:, :] = jnp.broadcast_to(code, (PAD, code.shape[1])).astype(jnp.int32).astype(jnp.int16)


def add_parts(part, part_picks, coded, coded_picks, first, blocks, block_rows, last):
    n, rows, cols = part.shape
    count = len(part_picks)
    picks = jnp.stack([jnp.stack([jnp.asarray(i, jnp.int32) for i in p]) for p in (part_picks, *coded_picks)])

    def spec(k):
        return pl.BlockSpec((1, 1, block_rows + PAD, cols), lambda i, b, pick: (pick[k, i], b, 0, 0))

    in_specs = [pl.BlockSpec((1, block_rows, cols), lambda i, b, pick: (pick[0, i], first + b, 0))]
    in_specs += [spec(k + 1) for k in range(len(coded))]
    if last:
        out_shape = jax.ShapeDtypeStruct((blocks * block_rows, cols), BF16)
        out_spec = pl.BlockSpec((block_rows, cols), lambda i, b, pick: (b, 0))
    else:
        out_shape = jax.ShapeDtypeStruct((count, blocks, block_rows + PAD, cols), jnp.int16)
        out_spec = pl.BlockSpec((1, 1, block_rows + PAD, cols), lambda i, b, pick: (i, b, 0, 0))
    values = count * blocks * block_rows * cols
    return pl.pallas_call(
        functools.partial(sum_kernel, len(coded), block_rows),
        grid_spec=pltpu.PrefetchScalarGridSpec(
            num_scalar_prefetch=1, grid=(count, blocks), in_specs=in_specs, out_specs=out_spec
        ),
        out_shape=out_shape,
        cost_estimate=pl.CostEstimate(flops=0, bytes_accessed=values * (6 + 2 * len(coded)), transcendentals=0),
        name="add_parts",
    )(picks, part, *coded)


def pack_kernel(gdown_ref, rdown_ref, gup_ref, rup_ref, out_ref):
    rank, width = gdown_ref.shape[1:]
    groups = gup_ref.shape[2] // width
    row = lax.broadcasted_iota(jnp.int32, (PAD, width), 0)
    codes = jnp.zeros((PAD, width), F32)
    down = gdown_ref[0] + rdown_ref[0]
    for g in range(groups + 1):
        if g == 0:
            v = down
        else:
            at = slice((g - 1) * width, g * width)
            v = gup_ref[0, :, at] + rup_ref[0, :, at]
        q, code = encode(v)
        out_ref[0, g * rank : (g + 1) * rank, :] = q
        codes = jnp.where(row == g, code, codes)
    out_ref[0, (groups + 1) * rank :, :] = codes.astype(jnp.int32).astype(jnp.int16)


def unpack_kernel(in_ref, down_ref, up_ref):
    rank = up_ref.shape[1]
    width = in_ref.shape[2]
    groups = up_ref.shape[2] // width

    @pl.when(pl.program_id(0) == 0)
    def _():
        up_ref[...] = jnp.zeros_like(up_ref)

    steps = ADAPTER_SCALE * step_of(in_ref[0, (groups + 1) * rank :, :])
    for g in range(groups + 1):
        v = in_ref[0, g * rank : (g + 1) * rank, :].astype(jnp.int32).astype(F32) * steps[g : g + 1]
        if g == 0:
            down_ref[0] = v.T
        else:
            up_ref[0, :, (g - 1) * width : g * width] += v


def body(
    tokens, frozen_weight, cotangent, adapter_down, adapter_up, seg_tiles, seg_adapter, owner_slot
):
    rows, width = tokens.shape
    cols = cotangent.shape[1]
    n = lax.axis_size("mp")
    n_data = lax.axis_size("dp")
    _, entire_width, rank = adapter_down.shape
    out_width = adapter_up.shape[2]
    slots = n_data * n
    tile_count = rows // TILE
    inner = INNER
    outer = n // inner
    me = lax.axis_index("mp")
    my_outer, my_inner = me // inner, me % inner
    other = 1 - my_inner
    my_data = lax.axis_index("dp")
    swap = [(i, i ^ 1) for i in range(n)]
    ring = [(i, (i + inner) % n) for i in range(n)]
    cores = [(i, 1 - i) for i in range(n_data)]

    cots, places = [], []
    block = cotangent
    for s in range(outer):
        at = ((my_outer - s) % outer) * inner
        cots += [block, lax.ppermute(block, "mp", swap)]
        places += [at + my_inner, at + other]
        if s < outer - 1:
            block = lax.ppermute(block, "mp", ring)

    turned = pl.pallas_call(
        turn_kernel,
        grid=(n,),
        in_specs=[pl.BlockSpec((1, width, rank), lambda i: (0, i, 0))],
        out_specs=pl.BlockSpec((1, rank, width), lambda i: (i, 0, 0)),
        out_shape=jax.ShapeDtypeStruct((n, rank, width), BF16),
        name="turn_down",
    )(adapter_down)
    down = lax.all_to_all(turned, "mp", split_axis=0, concat_axis=0, tiled=True)
    up = lax.all_gather(adapter_up, "mp", axis=0, tiled=True)
    down = jnp.concatenate([down, lax.ppermute(down, "dp", cores)], axis=0)
    up = jnp.concatenate([up, lax.ppermute(up, "dp", cores)], axis=0)
    down = jnp.concatenate([down, down], axis=1)
    up = jnp.concatenate([up, up], axis=1)

    ends = jnp.cumsum(seg_tiles[0])
    positions = jnp.arange(tile_count, dtype=jnp.int32)
    segment = jnp.sum((positions[:, None] >= ends[None, :]).astype(jnp.int32), axis=1)
    seg_pick = segment[:, None] == jnp.arange(ends.shape[0], dtype=jnp.int32)[None, :]
    tile_adapter = jnp.sum(jnp.where(seg_pick, seg_adapter[:, 0][None, :], 0), axis=1)
    adapt_pick = tile_adapter[:, None] == jnp.arange(slots, dtype=jnp.int32)[None, :]
    tile_slot = jnp.sum(jnp.where(adapt_pick, owner_slot[None, :], 0), axis=1)
    tile_slot = ((tile_slot // n + my_data) % n_data) * n + tile_slot % n

    block_rows = 4 * TILE
    steps = rows // block_rows
    once = pl.Buffered(1)
    part, split = pl.pallas_call(
        forward_kernel,
        grid_spec=pltpu.PrefetchScalarGridSpec(
            num_scalar_prefetch=1,
            grid=(steps,),
            in_specs=[
                pl.BlockSpec((block_rows, width), lambda i, s: (i, 0)),
                pl.BlockSpec((width, out_width), lambda i, s: (0, 0), pipeline_mode=once),
                pl.BlockSpec((slots, 2 * rank, width), lambda i, s: (0, 0, 0), pipeline_mode=once),
                pl.BlockSpec((slots, 2 * rank, out_width), lambda i, s: (0, 0, 0), pipeline_mode=once),
            ],
            out_specs=[
                pl.BlockSpec((n, block_rows, cols), lambda i, s: (0, i, 0)),
                pl.BlockSpec((block_rows, 2 * rank), lambda i, s: (i, 0)),
            ],
        ),
        out_shape=[
            jax.ShapeDtypeStruct((n, rows, cols), F32),
            jax.ShapeDtypeStruct((rows, 2 * rank), BF16),
        ],
        compiler_params=pltpu.CompilerParams(vmem_limit_bytes=VMEM),
        cost_estimate=pl.CostEstimate(
            flops=3 * rows * width * out_width, bytes_accessed=rows * (width * 2 + out_width * 4), transcendentals=0
        ),
        name="forward",
    )(tile_slot, tokens, frozen_weight, down, up)

    chunks = 4
    blocks = steps // chunks
    outs = []
    for c in range(chunks):
        add = functools.partial(add_parts, part, first=c * blocks, blocks=blocks, block_rows=block_rows)
        sent = add([z * inner + other for z in range(outer)], [], [], last=False)
        near = lax.ppermute(sent, "mp", swap)
        got, got_picks = [near], []
        for s in range(1, outer + 1):
            z = (my_outer - s) % outer
            coded_picks = [[z]] if s == 1 else [[z], [0]]
            total = add([z * inner + my_inner], got, coded_picks, last=s == outer)
            if s < outer:
                got = [near, lax.ppermute(total, "mp", ring)]
        outs.append(total)
    output = jnp.concatenate(outs, axis=0)

    if cols % 128:
        order = jnp.stack(cots)[jnp.argsort(jnp.stack(places))]
        cots = [jnp.transpose(order, (1, 0, 2)).reshape(rows, out_width)]
    token_gradient, gdown, gup = pl.pallas_call(
        functools.partial(backward_kernel, len(cots)),
        grid_spec=pltpu.PrefetchScalarGridSpec(
            num_scalar_prefetch=2,
            grid=(steps,),
            in_specs=[pl.BlockSpec((block_rows, a.shape[1]), lambda i, s, p: (i, 0)) for a in cots]
            + [
                pl.BlockSpec((block_rows, width), lambda i, s, p: (i, 0)),
                pl.BlockSpec((width, out_width), lambda i, s, p: (0, 0), pipeline_mode=once),
                pl.BlockSpec((slots, 2 * rank, width), lambda i, s, p: (0, 0, 0), pipeline_mode=once),
                pl.BlockSpec((slots, 2 * rank, out_width), lambda i, s, p: (0, 0, 0), pipeline_mode=once),
                pl.BlockSpec((block_rows, 2 * rank), lambda i, s, p: (i, 0)),
            ],
            out_specs=[
                pl.BlockSpec((block_rows, width), lambda i, s, p: (i, 0)),
                pl.BlockSpec((slots, rank, width), lambda i, s, p: (0, 0, 0), pipeline_mode=once),
                pl.BlockSpec((slots, rank, out_width), lambda i, s, p: (0, 0, 0), pipeline_mode=once),
            ],
            scratch_shapes=[pltpu.VMEM((block_rows, out_width), BF16)],
        ),
        out_shape=[
            jax.ShapeDtypeStruct((rows, width), BF16),
            jax.ShapeDtypeStruct((slots, rank, width), F32),
            jax.ShapeDtypeStruct((slots, rank, out_width), F32),
        ],
        compiler_params=pltpu.CompilerParams(vmem_limit_bytes=VMEM),
        cost_estimate=pl.CostEstimate(
            flops=4 * rows * width * out_width, bytes_accessed=rows * (width * 4 + out_width * 2), transcendentals=0
        ),
        name="backward",
    )(tile_slot, jnp.stack(places).astype(jnp.int32), *cots, tokens, frozen_weight, down, up, split)

    rdown = lax.ppermute(gdown[n:], "dp", cores)
    rup = lax.ppermute(gup[n:], "dp", cores)
    packed_rows = (1 + out_width // width) * rank + PAD
    packed = pl.pallas_call(
        pack_kernel,
        grid=(n,),
        in_specs=[
            pl.BlockSpec((1, rank, width), lambda i: (i, 0, 0)),
            pl.BlockSpec((1, rank, width), lambda i: (i, 0, 0)),
            pl.BlockSpec((1, rank, out_width), lambda i: (i, 0, 0)),
            pl.BlockSpec((1, rank, out_width), lambda i: (i, 0, 0)),
        ],
        out_specs=pl.BlockSpec((1, packed_rows, width), lambda i: (i, 0, 0)),
        out_shape=jax.ShapeDtypeStruct((n, packed_rows, width), jnp.int16),
        name="pack_gradients",
    )(gdown, rdown, gup, rup)
    packed = lax.all_to_all(packed, "mp", split_axis=0, concat_axis=0, tiled=True)
    down_gradient, up_gradient = pl.pallas_call(
        unpack_kernel,
        grid=(n,),
        in_specs=[pl.BlockSpec((1, packed_rows, width), lambda i: (i, 0, 0))],
        out_specs=[
            pl.BlockSpec((1, width, rank), lambda i: (0, i, 0)),
            pl.BlockSpec((1, rank, out_width), lambda i: (0, 0, 0)),
        ],
        out_shape=[
            jax.ShapeDtypeStruct((1, entire_width, rank), F32),
            jax.ShapeDtypeStruct((1, rank, out_width), F32),
        ],
        name="unpack_gradients",
    )(packed)
    return output, token_gradient, down_gradient, up_gradient


def solution(mesh):
    placed = (
        P(("groups", "dp"), "mp"),
        P("mp", None),
        P(("groups", "dp"), "mp"),
        P(("groups", "dp", "mp"), None, None),
        P(("groups", "dp", "mp"), None, None),
        P(("groups", "dp"), None),
        P(("groups", "dp"), None),
        P("groups"),
    )
    return jax.shard_map(
        body,
        mesh=mesh,
        in_specs=placed,
        out_specs=(
            P(("groups", "dp"), "mp"),
            P(("groups", "dp"), "mp"),
            P(("groups", "dp", "mp"), None, None),
            P(("groups", "dp", "mp"), None, None),
        ),
        check_vma=False,
    )
```

time: 726 us -> 474 us (0.65)
  waiting for transfers between devices: 477 us -> 233 us
  Pallas kernels: 0 us -> 148 us
  matrix products: 77.1 us -> 0 us
  local copies, waits for them, and re-layouts: 77.4 us -> 24.8 us
  blocking collectives: 35.5 us -> 0 us
  starting transfers between devices: 14.9 us -> 42.4 us
  other arithmetic: 21.2 us -> 10.1 us
    reduce_scatter x1 -> x0, waiting for transfers between devices: 246 us -> none  [body(): lax.psum_scatter(base_part, 'mp', scatter_dimension=1, tiled=True)]
    ppermute x0 -> x27, waiting for transfers between devices: none -> 189 us  [the longest x4 74.6 us: body(): near = lax.ppermute(sent, 'mp', swap)]
    pallas_call x0 -> x25, Pallas kernels: none -> 148 us  [the longest x20 68.4 us: add_parts(): pl.pallas_call(functools.partial(sum_kernel, len(coded), block_rows), gri...]
    all_to_all x3 -> x2, waiting for transfers between devices: 145 us -> 24.5 us  [the longest x1 24.5 us: body(): down = lax.all_to_all(turned, 'mp', split_axis=0, concat_axis=0, tiled=True)]
    psum x1 -> x0, waiting for transfers between devices: 84.7 us -> none  [body(): shrink, backward_result = lax.psum((shrink_part, back_part), 'mp')]
    dot_general x10 -> x0, matrix products: 77.1 us -> none  [the longest x1 17.3 us: body(): lax.dot_general(lax.all_gather(cotangent, 'mp', axis=1, tiled=True), froz...]
    all_to_all x1 -> x0, blocking collectives: 33 us -> none  [body(): lax.all_to_all(down_parts, 'mp', split_axis=0, concat_axis=0, tiled=True)]
    ppermute x0 -> x27, starting transfers between devices: none -> 30.7 us  [the longest x12 17.3 us: body(): got = [near, lax.ppermute(total, 'mp', ring)]]
  transfers between devices with their start and end apart: 7 -> 30, of which waited for: 4 -> 15; matrix products, arithmetic and copies ran while one was open for 17% -> 3% of each run, Pallas kernels for 0% -> 19%
where the time goes in v1:
time: 474 us; the launch traced here: 472 us
  waiting for transfers between devices  233 us (49%)
  Pallas kernels  148 us (31%)
  starting transfers between devices  42.4 us (9%)
  local copies, waits for them, and re-layouts  24.8 us (5%)
  between operations  14.2 us (3%)
  other arithmetic  10.1 us (2%)
    ppermute x4, waiting for transfers between devices, body(): near = lax.ppermute(sent, 'mp', swap)  74.6 us
    pallas_call x20, Pallas kernels, add_parts(): pl.pallas_call(functools.partial(sum_kernel, len(coded), block_rows), gri...  68.4 us
    ppermute x3, waiting for transfers between devices, body(): block = lax.ppermute(block, 'mp', ring)  63.5 us
    ppermute x4, waiting for transfers between devices, body(): cots += [block, lax.ppermute(block, 'mp', swap)]  39.7 us
    pallas_call x1, Pallas kernels, body(): pl.pallas_call(functools.partial(backward_kernel, len(cots)), grid_spec=p...  36.9 us
    all_to_all x1, waiting for transfers between devices, body(): down = lax.all_to_all(turned, 'mp', split_axis=0, concat_axis=0, tiled=True)  24.5 us
    pallas_call x1, Pallas kernels, body(): pl.pallas_call(forward_kernel, grid_spec=pltpu.PrefetchScalarGridSpec(num...  22.9 us
    unnamed x54, local copies, waits for them, and re-layouts  19.9 us
  transfers between devices with their start and end apart: 30, of which 15 were waited for; matrix products, arithmetic and copies ran while one was open for 3% of the time, Pallas kernels for 19%

profile of v1, /device:TPU:0, one launch (start us, length us, event | category | flops | bytes accessed | tf_op | source)
XLA Modules:
  0.0 472.2 jit_solution(18047918049447807299)
XLA Ops:
  7.2 2.8 copy.34.in_ref
  10.0 5.7 %turn_down.1 = bf16[8,64,1024]{2,1,0:T(8,128)(2,1)} custom-call(bf16[1,8192,64]{2,1,0:T(8,128)(2,1)} %copy.34.in_ref), custom_call_target="tpu_custom_call" | custom-call | tf_op jit(solution)/shard_map/turn_down/pallas_call | solution.py:208
  15.7 7.3 %all-to-all-start = ((bf16[8,64,1024]{2,1,0:T(8,128)(2,1)}), bf16[8,64,1024]{2,1,0:T(8,128)(2,1)S(1)}, u32[]{:S(2)}, u32[]{:S(2)}) async-start(bf16[8,64,1024]{2,1,0:T(8,128)(2,1)} %turn_down.1), calls=%async_computation | async-start | bytes 2097152 | tf_op jit(solution)/shard_map/all_to_all | solution.py:216
  25.8 45.1 %collective-permute-done.19.refs_2_ = bf16[4096,128]{1,0:T(8,128)(2,1)} collective-permute-done((bf16[4096,128]{1,0:T(8,128)(2,1)S(1)}, bf16[4096,128]{1,0:T(8,128)(2,1)}, u32[]{:S(2)}, u32[]{:S(2)}) %collective-permute-start.19) | collective-permute-done | bytes 1048608 | tf_op jit(solution)/shard_map/ppermute | solution.py:206
  73.5 24.5 %all-to-all-done = bf16[8,64,1024]{2,1,0:T(8,128)(2,1)S(1)} async-done(((bf16[8,64,1024]{2,1,0:T(8,128)(2,1)}), bf16[8,64,1024]{2,1,0:T(8,128)(2,1)S(1)}, u32[]{:S(2)}, u32[]{:S(2)}) %all-to-all-start) | async-done | bytes 1048608 | tf_op jit(solution)/shard_map/all_to_all | solution.py:216
  98.0 18.5 %all-gather.2.cloned.1.call-done = bf16[8,64,1024]{2,1,0:T(8,128)(2,1)} async-done(((bf16[1,64,1024]{2,1,0:T(8,128)(2,1)}), bf16[8,64,1024]{2,1,0:T(8,128)(2,1)}) %all-gather.2.cloned.1.call-update) | async-done | bytes 1048592 | tf_op jit(solution)/shard_map/all_gather | solution.py:217
  123.7 3.5 maximum_maximum_fusion.1.up_ref.refs_11_
  127.2 18.4 %collective-permute-done.23.refs_6_ = bf16[4096,128]{1,0:T(8,128)(2,1)} collective-permute-done((bf16[4096,128]{1,0:T(8,128)(2,1)}, bf16[4096,128]{1,0:T(8,128)(2,1)}, u32[]{:S(2)}, u32[]{:S(2)}) %collective-permute-start.23) | collective-permute-done | bytes 1048608 | tf_op jit(solution)/shard_map/ppermute | solution.py:206
  147.1 22.9 %forward.1 = (f32[8,4096,128]{2,1,0:T(8,128)}, bf16[4096,128]{1,0:T(8,128)(2,1)}) custom-call(s32[32]{0:T(128)} %fusion.slot_ref, bf16[4096,1024]{1,0:T(8,128)(2,1)} %refs_8_.1, bf16[1024,1024]{1,0:T(8,128)(2,1)} %refs_9_.1, bf16[16,128,1024]{2,1,0:T(8,128)(2,1)} %maximum_maximum_fusion.down_ref.refs_10_, ...), custom_call_target="tpu_custom_call" | custom-call | flops 12884901888 | bytes 25165824 | tf_op jit(solution)/shard_map/forward/pallas_call | solution.py:235
  170.0 17.7 %collective-permute-done.22.refs_5_ = bf16[4096,128]{1,0:T(8,128)(2,1)} collective-permute-done((bf16[4096,128]{1,0:T(8,128)(2,1)}, bf16[4096,128]{1,0:T(8,128)(2,1)}, u32[]{:S(2)}, u32[]{:S(2)}) %collective-permute-start.22) | collective-permute-done | bytes 1048608 | tf_op jit(solution)/shard_map/ppermute | solution.py:203
  187.7 22.0 %collective-permute-done.24.refs_7_ = bf16[4096,128]{1,0:T(8,128)(2,1)S(1)} collective-permute-done((bf16[4096,128]{1,0:T(8,128)(2,1)}, bf16[4096,128]{1,0:T(8,128)(2,1)S(1)}, u32[]{:S(2)}, u32[]{:S(2)}) %collective-permute-start.24) | collective-permute-done | bytes 1048608 | tf_op jit(solution)/shard_map/ppermute | solution.py:203
  210.7 36.9 %backward.1 = (bf16[4096,1024]{1,0:T(8,128)(2,1)}, f32[16,64,1024]{2,1,0:T(8,128)}, f32[16,64,1024]{2,1,0:T(8,128)}) custom-call(s32[32]{0:T(128)} %fusion.slot_ref, s32[8]{0:T(128)} %stack.105.place_ref, bf16[4096,128]{1,0:T(8,128)(2,1)} %refs_0_.1, bf16[4096,128]{1,0:T(8,128)(2,1)} %collective-permute-done.18.refs_1_, ...), custom_call_target="tpu_custom_call" | custom-call | flops 17179869184 | bytes 25165824 | tf_op jit(solution)/shard_map/backward/pallas_call | solution.py:282
  250.7 3.0 collective-permute-done.25.rdown_ref
  253.7 3.1 collective-permute-done.26.rup_ref
  256.8 7.2 %pack_gradients.1 = s16[8,144,1024]{2,1,0:T(8,128)(2,1)} custom-call(f32[16,64,1024]{2,1,0:T(8,128)} %get-tuple-element.14.gdown_ref, f32[8,64,1024]{2,1,0:T(8,128)} %copy-done.4, f32[16,64,1024]{2,1,0:T(8,128)} %get-tuple-element.15.gup_ref, f32[8,64,1024]{2,1,0:T(8,128)} %collective-permute-done.26.rup_ref), custom_call_target="tpu_custom_call" | custom-call | tf_op jit(solution)/shard_map/pack_gradients/pallas_call | solution.py:317
  264.1 4.4 all-to-all-start.1
  269.0 6.3 %add_parts.35 = s16[4,2,528,128]{3,2,1,0:T(8,128)(2,1)} custom-call(s32[1,4]{1,0:T(1,128)} %add_bitcast_fusion.pick_ref, f32[8,4096,128]{2,1,0:T(8,128)} %get-tuple-element.11.refs_0_), custom_call_target="tpu_custom_call" | custom-call | bytes 3145728 | tf_op jit(solution)/shard_map/add_parts/pallas_call | solution.py:131
  277.2 6.3 %add_parts.30 = s16[4,2,528,128]{3,2,1,0:T(8,128)(2,1)} custom-call(s32[1,4]{1,0:T(1,128)} %add_bitcast_fusion.pick_ref, f32[8,4096,128]{2,1,0:T(8,128)} %get-tuple-element.11.refs_0_), custom_call_target="tpu_custom_call" | custom-call | bytes 3145728 | tf_op jit(solution)/shard_map/add_parts/pallas_call | solution.py:131
  283.7 6.3 %add_parts.25 = s16[4,2,528,128]{3,2,1,0:T(8,128)(2,1)} custom-call(s32[1,4]{1,0:T(1,128)} %add_bitcast_fusion.pick_ref, f32[8,4096,128]{2,1,0:T(8,128)} %get-tuple-element.11.refs_0_), custom_call_target="tpu_custom_call" | custom-call | bytes 3145728 | tf_op jit(solution)/shard_map/add_parts/pallas_call | solution.py:131
  291.9 6.3 %add_parts.20 = s16[4,2,528,128]{3,2,1,0:T(8,128)(2,1)} custom-call(s32[1,4]{1,0:T(1,128)} %add_bitcast_fusion.pick_ref, f32[8,4096,128]{2,1,0:T(8,128)} %get-tuple-element.11.refs_0_), custom_call_target="tpu_custom_call" | custom-call | bytes 3145728 | tf_op jit(solution)/shard_map/add_parts/pallas_call | solution.py:131
  298.9 21.2 %collective-permute-done.14.refs_1_ = s16[4,2,528,128]{3,2,1,0:T(8,128)(2,1)} collective-permute-done((s16[4,2,528,128]{3,2,1,0:T(8,128)(2,1)}, s16[4,2,528,128]{3,2,1,0:T(8,128)(2,1)}, u32[]{:S(2)}, u32[]{:S(2)}) %collective-permute-start.14) | collective-permute-done | bytes 1081376 | tf_op jit(solution)/shard_map/ppermute | solution.py:268
  324.7 18.5 %collective-permute-done.10.refs_1_ = s16[4,2,528,128]{3,2,1,0:T(8,128)(2,1)S(1)} collective-permute-done((s16[4,2,528,128]{3,2,1,0:T(8,128)(2,1)}, s16[4,2,528,128]{3,2,1,0:T(8,128)(2,1)S(1)}, u32[]{:S(2)}, u32[]{:S(2)}) %collective-permute-start.10) | collective-permute-done | bytes 1081376 | tf_op jit(solution)/shard_map/ppermute | solution.py:268
  348.7 17.6 %collective-permute-done.6.refs_1_ = s16[4,2,528,128]{3,2,1,0:T(8,128)(2,1)S(1)} collective-permute-done((s16[4,2,528,128]{3,2,1,0:T(8,128)(2,1)}, s16[4,2,528,128]{3,2,1,0:T(8,128)(2,1)S(1)}, u32[]{:S(2)}, u32[]{:S(2)}) %collective-permute-start.6) | collective-permute-done | bytes 1081376 | tf_op jit(solution)/shard_map/ppermute | solution.py:268
  372.0 17.2 %collective-permute-done.2.refs_1_ = s16[4,2,528,128]{3,2,1,0:T(8,128)(2,1)S(1)} collective-permute-done((s16[4,2,528,128]{3,2,1,0:T(8,128)(2,1)}, s16[4,2,528,128]{3,2,1,0:T(8,128)(2,1)S(1)}, u32[]{:S(2)}, u32[]{:S(2)}) %collective-permute-start.2) | collective-permute-done | bytes 1081376 | tf_op jit(solution)/shard_map/ppermute | solution.py:268
  400.6 2.8 add_parts.32
  406.0 2.8 add_parts.27
  409.6 2.7 add_parts.22
  420.2 2.8 add_parts.33
  425.5 2.8 add_parts.28
  429.1 2.7 add_parts.23
  454.7 6.8 %unpack_gradients.1 = (f32[1,8192,64]{2,1,0:T(8,128)}, f32[1,64,1024]{2,1,0:T(8,128)}) custom-call(s16[8,144,1024]{2,1,0:T(8,128)(2,1)} %all-to-all-done.1.in_ref), custom_call_target="tpu_custom_call" | custom-call | tf_op jit(solution)/shard_map/unpack_gradients/pallas_call | solution.py:331
  461.5 3.8 copy.47
  (129 shorter events, 88.0 us)
Async XLA Ops:
  7.2 110.9 %copy-start.24 = (s32[24,1]{0,1:T(1,128)S(1)}, s32[24,1]{0,1:T(1,128)}, u32[]{:S(2)}) copy-start(s32[24,1]{0,1:T(1,128)} %param.14) | copy-start | bytes 292
  7.2 111.5 %copy-start.25 = (s32[16]{0:T(128)S(1)}, s32[16]{0:T(128)}, u32[]{:S(2)}) copy-start(s32[16]{0:T(128)} %param.15) | copy-start | bytes 196
  15.7 82.3 %all-to-all-start = ((bf16[8,64,1024]{2,1,0:T(8,128)(2,1)}), bf16[8,64,1024]{2,1,0:T(8,128)(2,1)S(1)}, u32[]{:S(2)}, u32[]{:S(2)}) async-start(bf16[8,64,1024]{2,1,0:T(8,128)(2,1)} %turn_down.1), calls=%async_computation | async-start | bytes 2097152 | tf_op jit(solution)/shard_map/all_to_all | solution.py:216
  23.0 93.5 %all-gather.2.cloned.1.call-start = ((), (), s32[]{:S(2)}) async-start(), calls=%async_computation.2 | async-start | bytes 1179648 | tf_op jit(solution)/shard_map/all_gather | solution.py:217
  23.8 47.2 %collective-permute-start.19 = (bf16[4096,128]{1,0:T(8,128)(2,1)S(1)}, bf16[4096,128]{1,0:T(8,128)(2,1)}, u32[]{:S(2)}, u32[]{:S(2)}) collective-permute-start(bf16[4096,128]{1,0:T(8,128)(2,1)S(1)} %copy-done.22), channel_id=1, source_target_pairs={{0,2},{1,3},{2,4},{3,5},{4,6},{5,7},{6,0},{7,1},{8,10},{9,11},{10,... | collective-permute-start | bytes 3145736 | tf_op jit(solution)/shard_map/ppermute | solution.py:206
  70.9 47.2 %collective-permute-start.21 = (bf16[4096,128]{1,0:T(8,128)(2,1)}, bf16[4096,128]{1,0:T(8,128)(2,1)}, u32[]{:S(2)}, u32[]{:S(2)}) collective-permute-start(bf16[4096,128]{1,0:T(8,128)(2,1)} %collective-permute-done.19.refs_2_), channel_id=1, source_target_pairs={{0,2},{1,3},{2,4},{3,5},{4,6},{5,7},{6,0},{7,1},{8,10},{9,11},{10,... | collective-permute-start | bytes 3145736 | tf_op jit(solution)/shard_map/ppermute | solution.py:206
  98.0 22.8 %collective-permute-start = (bf16[8,64,1024]{2,1,0:T(8,128)(2,1)S(1)}, bf16[8,64,1024]{2,1,0:T(8,128)(2,1)S(1)}, u32[]{:S(2)}, u32[]{:S(2)}) collective-permute-start(bf16[8,64,1024]{2,1,0:T(8,128)(2,1)S(1)} %all-to-all-done), channel_id=1, source_target_pairs={{0,8},{8,0},{1,9},{9,1},{2,10},{10,2},{3,11},{11,3},{4,12},{12,4},... | collective-permute-start | bytes 3145736 | tf_op jit(solution)/shard_map/ppermute | solution.py:218
  116.5 7.2 %collective-permute-start.1 = (bf16[8,64,1024]{2,1,0:T(8,128)(2,1)}, bf16[8,64,1024]{2,1,0:T(8,128)(2,1)}, u32[]{:S(2)}, u32[]{:S(2)}) collective-permute-start(bf16[8,64,1024]{2,1,0:T(8,128)(2,1)} %all-gather.2.cloned.1.call-done), channel_id=1, source_target_pairs={{0,8},{8,0},{1,9},{9,1},{2,10},{10,2},{3,11},{11,3},{4,12},{12,4},... | collective-permute-start | bytes 3145736 | tf_op jit(solution)/shard_map/ppermute | solution.py:219
  116.5 53.5 %collective-permute-start.18 = (bf16[4096,128]{1,0:T(8,128)(2,1)}, bf16[4096,128]{1,0:T(8,128)(2,1)}, u32[]{:S(2)}, u32[]{:S(2)}) collective-permute-start(bf16[4096,128]{1,0:T(8,128)(2,1)} %refs_0_.1), channel_id=1, source_target_pairs={{0,1},{1,0},{2,3},{3,2},{4,5},{5,4},{6,7},{7,6},{8,9},{9,8},{10,11... | collective-permute-start | bytes 3145736 | tf_op jit(solution)/shard_map/ppermute | solution.py:203
  118.2 27.5 %collective-permute-start.23 = (bf16[4096,128]{1,0:T(8,128)(2,1)}, bf16[4096,128]{1,0:T(8,128)(2,1)}, u32[]{:S(2)}, u32[]{:S(2)}) collective-permute-start(bf16[4096,128]{1,0:T(8,128)(2,1)} %collective-permute-done.21.refs_4_), channel_id=1, source_target_pairs={{0,2},{1,3},{2,4},{3,5},{4,6},{5,7},{6,0},{7,1},{8,10},{9,11},{10,... | collective-permute-start | bytes 3145736 | tf_op jit(solution)/shard_map/ppermute | solution.py:206
  119.4 50.6 %collective-permute-start.20 = (bf16[4096,128]{1,0:T(8,128)(2,1)}, bf16[4096,128]{1,0:T(8,128)(2,1)}, u32[]{:S(2)}, u32[]{:S(2)}) collective-permute-start(bf16[4096,128]{1,0:T(8,128)(2,1)} %collective-permute-done.19.refs_2_), channel_id=1, source_target_pairs={{0,1},{1,0},{2,3},{3,2},{4,5},{5,4},{6,7},{7,6},{8,9},{9,8},{10,11... | collective-permute-start | bytes 3145736 | tf_op jit(solution)/shard_map/ppermute | solution.py:203
  120.8 66.9 %collective-permute-start.22 = (bf16[4096,128]{1,0:T(8,128)(2,1)}, bf16[4096,128]{1,0:T(8,128)(2,1)}, u32[]{:S(2)}, u32[]{:S(2)}) collective-permute-start(bf16[4096,128]{1,0:T(8,128)(2,1)} %collective-permute-done.21.refs_4_), channel_id=1, source_target_pairs={{0,1},{1,0},{2,3},{3,2},{4,5},{5,4},{6,7},{7,6},{8,9},{9,8},{10,11... | collective-permute-start | bytes 3145736 | tf_op jit(solution)/shard_map/ppermute | solution.py:203
  145.6 64.1 %collective-permute-start.24 = (bf16[4096,128]{1,0:T(8,128)(2,1)}, bf16[4096,128]{1,0:T(8,128)(2,1)S(1)}, u32[]{:S(2)}, u32[]{:S(2)}) collective-permute-start(bf16[4096,128]{1,0:T(8,128)(2,1)} %collective-permute-done.23.refs_6_), channel_id=1, source_target_pairs={{0,1},{1,0},{2,3},{3,2},{4,5},{5,4},{6,7},{7,6},{8,9},{9,8},{10,11... | collective-permute-start | bytes 3145736 | tf_op jit(solution)/shard_map/ppermute | solution.py:203
  249.5 4.2 collective-permute-start.25
  250.6 6.2 %collective-permute-start.26 = (f32[8,64,1024]{2,1,0:T(8,128)S(1)}, f32[8,64,1024]{2,1,0:T(8,128)}, u32[]{:S(2)}, u32[]{:S(2)}) collective-permute-start(f32[8,64,1024]{2,1,0:T(8,128)S(1)} %slice.7), channel_id=1, source_target_pairs={{0,8},{8,0},{1,9},{9,1},{2,10},{10,2},{3,11},{11,3},{4,12},{12,4},... | collective-permute-start | bytes 6291464 | tf_op jit(solution)/shard_map/ppermute | solution.py:315
  264.1 190.7 %all-to-all-start.1 = ((s16[8,144,1024]{2,1,0:T(8,128)(2,1)}), s16[8,144,1024]{2,1,0:T(8,128)(2,1)}, u32[]{:S(2)}, u32[]{:S(2)}) async-start(s16[8,144,1024]{2,1,0:T(8,128)(2,1)} %pack_gradients.1), calls=%async_computation.1 | async-start | bytes 4718592 | tf_op jit(solution)/shard_map/all_to_all | solution.py:330
  275.3 44.8 %collective-permute-start.14 = (s16[4,2,528,128]{3,2,1,0:T(8,128)(2,1)}, s16[4,2,528,128]{3,2,1,0:T(8,128)(2,1)}, u32[]{:S(2)}, u32[]{:S(2)}) collective-permute-start(s16[4,2,528,128]{3,2,1,0:T(8,128)(2,1)} %add_parts.35), channel_id=1, source_target_pairs={{0,1},{1,0},{2,3},{3,2},{4,5},{5,4},{6,7},{7,6},{8,9},{9,8},{10,11... | collective-permute-start | bytes 3244040 | tf_op jit(solution)/shard_map/ppermute | solution.py:268
  283.5 59.7 %collective-permute-start.10 = (s16[4,2,528,128]{3,2,1,0:T(8,128)(2,1)}, s16[4,2,528,128]{3,2,1,0:T(8,128)(2,1)S(1)}, u32[]{:S(2)}, u32[]{:S(2)}) collective-permute-start(s16[4,2,528,128]{3,2,1,0:T(8,128)(2,1)} %add_parts.30), channel_id=1, source_target_pairs={{0,1},{1,0},{2,3},{3,2},{4,5},{5,4},{6,7},{7,6},{8,9},{9,8},{10,11... | collective-permute-start | bytes 3244040 | tf_op jit(solution)/shard_map/ppermute | solution.py:268
  290.0 76.4 %collective-permute-start.6 = (s16[4,2,528,128]{3,2,1,0:T(8,128)(2,1)}, s16[4,2,528,128]{3,2,1,0:T(8,128)(2,1)S(1)}, u32[]{:S(2)}, u32[]{:S(2)}) collective-permute-start(s16[4,2,528,128]{3,2,1,0:T(8,128)(2,1)} %add_parts.25), channel_id=1, source_target_pairs={{0,1},{1,0},{2,3},{3,2},{4,5},{5,4},{6,7},{7,6},{8,9},{9,8},{10,11... | collective-permute-start | bytes 3244040 | tf_op jit(solution)/shard_map/ppermute | solution.py:268
  298.2 91.0 %collective-permute-start.2 = (s16[4,2,528,128]{3,2,1,0:T(8,128)(2,1)}, s16[4,2,528,128]{3,2,1,0:T(8,128)(2,1)S(1)}, u32[]{:S(2)}, u32[]{:S(2)}) collective-permute-start(s16[4,2,528,128]{3,2,1,0:T(8,128)(2,1)} %add_parts.20), channel_id=1, source_target_pairs={{0,1},{1,0},{2,3},{3,2},{4,5},{5,4},{6,7},{7,6},{8,9},{9,8},{10,11... | collective-permute-start | bytes 3244040 | tf_op jit(solution)/shard_map/ppermute | solution.py:268
  322.7 72.3 %collective-permute-start.15 = (s16[1,2,528,128]{3,2,1,0:T(8,128)(2,1)}, s16[1,2,528,128]{3,2,1,0:T(8,128)(2,1)S(1)}, u32[]{:S(2)}, u32[]{:S(2)}) collective-permute-start(s16[1,2,528,128]{3,2,1,0:T(8,128)(2,1)} %add_parts.36), channel_id=1, source_target_pairs={{0,2},{1,3},{2,4},{3,5},{4,6},{5,7},{6,0},{7,1},{8,10},{9,11},{10,... | collective-permute-start | bytes 811016 | tf_op jit(solution)/shard_map/ppermute | solution.py:275
  346.8 53.1 %collective-permute-start.11 = (s16[1,2,528,128]{3,2,1,0:T(8,128)(2,1)}, s16[1,2,528,128]{3,2,1,0:T(8,128)(2,1)S(1)}, u32[]{:S(2)}, u32[]{:S(2)}) collective-permute-start(s16[1,2,528,128]{3,2,1,0:T(8,128)(2,1)} %add_parts.31), channel_id=1, source_target_pairs={{0,2},{1,3},{2,4},{3,5},{4,6},{5,7},{6,0},{7,1},{8,10},{9,11},{10,... | collective-permute-start | bytes 811016 | tf_op jit(solution)/shard_map/ppermute | solution.py:275
  370.0 35.3 %collective-permute-start.7 = (s16[1,2,528,128]{3,2,1,0:T(8,128)(2,1)}, s16[1,2,528,128]{3,2,1,0:T(8,128)(2,1)S(1)}, u32[]{:S(2)}, u32[]{:S(2)}) collective-permute-start(s16[1,2,528,128]{3,2,1,0:T(8,128)(2,1)} %add_parts.26), channel_id=1, source_target_pairs={{0,2},{1,3},{2,4},{3,5},{4,6},{5,7},{6,0},{7,1},{8,10},{9,11},{10,... | collective-permute-start | bytes 811016 | tf_op jit(solution)/shard_map/ppermute | solution.py:275
  392.8 16.1 %collective-permute-start.3 = (s16[1,2,528,128]{3,2,1,0:T(8,128)(2,1)}, s16[1,2,528,128]{3,2,1,0:T(8,128)(2,1)S(1)}, u32[]{:S(2)}, u32[]{:S(2)}) collective-permute-start(s16[1,2,528,128]{3,2,1,0:T(8,128)(2,1)} %add_parts.21), channel_id=1, source_target_pairs={{0,2},{1,3},{2,4},{3,5},{4,6},{5,7},{6,0},{7,1},{8,10},{9,11},{10,... | collective-permute-start | bytes 811016 | tf_op jit(solution)/shard_map/ppermute | solution.py:275
  398.5 16.1 %collective-permute-start.16 = (s16[1,2,528,128]{3,2,1,0:T(8,128)(2,1)}, s16[1,2,528,128]{3,2,1,0:T(8,128)(2,1)S(1)}, u32[]{:S(2)}, u32[]{:S(2)}) collective-permute-start(s16[1,2,528,128]{3,2,1,0:T(8,128)(2,1)} %add_parts.37), channel_id=1, source_target_pairs={{0,2},{1,3},{2,4},{3,5},{4,6},{5,7},{6,0},{7,1},{8,10},{9,11},{10,... | collective-permute-start | bytes 811016 | tf_op jit(solution)/shard_map/ppermute | solution.py:275
  403.4 16.1 %collective-permute-start.12 = (s16[1,2,528,128]{3,2,1,0:T(8,128)(2,1)}, s16[1,2,528,128]{3,2,1,0:T(8,128)(2,1)S(1)}, u32[]{:S(2)}, u32[]{:S(2)}) collective-permute-start(s16[1,2,528,128]{3,2,1,0:T(8,128)(2,1)} %add_parts.32), channel_id=1, source_target_pairs={{0,2},{1,3},{2,4},{3,5},{4,6},{5,7},{6,0},{7,1},{8,10},{9,11},{10,... | collective-permute-start | bytes 811016 | tf_op jit(solution)/shard_map/ppermute | solution.py:275
  408.8 16.1 %collective-permute-start.8 = (s16[1,2,528,128]{3,2,1,0:T(8,128)(2,1)}, s16[1,2,528,128]{3,2,1,0:T(8,128)(2,1)S(1)}, u32[]{:S(2)}, u32[]{:S(2)}) collective-permute-start(s16[1,2,528,128]{3,2,1,0:T(8,128)(2,1)} %add_parts.27), channel_id=1, source_target_pairs={{0,2},{1,3},{2,4},{3,5},{4,6},{5,7},{6,0},{7,1},{8,10},{9,11},{10,... | collective-permute-start | bytes 811016 | tf_op jit(solution)/shard_map/ppermute | solution.py:275
  412.3 16.1 %collective-permute-start.4 = (s16[1,2,528,128]{3,2,1,0:T(8,128)(2,1)}, s16[1,2,528,128]{3,2,1,0:T(8,128)(2,1)S(1)}, u32[]{:S(2)}, u32[]{:S(2)}) collective-permute-start(s16[1,2,528,128]{3,2,1,0:T(8,128)(2,1)} %add_parts.22), channel_id=1, source_target_pairs={{0,2},{1,3},{2,4},{3,5},{4,6},{5,7},{6,0},{7,1},{8,10},{9,11},{10,... | collective-permute-start | bytes 811016 | tf_op jit(solution)/shard_map/ppermute | solution.py:275
  418.0 16.1 %collective-permute-start.17 = (s16[1,2,528,128]{3,2,1,0:T(8,128)(2,1)}, s16[1,2,528,128]{3,2,1,0:T(8,128)(2,1)S(1)}, u32[]{:S(2)}, u32[]{:S(2)}) collective-permute-start(s16[1,2,528,128]{3,2,1,0:T(8,128)(2,1)} %add_parts.38), channel_id=1, source_target_pairs={{0,2},{1,3},{2,4},{3,5},{4,6},{5,7},{6,0},{7,1},{8,10},{9,11},{10,... | collective-permute-start | bytes 811016 | tf_op jit(solution)/shard_map/ppermute | solution.py:275
  422.9 16.0 %collective-permute-start.13 = (s16[1,2,528,128]{3,2,1,0:T(8,128)(2,1)}, s16[1,2,528,128]{3,2,1,0:T(8,128)(2,1)S(1)}, u32[]{:S(2)}, u32[]{:S(2)}) collective-permute-start(s16[1,2,528,128]{3,2,1,0:T(8,128)(2,1)} %add_parts.33), channel_id=1, source_target_pairs={{0,2},{1,3},{2,4},{3,5},{4,6},{5,7},{6,0},{7,1},{8,10},{9,11},{10,... | collective-permute-start | bytes 811016 | tf_op jit(solution)/shard_map/ppermute | solution.py:275
  428.3 16.4 %collective-permute-start.9 = (s16[1,2,528,128]{3,2,1,0:T(8,128)(2,1)}, s16[1,2,528,128]{3,2,1,0:T(8,128)(2,1)S(1)}, u32[]{:S(2)}, u32[]{:S(2)}) collective-permute-start(s16[1,2,528,128]{3,2,1,0:T(8,128)(2,1)} %add_parts.28), channel_id=1, source_target_pairs={{0,2},{1,3},{2,4},{3,5},{4,6},{5,7},{6,0},{7,1},{8,10},{9,11},{10,... | collective-permute-start | bytes 811016 | tf_op jit(solution)/shard_map/ppermute | solution.py:275
  431.9 17.5 %collective-permute-start.5 = (s16[1,2,528,128]{3,2,1,0:T(8,128)(2,1)}, s16[1,2,528,128]{3,2,1,0:T(8,128)(2,1)S(1)}, u32[]{:S(2)}, u32[]{:S(2)}) collective-permute-start(s16[1,2,528,128]{3,2,1,0:T(8,128)(2,1)} %add_parts.23), channel_id=1, source_target_pairs={{0,2},{1,3},{2,4},{3,5},{4,6},{5,7},{6,0},{7,1},{8,10},{9,11},{10,... | collective-permute-start | bytes 811016 | tf_op jit(solution)/shard_map/ppermute | solution.py:275
  (24 other events, 166.1 us)
Sparse Core Ops, SparseCore 0:
  26.0 90.4 all-gather.1

commit v2 on v1

v2 whole, which is shorter than its diff:
```python
import functools

import jax
import jax.numpy as jnp
from jax import lax
from jax.experimental import pallas as pl
from jax.experimental.pallas import tpu as pltpu
from jax.sharding import PartitionSpec as P

TILE = 128
ADAPTER_SCALE = 2.0
INNER = 2
PAD = 16
TOP = 32700.0
STEPS = 64.0
TINY = 1e-30
VMEM = 60 * 1024 * 1024
F32 = jnp.float32
BF16 = jnp.bfloat16
NT = (((1,), (1,)), ((), ()))
TN = (((0,), (0,)), ((), ()))


def dot(a, b, dims=(((1,), (0,)), ((), ()))):
    return lax.dot_general(a, b, dims, preferred_element_type=F32)


def split_halves(twice, rank):
    high = twice.astype(BF16).astype(F32)
    lane = lax.broadcasted_iota(jnp.int32, twice.shape, 1)
    return jnp.where(lane < rank, high, twice - high).astype(BF16)


def encode(v):
    most = jnp.max(jnp.abs(v), axis=0, keepdims=True)
    code = jnp.ceil(jnp.log2(jnp.maximum(most, TINY)) * STEPS)
    gain = jnp.exp2(code * (-1.0 / STEPS)) * TOP
    return jnp.round(v * gain).astype(jnp.int32).astype(jnp.int16), code


def step_of(code):
    return jnp.exp2(code.astype(jnp.int32).astype(F32) * (1.0 / STEPS)) * (1.0 / TOP)


def decode(q, code):
    return q.astype(jnp.int32).astype(F32) * step_of(code)


def turn_kernel(in_ref, out_ref):
    out_ref[0] = in_ref[0].T


def fill_twice(pair_ref, near_ref, far_ref):
    n, rank = near_ref.shape[:2]
    for k, ref in enumerate((near_ref, far_ref)):
        pair_ref[k * n : (k + 1) * n, :rank, :] = ref[...]
        pair_ref[k * n : (k + 1) * n, rank:, :] = ref[...]


def forward_kernel(first, slot_ref, upslot_ref, place_ref, *refs):
    x_ref, w_ref, ndown_ref, fdown_ref, nup_ref, fup_ref, sent_ref, kept_ref, split_ref, down_ref, up_ref, sum_ref = refs
    step = pl.program_id(0)
    outer, rows, cols = kept_ref.shape
    tiles = rows // TILE
    rank = down_ref.shape[1] // 2
    n = ndown_ref.shape[0]
    inner = n // outer

    @pl.when(step == 0)
    def _():
        fill_twice(down_ref, ndown_ref, fdown_ref)
        fill_twice(up_ref, nup_ref, fup_ref)

    base = dot(x_ref[...], w_ref[...])
    for t in range(tiles):
        at = slice(t * TILE, (t + 1) * TILE)
        tile = first + step * tiles + t
        pieces = split_halves(dot(x_ref[at, :], down_ref[slot_ref[tile]], NT), rank)
        split_ref[at, :] = pieces
        total = base[at] + ADAPTER_SCALE * dot(pieces, up_ref[upslot_ref[tile]])
        for j in range(n):
            sum_ref[j, at, :] = total[:, j * cols : (j + 1) * cols]
    mine = place_ref[1]
    for z in range(outer):
        kept_ref[z] = sum_ref[z * inner + mine]
        q, code = encode(sum_ref[z * inner + 1 - mine])
        put(sent_ref.at[z, 0], q, code)


def gradient_kernel(blocks, slot_ref, upslot_ref, order_ref, *refs):
    cots = refs[:blocks]
    x_ref, nup_ref, fup_ref, split_ref = refs[blocks : blocks + 4]
    all_ref, back_ref, ndown_ref, fdown_ref, nsum_ref, fsum_ref, up_ref, cot_ref, gdown_ref, gup_ref = refs[blocks + 4 :]
    step = pl.program_id(0)
    rows = x_ref.shape[0]
    tiles = rows // TILE
    rank = up_ref.shape[1] // 2

    @pl.when(step == 0)
    def _():
        fill_twice(up_ref, nup_ref, fup_ref)
        gdown_ref[...] = jnp.zeros_like(gdown_ref)
        gup_ref[...] = jnp.zeros_like(gup_ref)

    for j, block in enumerate(cots):
        wide = block.shape[1]
        if blocks == 1:
            cot_ref[...] = block[...]
        else:
            cot_ref[:, pl.ds(pl.multiple_of(order_ref[j] * wide, wide), wide)] = block[...]
    all_ref[...] = cot_ref[...]
    for t in range(tiles):
        at = slice(t * TILE, (t + 1) * TILE)
        slot = slot_ref[step * tiles + t]
        cot = cot_ref[at, :]
        pieces = split_halves(dot(cot, up_ref[upslot_ref[step * tiles + t]], NT), rank)
        back_ref[at, :] = pieces
        grad = dot(pieces, x_ref[at, :], TN)
        gdown_ref[slot] += grad[:rank] + grad[rank:]
        grad = dot(split_ref[at, :], cot, TN)
        gup_ref[slot] += grad[:rank] + grad[rank:]

    @pl.when(step == pl.num_programs(0) - 1)
    def _():
        n = ndown_ref.shape[0]
        ndown_ref[...] = gdown_ref[:n]
        fdown_ref[...] = gdown_ref[n:]
        nsum_ref[...] = gup_ref[:n]
        fsum_ref[...] = gup_ref[n:]


def token_kernel(slot_ref, cot_ref, w_ref, near_ref, far_ref, back_ref, after_ref, out_ref, down_ref):
    step = pl.program_id(0)
    tiles = cot_ref.shape[0] // TILE

    @pl.when(step == 0)
    def _():
        fill_twice(down_ref, near_ref, far_ref)

    base = dot(cot_ref[...], w_ref[...], NT)
    for t in range(tiles):
        at = slice(t * TILE, (t + 1) * TILE)
        slot = slot_ref[step * tiles + t]
        out_ref[at, :] = (base[at] + ADAPTER_SCALE * dot(back_ref[at, :], down_ref[slot])).astype(BF16)


def put(ref, q, code):
    rows = q.shape[0]
    ref[:rows, :] = q
    ref[rows:, :] = jnp.broadcast_to(code, (PAD, code.shape[1])).astype(jnp.int32).astype(jnp.int16)


def sum_kernel(coded, place_ref, *refs):
    total = refs[0][0]
    rows = total.shape[0]
    for ref in refs[1 : 1 + coded]:
        total = total + decode(ref[0, 0, :rows, :], ref[0, 0, rows : rows + 1, :])
    out_ref = refs[-1]
    if out_ref.dtype == BF16:
        out_ref[...] = total.astype(BF16)
    else:
        put(out_ref.at[0, 0], *encode(total))


def add_parts(place, back, kept, near, run, last):
    outer, rows, cols = kept.shape
    blocks, held = near.shape[1:3]
    block_rows = held - PAD

    def at(place):
        return lax.rem(place[0] - back + outer, outer)

    in_specs = [
        pl.BlockSpec((1, block_rows, cols), lambda b, p: (at(p), b, 0)),
        pl.BlockSpec((1, 1, held, cols), lambda b, p: (at(p), b, 0, 0)),
    ]
    in_specs += [pl.BlockSpec((1, 1, held, cols), lambda b, p: (0, b, 0, 0)) for _ in run]
    if last:
        out_shape = jax.ShapeDtypeStruct((rows, cols), BF16)
        out_spec = pl.BlockSpec((block_rows, cols), lambda b, p: (b, 0))
    else:
        out_shape = jax.ShapeDtypeStruct((1, blocks, held, cols), jnp.int16)
        out_spec = pl.BlockSpec((1, 1, held, cols), lambda b, p: (0, b, 0, 0))
    return pl.pallas_call(
        functools.partial(sum_kernel, 1 + len(run)),
        grid_spec=pltpu.PrefetchScalarGridSpec(
            num_scalar_prefetch=1, grid=(blocks,), in_specs=in_specs, out_specs=out_spec
        ),
        out_shape=out_shape,
        cost_estimate=pl.CostEstimate(flops=0, bytes_accessed=rows * cols * 8, transcendentals=0),
        name="add_parts",
    )(place, kept, near, *run)


def pack_kernel(gdown_ref, rdown_ref, gup_ref, rup_ref, out_ref):
    rank, width = gdown_ref.shape[1:]
    groups = gup_ref.shape[2] // width
    row = lax.broadcasted_iota(jnp.int32, (PAD, width), 0)
    codes = jnp.zeros((PAD, width), F32)
    down = gdown_ref[0] + rdown_ref[0]
    for g in range(groups + 1):
        if g == 0:
            v = down
        else:
            at = slice((g - 1) * width, g * width)
            v = gup_ref[0, :, at] + rup_ref[0, :, at]
        q, code = encode(v)
        out_ref[0, g * rank : (g + 1) * rank, :] = q
        codes = jnp.where(row == g, code, codes)
    out_ref[0, (groups + 1) * rank :, :] = codes.astype(jnp.int32).astype(jnp.int16)


def unpack_kernel(in_ref, down_ref, up_ref):
    rank = up_ref.shape[1]
    width = in_ref.shape[2]
    groups = up_ref.shape[2] // width

    @pl.when(pl.program_id(0) == 0)
    def _():
        up_ref[...] = jnp.zeros_like(up_ref)

    steps = ADAPTER_SCALE * step_of(in_ref[0, (groups + 1) * rank :, :])
    for g in range(groups + 1):
        v = in_ref[0, g * rank : (g + 1) * rank, :].astype(jnp.int32).astype(F32) * steps[g : g + 1]
        if g == 0:
            down_ref[0] = v.T
        else:
            up_ref[0, :, (g - 1) * width : g * width] += v


def body(
    tokens, frozen_weight, cotangent, adapter_down, adapter_up, seg_tiles, seg_adapter, owner_slot
):
    rows, width = tokens.shape
    cols = cotangent.shape[1]
    n = lax.axis_size("mp")
    n_data = lax.axis_size("dp")
    _, entire_width, rank = adapter_down.shape
    out_width = adapter_up.shape[2]
    slots = n_data * n
    tile_count = rows // TILE
    inner = INNER
    outer = n // inner
    me = lax.axis_index("mp")
    my_outer, my_inner = me // inner, me % inner
    other = 1 - my_inner
    my_data = lax.axis_index("dp")
    swap = [(i, i ^ 1) for i in range(n)]
    ring = [(i, (i + inner) % n) for i in range(n)]
    cores = [(i, 1 - i) for i in range(n_data)]

    place = jnp.stack([my_outer, my_inner]).astype(jnp.int32)

    ups = [adapter_up]
    for s in range(1, outer):
        ups.append(lax.ppermute(adapter_up, "mp", [(i, (i + s * inner) % n) for i in range(n)]))
    ups = jnp.concatenate(ups, axis=0)
    near_up = jnp.concatenate([ups, lax.ppermute(ups, "mp", swap)], axis=0)
    far_up = lax.ppermute(near_up, "dp", cores)

    turned = pl.pallas_call(
        turn_kernel,
        grid=(n,),
        in_specs=[pl.BlockSpec((1, width, rank), lambda i: (0, i, 0))],
        out_specs=pl.BlockSpec((1, rank, width), lambda i: (i, 0, 0)),
        out_shape=jax.ShapeDtypeStruct((n, rank, width), BF16),
        name="turn_down",
    )(adapter_down)
    near_down = lax.all_to_all(turned, "mp", split_axis=0, concat_axis=0, tiled=True)
    far_down = lax.ppermute(near_down, "dp", cores)

    cots, order = [], []
    block, swapped = cotangent, None
    for s in range(outer):
        at = ((my_outer - s) % outer) * inner
        swapped = lax.ppermute(block, "mp", swap)
        cots += [block, swapped]
        order += [at + my_inner, at + other]
        if s < outer - 1:
            block, cots[-1] = lax.optimization_barrier((lax.ppermute(block, "mp", ring), swapped))

    ends = jnp.cumsum(seg_tiles[0])
    positions = jnp.arange(tile_count, dtype=jnp.int32)
    segment = jnp.sum((positions[:, None] >= ends[None, :]).astype(jnp.int32), axis=1)
    seg_pick = segment[:, None] == jnp.arange(ends.shape[0], dtype=jnp.int32)[None, :]
    tile_adapter = jnp.sum(jnp.where(seg_pick, seg_adapter[:, 0][None, :], 0), axis=1)
    adapt_pick = tile_adapter[:, None] == jnp.arange(slots, dtype=jnp.int32)[None, :]
    tile_slot = jnp.sum(jnp.where(adapt_pick, owner_slot[None, :], 0), axis=1)
    core, owner = (tile_slot // n + my_data) % n_data, tile_slot % n
    tile_slot = core * n + owner
    tile_up = core * n + ((owner + my_inner) % inner) * outer + (my_outer - owner // inner) % outer

    block_rows = 4 * TILE
    steps = rows // block_rows
    chunks = 4
    blocks = steps // chunks
    chunk_rows = rows // chunks
    once = pl.Buffered(1)
    params = pltpu.CompilerParams(vmem_limit_bytes=VMEM)
    held = block_rows + PAD

    def whole(*shape):
        return pl.BlockSpec(shape, lambda i, *_: (0,) * len(shape), pipeline_mode=once)

    def strip(wide, first=0):
        return pl.BlockSpec((block_rows, wide), lambda i, *_: (first + i, 0))

    def forward(c):
        return pl.pallas_call(
            functools.partial(forward_kernel, c * blocks * (block_rows // TILE)),
            grid_spec=pltpu.PrefetchScalarGridSpec(
                num_scalar_prefetch=3,
                grid=(blocks,),
                in_specs=[
                    strip(width, c * blocks),
                    whole(width, out_width),
                    whole(n, rank, width),
                    whole(n, rank, width),
                    whole(n, rank, out_width),
                    whole(n, rank, out_width),
                ],
                out_specs=[
                    pl.BlockSpec((outer, 1, held, cols), lambda i, *_: (0, i, 0, 0)),
                    pl.BlockSpec((outer, block_rows, cols), lambda i, *_: (0, i, 0)),
                    strip(2 * rank),
                ],
                scratch_shapes=[
                    pltpu.VMEM((slots, 2 * rank, width), BF16),
                    pltpu.VMEM((slots, 2 * rank, out_width), BF16),
                    pltpu.VMEM((n, block_rows, cols), F32),
                ],
            ),
            out_shape=[
                jax.ShapeDtypeStruct((outer, blocks, held, cols), jnp.int16),
                jax.ShapeDtypeStruct((outer, chunk_rows, cols), F32),
                jax.ShapeDtypeStruct((chunk_rows, 2 * rank), BF16),
            ],
            compiler_params=params,
            cost_estimate=pl.CostEstimate(
                flops=4 * chunk_rows * width * out_width, bytes_accessed=chunk_rows * width * 6, transcendentals=0
            ),
            name="forward",
        )(tile_slot, tile_up, place, tokens, frozen_weight, near_down, far_down, near_up, far_up)

    sents, kepts, splits = zip(*[forward(c) for c in range(chunks)])
    split = jnp.concatenate(splits, axis=0)
    first, cots[-1] = lax.optimization_barrier((sents[0], cots[-1]))
    nears = [lax.ppermute(first, "mp", swap)]
    for c in range(1, chunks):
        sent, nears[-1] = lax.optimization_barrier((sents[c], nears[-1]))
        nears.append(lax.ppermute(sent, "mp", swap))

    if cols % 128:
        natural = jnp.stack(cots)[jnp.argsort(jnp.stack(order))]
        cots = [jnp.transpose(natural, (1, 0, 2)).reshape(rows, out_width)]
    cot_all, back, gdown, rdown, gup, rup = pl.pallas_call(
        functools.partial(gradient_kernel, len(cots)),
        grid_spec=pltpu.PrefetchScalarGridSpec(
            num_scalar_prefetch=3,
            grid=(steps,),
            in_specs=[strip(a.shape[1]) for a in cots]
            + [strip(width), whole(n, rank, out_width), whole(n, rank, out_width), strip(2 * rank)],
            out_specs=[
                strip(out_width),
                strip(2 * rank),
                whole(n, rank, width),
                whole(n, rank, width),
                whole(n, rank, out_width),
                whole(n, rank, out_width),
            ],
            scratch_shapes=[
                pltpu.VMEM((slots, 2 * rank, out_width), BF16),
                pltpu.VMEM((block_rows, out_width), BF16),
                pltpu.VMEM((slots, rank, width), F32),
                pltpu.VMEM((slots, rank, out_width), F32),
            ],
        ),
        out_shape=[
            jax.ShapeDtypeStruct((rows, out_width), BF16),
            jax.ShapeDtypeStruct((rows, 2 * rank), BF16),
            jax.ShapeDtypeStruct((n, rank, width), F32),
            jax.ShapeDtypeStruct((n, rank, width), F32),
            jax.ShapeDtypeStruct((n, rank, out_width), F32),
            jax.ShapeDtypeStruct((n, rank, out_width), F32),
        ],
        compiler_params=params,
        cost_estimate=pl.CostEstimate(
            flops=2 * rows * width * out_width, bytes_accessed=rows * (width * 2 + out_width * 4), transcendentals=0
        ),
        name="gradients",
    )(tile_slot, tile_up, jnp.stack(order).astype(jnp.int32), *cots, tokens, near_up, far_up, split)
    nears[0], rdown, rup = lax.optimization_barrier((nears[0], rdown, rup))

    outs = []
    for near, kept in zip(nears, kepts):
        run = []
        for s in range(1, outer):
            run = [lax.ppermute(add_parts(place, s, kept, near, run, last=False), "mp", ring)]
        outs.append(add_parts(place, 0, kept, near, run, last=True))
    output = jnp.concatenate(outs, axis=0)

    token_gradient = pl.pallas_call(
        token_kernel,
        grid_spec=pltpu.PrefetchScalarGridSpec(
            num_scalar_prefetch=1,
            grid=(steps,),
            in_specs=[
                strip(out_width),
                whole(width, out_width),
                whole(n, rank, width),
                whole(n, rank, width),
                strip(2 * rank),
                pl.BlockSpec(memory_space=pl.ANY),
            ],
            out_specs=strip(width),
            scratch_shapes=[pltpu.VMEM((slots, 2 * rank, width), BF16)],
        ),
        out_shape=jax.ShapeDtypeStruct((rows, width), BF16),
        compiler_params=params,
        cost_estimate=pl.CostEstimate(
            flops=3 * rows * width * out_width, bytes_accessed=rows * (width * 2 + out_width * 2), transcendentals=0
        ),
        name="token_gradient",
    )(tile_slot, cot_all, frozen_weight, near_down, far_down, back, nears[-1])

    rdown = lax.ppermute(rdown, "dp", cores)
    rup = lax.ppermute(rup, "dp", cores)
    packed_rows = (1 + out_width // width) * rank + PAD
    packed = pl.pallas_call(
        pack_kernel,
        grid=(n,),
        in_specs=[
            pl.BlockSpec((1, rank, width), lambda i: (i, 0, 0)),
            pl.BlockSpec((1, rank, width), lambda i: (i, 0, 0)),
            pl.BlockSpec((1, rank, out_width), lambda i: (i, 0, 0)),
            pl.BlockSpec((1, rank, out_width), lambda i: (i, 0, 0)),
        ],
        out_specs=pl.BlockSpec((1, packed_rows, width), lambda i: (i, 0, 0)),
        out_shape=jax.ShapeDtypeStruct((n, packed_rows, width), jnp.int16),
        name="pack_gradients",
    )(gdown, rdown, gup, rup)
    packed = lax.all_to_all(packed, "mp", split_axis=0, concat_axis=0, tiled=True)
    down_gradient, up_gradient = pl.pallas_call(
        unpack_kernel,
        grid=(n,),
        in_specs=[pl.BlockSpec((1, packed_rows, width), lambda i: (i, 0, 0))],
        out_specs=[
            pl.BlockSpec((1, width, rank), lambda i: (0, i, 0)),
            pl.BlockSpec((1, rank, out_width), lambda i: (0, 0, 0)),
        ],
        out_shape=[
            jax.ShapeDtypeStruct((1, entire_width, rank), F32),
            jax.ShapeDtypeStruct((1, rank, out_width), F32),
        ],
        name="unpack_gradients",
    )(packed)
    return output, token_gradient, down_gradient, up_gradient


def solution(mesh):
    placed = (
        P(("groups", "dp"), "mp"),
        P("mp", None),
        P(("groups", "dp"), "mp"),
        P(("groups", "dp", "mp"), None, None),
        P(("groups", "dp", "mp"), None, None),
        P(("groups", "dp"), None),
        P(("groups", "dp"), None),
        P("groups"),
    )
    return jax.shard_map(
        body,
        mesh=mesh,
        in_specs=placed,
        out_specs=(
            P(("groups", "dp"), "mp"),
            P(("groups", "dp"), "mp"),
            P(("groups", "dp", "mp"), None, None),
            P(("groups", "dp", "mp"), None, None),
        ),
        check_vma=False,
    )
```

time: 474 us -> 395 us (0.83)
  waiting for transfers between devices: 233 us -> 157 us
  starting transfers between devices: 42.4 us -> 65.8 us
  between operations: 14.2 us -> 0.92 us
  local copies, waits for them, and re-layouts: 24.8 us -> 17.9 us
    ppermute x27 -> x31, waiting for transfers between devices: 189 us -> 157 us  [the longest x3 52.5 us: body(): nears.append(lax.ppermute(sent, 'mp', swap))]
    all_to_all x1, waiting for transfers between devices: 24.5 us -> 0.01 us  [body(): lax.all_to_all(turned, 'mp', split_axis=0, concat_axis=0, tiled=True)]
    ppermute x27 -> x31, starting transfers between devices: 30.7 us -> 54.1 us  [the longest x12 27.6 us: body(): lax.ppermute(add_parts(place, s, kept, near, run, last=False), 'mp', ring)]
    all_gather x1 -> x0, waiting for transfers between devices: 18.5 us -> none  [body(): up = lax.all_gather(adapter_up, 'mp', axis=0, tiled=True)]
    unnamed x54 -> x72, local copies, waits for them, and re-layouts: 19.9 us -> 17.1 us
  transfers between devices with their start and end apart: 30 -> 33, of which waited for: 15 -> 10; matrix products, arithmetic and copies ran while one was open for 3% -> 2% of each run, Pallas kernels for 19% -> 34%
where the time goes in v2:
time: 395 us; the launch traced here: 393 us
  waiting for transfers between devices  157 us (40%)
  Pallas kernels  145 us (37%)
  starting transfers between devices  65.8 us (17%)
  local copies, waits for them, and re-layouts  17.9 us (5%)
  other arithmetic  6.23 us (2%)
    ppermute x3, waiting for transfers between devices, body(): nears.append(lax.ppermute(sent, 'mp', swap))  52.5 us
    pallas_call x16, Pallas kernels, add_parts(): pl.pallas_call(functools.partial(sum_kernel, 1 + len(run)), grid_spec=plt...  42.5 us
    pallas_call x4, Pallas kernels, forward(): pl.pallas_call(functools.partial(forward_kernel, c * blocks * (block_rows...  41 us
    ppermute x3, waiting for transfers between devices, body(): lax.ppermute(block, 'mp', ring)  40.4 us
    ppermute x3, waiting for transfers between devices, body(): lax.ppermute(adapter_up, 'mp', [(i, (i + s * inner) % n) for i in range(n)])  27.9 us
    ppermute x12, starting transfers between devices, body(): lax.ppermute(add_parts(place, s, kept, near, run, last=False), 'mp', ring)  27.6 us
    pallas_call x1, Pallas kernels, body(): pl.pallas_call(functools.partial(gradient_kernel, len(cots)), grid_spec=p...  24.4 us
    pallas_call x1, Pallas kernels, body(): pl.pallas_call(token_kernel, grid_spec=pltpu.PrefetchScalarGridSpec(num_s...  17.2 us
  transfers between devices with their start and end apart: 33, of which 10 were waited for; matrix products, arithmetic and copies ran while one was open for 2% of the time, Pallas kernels for 34%

profile of v2, /device:TPU:0, one launch (start us, length us, event | category | flops | bytes accessed | tf_op | source)
XLA Modules:
  0.0 392.9 jit_solution(5875546163823408288)
XLA Ops:
  0.6 2.7 copy.19.in_ref
  3.4 5.8 %turn_down.1 = bf16[8,64,1024]{2,1,0:T(8,128)(2,1)} custom-call(bf16[1,8192,64]{2,1,0:T(8,128)(2,1)} %copy.19.in_ref), custom_call_target="tpu_custom_call" | custom-call | tf_op jit(solution)/shard_map/turn_down/pallas_call | solution.py:261
  9.2 7.3 %all-to-all-start = ((bf16[8,64,1024]{2,1,0:T(8,128)(2,1)}), bf16[8,64,1024]{2,1,0:T(8,128)(2,1)S(1)}, u32[]{:S(2)}, u32[]{:S(2)}) async-start(bf16[8,64,1024]{2,1,0:T(8,128)(2,1)} %turn_down.1), calls=%async_computation | async-start | bytes 2097152 | tf_op jit(solution)/shard_map/all_to_all | solution.py:269
  24.4 37.1 %collective-permute-done.6.refs_2_ = bf16[4096,128]{1,0:T(8,128)(2,1)} collective-permute-done((bf16[4096,128]{1,0:T(8,128)(2,1)S(1)}, bf16[4096,128]{1,0:T(8,128)(2,1)}, u32[]{:S(2)}, u32[]{:S(2)}) %collective-permute-start.6) | collective-permute-done | bytes 1048608 | tf_op jit(solution)/shard_map/ppermute | solution.py:280
  63.0 7.5 %collective-permute-start.8 = (bf16[4096,128]{1,0:T(8,128)(2,1)}, bf16[4096,128]{1,0:T(8,128)(2,1)}, u32[]{:S(2)}, u32[]{:S(2)}) collective-permute-start(bf16[4096,128]{1,0:T(8,128)(2,1)} %collective-permute-done.6.refs_2_), channel_id=1, source_target_pairs={{0,2},{1,3},{2,4},{3,5},{4,6},{5,7},{6,0},{7,1},{8,10},{9,11},{10,... | collective-permute-start | bytes 3145736 | tf_op jit(solution)/shard_map/ppermute | solution.py:280
  70.5 27.9 %collective-permute-done.2 = bf16[1,64,1024]{2,1,0:T(8,128)(2,1)S(1)} collective-permute-done((bf16[1,64,1024]{2,1,0:T(8,128)(2,1)S(1)}, bf16[1,64,1024]{2,1,0:T(8,128)(2,1)S(1)}, u32[]{:S(2)}, u32[]{:S(2)}) %collective-permute-start.2) | collective-permute-done | bytes 131104 | tf_op jit(solution)/shard_map/ppermute | solution.py:256
  100.1 11.1 %collective-permute-done.4 = bf16[4,64,1024]{2,1,0:T(8,128)(2,1)S(1)} collective-permute-done((bf16[4,64,1024]{2,1,0:T(8,128)(2,1)S(1)}, bf16[4,64,1024]{2,1,0:T(8,128)(2,1)S(1)}, u32[]{:S(2)}, u32[]{:S(2)}) %collective-permute-start.4) | collective-permute-done | bytes 524320 | tf_op jit(solution)/shard_map/ppermute | solution.py:258
  117.5 10.2 %forward.7 = (s16[4,2,528,128]{3,2,1,0:T(8,128)(2,1)}, f32[4,1024,128]{2,1,0:T(8,128)}, bf16[1024,128]{1,0:T(8,128)(2,1)}) custom-call(s32[32]{0:T(128)} %fusion.7.slot_ref, s32[32]{0:T(128)} %get-tuple-element.90.upslot_ref, s32[2]{0:T(128)} %pad_add_fusion.place_ref, bf16[4096,1024]{1,0:T(8,128)(2,1)} %refs_8_.1, bf16[1024,1024]{1,0:T(8,128)(2,1)} %w_ref.1, ...), custom_call_target="tpu_custom_call" | custom-call | flops 4294967296 | bytes 6291456 | tf_op jit(solution)/shard_map/forward/pallas_call | solution.py:309
  127.7 10.7 %collective-permute-done.11.refs_5_ = bf16[4096,128]{1,0:T(8,128)(2,1)} collective-permute-done((bf16[4096,128]{1,0:T(8,128)(2,1)}, bf16[4096,128]{1,0:T(8,128)(2,1)}, u32[]{:S(2)}, u32[]{:S(2)}) %collective-permute-start.11) | collective-permute-done | bytes 1048608 | tf_op jit(solution)/shard_map/ppermute | solution.py:276
  138.4 3.3 collective-permute-done.10.refs_6_
  142.0 10.2 %forward.6 = (s16[4,2,528,128]{3,2,1,0:T(8,128)(2,1)}, f32[4,1024,128]{2,1,0:T(8,128)}, bf16[1024,128]{1,0:T(8,128)(2,1)}) custom-call(s32[32]{0:T(128)} %fusion.7.slot_ref, s32[32]{0:T(128)} %get-tuple-element.90.upslot_ref, s32[2]{0:T(128)} %pad_add_fusion.place_ref, bf16[4096,1024]{1,0:T(8,128)(2,1)} %refs_8_.1, bf16[1024,1024]{1,0:T(8,128)(2,1)} %w_ref.1, ...), custom_call_target="tpu_custom_call" | custom-call | flops 4294967296 | bytes 6291456 | tf_op jit(solution)/shard_map/forward/pallas_call | solution.py:309
  152.2 10.2 %forward.5 = (s16[4,2,528,128]{3,2,1,0:T(8,128)(2,1)}, f32[4,1024,128]{2,1,0:T(8,128)}, bf16[1024,128]{1,0:T(8,128)(2,1)}) custom-call(s32[32]{0:T(128)} %fusion.7.slot_ref, s32[32]{0:T(128)} %get-tuple-element.90.upslot_ref, s32[2]{0:T(128)} %pad_add_fusion.place_ref, bf16[4096,1024]{1,0:T(8,128)(2,1)} %refs_8_.1, bf16[1024,1024]{1,0:T(8,128)(2,1)} %w_ref.1, ...), custom_call_target="tpu_custom_call" | custom-call | flops 4294967296 | bytes 6291456 | tf_op jit(solution)/shard_map/forward/pallas_call | solution.py:309
  162.5 10.4 %forward.4 = (s16[4,2,528,128]{3,2,1,0:T(8,128)(2,1)}, f32[4,1024,128]{2,1,0:T(8,128)}, bf16[1024,128]{1,0:T(8,128)(2,1)}) custom-call(s32[32]{0:T(128)} %fusion.7.slot_ref, s32[32]{0:T(128)} %get-tuple-element.90.upslot_ref, s32[2]{0:T(128)} %pad_add_fusion.place_ref, bf16[4096,1024]{1,0:T(8,128)(2,1)} %refs_8_.1, bf16[1024,1024]{1,0:T(8,128)(2,1)} %w_ref.1, ...), custom_call_target="tpu_custom_call" | custom-call | flops 4294967296 | bytes 6291456 | tf_op jit(solution)/shard_map/forward/pallas_call | solution.py:309
  176.7 24.4 %gradients.1 = (bf16[4096,1024]{1,0:T(8,128)(2,1)}, bf16[4096,128]{1,0:T(8,128)(2,1)}, f32[8,64,1024]{2,1,0:T(8,128)}, f32[8,64,1024]{2,1,0:T(8,128)}, f32[8,64,1024]{2,1,0:T(8,128)}, /*index=5*/f32[8,64,1024]{2,1,0:T(8,128)}) custom-call(s32[32]{0:T(128)} %fusion.7.slot_ref, s32[32]{0:T(128)} %get-tuple-element.90.upslot_ref, s32[8]{0:T(128)} %stack.47.order_ref, ...), custom_call_target="tpu_custom_call" | custom-call | flops 8589934592 | bytes 25165824 | tf_op jit(solution)/shard_map/gradients/pallas_call | solution.py:356
  202.0 25.5 %collective-permute-done.17.refs_1_ = s16[4,2,528,128]{3,2,1,0:T(8,128)(2,1)S(1)} collective-permute-done((s16[4,2,528,128]{3,2,1,0:T(8,128)(2,1)S(1)}, s16[4,2,528,128]{3,2,1,0:T(8,128)(2,1)S(1)}, u32[]{:S(2)}, u32[]{:S(2)}) %collective-permute-start.17) | collective-permute-done | bytes 1081376 | tf_op jit(solution)/shard_map/ppermute | solution.py:351
  227.9 7.2 %pack_gradients.1 = s16[8,144,1024]{2,1,0:T(8,128)(2,1)} custom-call(f32[8,64,1024]{2,1,0:T(8,128)} %get-tuple-element.72.gdown_ref, f32[8,64,1024]{2,1,0:T(8,128)} %collective-permute-done.29.rdown_ref, f32[8,64,1024]{2,1,0:T(8,128)} %get-tuple-element.74.gup_ref, f32[8,64,1024]{2,1,0:T(8,128)} %collective-permute-done.30.rup_ref), custom_call_target="tpu_custom_call" | custom-call | tf_op jit(solution)/shard_map/pack_gradients/pallas_call | solution.py:429
  235.1 4.4 %all-to-all-start.1 = ((s16[8,144,1024]{2,1,0:T(8,128)(2,1)}), s16[8,144,1024]{2,1,0:T(8,128)(2,1)}, u32[]{:S(2)}, u32[]{:S(2)}) async-start(s16[8,144,1024]{2,1,0:T(8,128)(2,1)} %pack_gradients.1), calls=%async_computation.1 | async-start | bytes 4718592 | tf_op jit(solution)/shard_map/all_to_all | solution.py:442
  239.5 27.0 %collective-permute-done.21.refs_1_ = s16[4,2,528,128]{3,2,1,0:T(8,128)(2,1)S(1)} collective-permute-done((s16[4,2,528,128]{3,2,1,0:T(8,128)(2,1)}, s16[4,2,528,128]{3,2,1,0:T(8,128)(2,1)S(1)}, u32[]{:S(2)}, u32[]{:S(2)}) %collective-permute-start.21) | collective-permute-done | bytes 1081376 | tf_op jit(solution)/shard_map/ppermute | solution.py:351
  276.6 12.3 %collective-permute-done.14.refs_2_ = s16[1,2,528,128]{3,2,1,0:T(8,128)(2,1)S(1)} collective-permute-done((s16[1,2,528,128]{3,2,1,0:T(8,128)(2,1)}, s16[1,2,528,128]{3,2,1,0:T(8,128)(2,1)S(1)}, u32[]{:S(2)}, u32[]{:S(2)}) %collective-permute-start.14) | collective-permute-done | bytes 270368 | tf_op jit(solution)/shard_map/ppermute | solution.py:398
  289.6 2.7 add_parts.17
  292.3 9.5 %collective-permute-start.15 = (s16[1,2,528,128]{3,2,1,0:T(8,128)(2,1)}, s16[1,2,528,128]{3,2,1,0:T(8,128)(2,1)S(1)}, u32[]{:S(2)}, u32[]{:S(2)}) collective-permute-start(s16[1,2,528,128]{3,2,1,0:T(8,128)(2,1)} %add_parts.17), channel_id=1, source_target_pairs={{0,2},{1,3},{2,4},{3,5},{4,6},{5,7},{6,0},{7,1},{8,10},{9,11},{10,... | collective-permute-start | bytes 811016 | tf_op jit(solution)/shard_map/ppermute | solution.py:398
  302.6 2.7 add_parts.21
  308.4 2.7 add_parts.25
  320.1 2.7 add_parts.18
  323.6 2.7 add_parts.22
  327.2 2.7 add_parts.26
  333.0 2.7 add_parts.29
  351.0 2.7 add_parts.30
  353.7 6.0 %collective-permute-start.28 = (s16[1,2,528,128]{3,2,1,0:T(8,128)(2,1)}, s16[1,2,528,128]{3,2,1,0:T(8,128)(2,1)S(1)}, u32[]{:S(2)}, u32[]{:S(2)}) collective-permute-start(s16[1,2,528,128]{3,2,1,0:T(8,128)(2,1)} %add_parts.30), channel_id=1, source_target_pairs={{0,2},{1,3},{2,4},{3,5},{4,6},{5,7},{6,0},{7,1},{8,10},{9,11},{10,... | collective-permute-start | bytes 811016 | tf_op jit(solution)/shard_map/ppermute | solution.py:398
  359.7 17.2 %token_gradient.1 = bf16[4096,1024]{1,0:T(8,128)(2,1)} custom-call(s32[32]{0:T(128)} %fusion.7.slot_ref, bf16[4096,1024]{1,0:T(8,128)(2,1)} %get-tuple-element.70.cot_ref, bf16[1024,1024]{1,0:T(8,128)(2,1)} %w_ref.1, bf16[8,64,1024]{2,1,0:T(8,128)(2,1)} %copy-done.4, bf16[8,64,1024]{2,1,0:T(8,128)(2,1)} %copy-done.28, ...), custom_call_target="tpu_custom_call" | custom-call | flops 12884901888 | bytes 16777216 | tf_op jit(solution)/shard_map/token_gradient/pallas_call | solution.py:402
  382.3 6.8 %unpack_gradients.1 = (f32[1,8192,64]{2,1,0:T(8,128)}, f32[1,64,1024]{2,1,0:T(8,128)}) custom-call(s16[8,144,1024]{2,1,0:T(8,128)(2,1)} %all-to-all-done.1.in_ref), custom_call_target="tpu_custom_call" | custom-call | tf_op jit(solution)/shard_map/unpack_gradients/pallas_call | solution.py:443
  389.1 3.8 copy.20
  (145 shorter events, 71.7 us)
Async XLA Ops:
  9.2 102.1 %all-to-all-start = ((bf16[8,64,1024]{2,1,0:T(8,128)(2,1)}), bf16[8,64,1024]{2,1,0:T(8,128)(2,1)S(1)}, u32[]{:S(2)}, u32[]{:S(2)}) async-start(bf16[8,64,1024]{2,1,0:T(8,128)(2,1)} %turn_down.1), calls=%async_computation | async-start | bytes 2097152 | tf_op jit(solution)/shard_map/all_to_all | solution.py:269
  16.5 45.0 %collective-permute-start.6 = (bf16[4096,128]{1,0:T(8,128)(2,1)S(1)}, bf16[4096,128]{1,0:T(8,128)(2,1)}, u32[]{:S(2)}, u32[]{:S(2)}) collective-permute-start(bf16[4096,128]{1,0:T(8,128)(2,1)S(1)} %copy-done.27), channel_id=1, source_target_pairs={{0,2},{1,3},{2,4},{3,5},{4,6},{5,7},{6,0},{7,1},{8,10},{9,11},{10,... | collective-permute-start | bytes 3145736 | tf_op jit(solution)/shard_map/ppermute | solution.py:280
  18.6 43.0 %collective-permute-start.7 = (bf16[4096,128]{1,0:T(8,128)(2,1)S(1)}, bf16[4096,128]{1,0:T(8,128)(2,1)S(1)}, u32[]{:S(2)}, u32[]{:S(2)}) collective-permute-start(bf16[4096,128]{1,0:T(8,128)(2,1)S(1)} %copy-done.27), channel_id=1, source_target_pairs={{0,1},{1,0},{2,3},{3,2},{4,5},{5,4},{6,7},{7,6},{8,9},{9,8},{10,11... | collective-permute-start | bytes 3145736 | tf_op jit(solution)/shard_map/ppermute | solution.py:276
  20.0 50.5 %collective-permute-start.3 = (bf16[1,64,1024]{2,1,0:T(8,128)(2,1)S(1)}, bf16[1,64,1024]{2,1,0:T(8,128)(2,1)S(1)}, u32[]{:S(2)}, u32[]{:S(2)}) collective-permute-start(bf16[1,64,1024]{2,1,0:T(8,128)(2,1)S(1)} %copy-done.8), channel_id=1, source_target_pairs={{0,6},{1,7},{2,0},{3,1},{4,2},{5,3},{6,4},{7,5},{8,14},{9,15},{10,... | collective-permute-start | bytes 393224 | tf_op jit(solution)/shard_map/ppermute | solution.py:256
  22.4 76.0 %collective-permute-start.2 = (bf16[1,64,1024]{2,1,0:T(8,128)(2,1)S(1)}, bf16[1,64,1024]{2,1,0:T(8,128)(2,1)S(1)}, u32[]{:S(2)}, u32[]{:S(2)}) collective-permute-start(bf16[1,64,1024]{2,1,0:T(8,128)(2,1)S(1)} %copy-done.8), channel_id=1, source_target_pairs={{0,4},{1,5},{2,6},{3,7},{4,0},{5,1},{6,2},{7,3},{8,12},{9,13},{10,... | collective-permute-start | bytes 393224 | tf_op jit(solution)/shard_map/ppermute | solution.py:256
  23.0 75.5 %collective-permute-start.1 = (bf16[1,64,1024]{2,1,0:T(8,128)(2,1)S(1)}, bf16[1,64,1024]{2,1,0:T(8,128)(2,1)S(1)}, u32[]{:S(2)}, u32[]{:S(2)}) collective-permute-start(bf16[1,64,1024]{2,1,0:T(8,128)(2,1)S(1)} %copy-done.8), channel_id=1, source_target_pairs={{0,2},{1,3},{2,4},{3,5},{4,6},{5,7},{6,0},{7,1},{8,10},{9,11},{10,... | collective-permute-start | bytes 393224 | tf_op jit(solution)/shard_map/ppermute | solution.py:256
  61.5 51.4 %collective-permute-start.9 = (bf16[4096,128]{1,0:T(8,128)(2,1)}, bf16[4096,128]{1,0:T(8,128)(2,1)}, u32[]{:S(2)}, u32[]{:S(2)}) collective-permute-start(bf16[4096,128]{1,0:T(8,128)(2,1)} %collective-permute-done.6.refs_2_), channel_id=1, source_target_pairs={{0,1},{1,0},{2,3},{3,2},{4,5},{5,4},{6,7},{7,6},{8,9},{9,8},{10,11... | collective-permute-start | bytes 3145736 | tf_op jit(solution)/shard_map/ppermute | solution.py:276
  63.0 49.9 %collective-permute-start.8 = (bf16[4096,128]{1,0:T(8,128)(2,1)}, bf16[4096,128]{1,0:T(8,128)(2,1)}, u32[]{:S(2)}, u32[]{:S(2)}) collective-permute-start(bf16[4096,128]{1,0:T(8,128)(2,1)} %collective-permute-done.6.refs_2_), channel_id=1, source_target_pairs={{0,2},{1,3},{2,4},{3,5},{4,6},{5,7},{6,0},{7,1},{8,10},{9,11},{10,... | collective-permute-start | bytes 3145736 | tf_op jit(solution)/shard_map/ppermute | solution.py:280
  98.5 12.6 %collective-permute-start.4 = (bf16[4,64,1024]{2,1,0:T(8,128)(2,1)S(1)}, bf16[4,64,1024]{2,1,0:T(8,128)(2,1)S(1)}, u32[]{:S(2)}, u32[]{:S(2)}) collective-permute-start(bf16[4,64,1024]{2,1,0:T(8,128)(2,1)S(1)} %pad_maximum_fusion.2), channel_id=1, source_target_pairs={{0,1},{1,0},{2,3},{3,2},{4,5},{5,4},{6,7},{7,6},{8,9},{9,8},{10,11... | collective-permute-start | bytes 1572872 | tf_op jit(solution)/shard_map/ppermute | solution.py:258
  111.2 5.4 %collective-permute-start.5 = (bf16[8,64,1024]{2,1,0:T(8,128)(2,1)S(1)}, bf16[8,64,1024]{2,1,0:T(8,128)(2,1)}, u32[]{:S(2)}, u32[]{:S(2)}) collective-permute-start(bf16[8,64,1024]{2,1,0:T(8,128)(2,1)S(1)} %constant_dynamic-update-slice_fusion.refs_4_.refs_9_), channel_id=1, source_target_pairs={{0,8},{8,0},{1,9},{9,1},{2,10},{10,2},{3,11},{11,3},{4,12},{12,4},... | collective-permute-start | bytes 3145736 | tf_op jit(solution)/shard_map/ppermute | solution.py:259
  112.9 25.6 %collective-permute-start.11 = (bf16[4096,128]{1,0:T(8,128)(2,1)}, bf16[4096,128]{1,0:T(8,128)(2,1)}, u32[]{:S(2)}, u32[]{:S(2)}) collective-permute-start(bf16[4096,128]{1,0:T(8,128)(2,1)} %collective-permute-done.8.refs_4_), channel_id=1, source_target_pairs={{0,1},{1,0},{2,3},{3,2},{4,5},{5,4},{6,7},{7,6},{8,9},{9,8},{10,11... | collective-permute-start | bytes 3145736 | tf_op jit(solution)/shard_map/ppermute | solution.py:276
  114.7 27.0 %collective-permute-start.10 = (bf16[4096,128]{1,0:T(8,128)(2,1)}, bf16[4096,128]{1,0:T(8,128)(2,1)}, u32[]{:S(2)}, u32[]{:S(2)}) collective-permute-start(bf16[4096,128]{1,0:T(8,128)(2,1)} %collective-permute-done.8.refs_4_), channel_id=1, source_target_pairs={{0,2},{1,3},{2,4},{3,5},{4,6},{5,7},{6,0},{7,1},{8,10},{9,11},{10,... | collective-permute-start | bytes 3145736 | tf_op jit(solution)/shard_map/ppermute | solution.py:280
  141.7 31.2 %collective-permute-start.12 = (bf16[4096,128]{1,0:T(8,128)(2,1)}, bf16[4096,128]{1,0:T(8,128)(2,1)S(1)}, u32[]{:S(2)}, u32[]{:S(2)}) collective-permute-start(bf16[4096,128]{1,0:T(8,128)(2,1)} %collective-permute-done.10.refs_6_), channel_id=1, source_target_pairs={{0,1},{1,0},{2,3},{3,2},{4,5},{5,4},{6,7},{7,6},{8,9},{9,8},{10,11... | collective-permute-start | bytes 3145736 | tf_op jit(solution)/shard_map/ppermute | solution.py:276
  172.9 28.2 %collective-permute-start.13 = (s16[4,2,528,128]{3,2,1,0:T(8,128)(2,1)}, s16[4,2,528,128]{3,2,1,0:T(8,128)(2,1)S(1)}, u32[]{:S(2)}, u32[]{:S(2)}) collective-permute-start(s16[4,2,528,128]{3,2,1,0:T(8,128)(2,1)} %get-tuple-element.47), channel_id=1, source_target_pairs={{0,1},{1,0},{2,3},{3,2},{4,5},{5,4},{6,7},{7,6},{8,9},{9,8},{10,11... | collective-permute-start | bytes 3244040 | tf_op jit(solution)/shard_map/ppermute | solution.py:348
  201.1 26.8 %collective-permute-start.29 = (f32[8,64,1024]{2,1,0:T(8,128)}, f32[8,64,1024]{2,1,0:T(8,128)}, u32[]{:S(2)}, u32[]{:S(2)}) collective-permute-start(f32[8,64,1024]{2,1,0:T(8,128)} %get-tuple-element.73), channel_id=1, source_target_pairs={{0,8},{8,0},{1,9},{9,1},{2,10},{10,2},{3,11},{11,3},{4,12},{12,4},... | collective-permute-start | bytes 6291464 | tf_op jit(solution)/shard_map/ppermute | solution.py:426
  201.2 26.7 %collective-permute-start.30 = (f32[8,64,1024]{2,1,0:T(8,128)}, f32[8,64,1024]{2,1,0:T(8,128)}, u32[]{:S(2)}, u32[]{:S(2)}) collective-permute-start(f32[8,64,1024]{2,1,0:T(8,128)} %get-tuple-element.75), channel_id=1, source_target_pairs={{0,8},{8,0},{1,9},{9,1},{2,10},{10,2},{3,11},{11,3},{4,12},{12,4},... | collective-permute-start | bytes 6291464 | tf_op jit(solution)/shard_map/ppermute | solution.py:427
  201.7 25.8 %collective-permute-start.17 = (s16[4,2,528,128]{3,2,1,0:T(8,128)(2,1)S(1)}, s16[4,2,528,128]{3,2,1,0:T(8,128)(2,1)S(1)}, u32[]{:S(2)}, u32[]{:S(2)}) collective-permute-start(s16[4,2,528,128]{3,2,1,0:T(8,128)(2,1)S(1)} %copy-done.26), channel_id=1, source_target_pairs={{0,1},{1,0},{2,3},{3,2},{4,5},{5,4},{6,7},{7,6},{8,9},{9,8},{10,11... | collective-permute-start | bytes 3244040 | tf_op jit(solution)/shard_map/ppermute | solution.py:351
  227.5 39.0 %collective-permute-start.21 = (s16[4,2,528,128]{3,2,1,0:T(8,128)(2,1)}, s16[4,2,528,128]{3,2,1,0:T(8,128)(2,1)S(1)}, u32[]{:S(2)}, u32[]{:S(2)}) collective-permute-start(s16[4,2,528,128]{3,2,1,0:T(8,128)(2,1)} %get-tuple-element.66), channel_id=1, source_target_pairs={{0,1},{1,0},{2,3},{3,2},{4,5},{5,4},{6,7},{7,6},{8,9},{9,8},{10,11... | collective-permute-start | bytes 3244040 | tf_op jit(solution)/shard_map/ppermute | solution.py:351
  235.1 147.2 %all-to-all-start.1 = ((s16[8,144,1024]{2,1,0:T(8,128)(2,1)}), s16[8,144,1024]{2,1,0:T(8,128)(2,1)}, u32[]{:S(2)}, u32[]{:S(2)}) async-start(s16[8,144,1024]{2,1,0:T(8,128)(2,1)} %pack_gradients.1), calls=%async_computation.1 | async-start | bytes 4718592 | tf_op jit(solution)/shard_map/all_to_all | solution.py:442
  266.6 46.9 %collective-permute-start.25 = (s16[4,2,528,128]{3,2,1,0:T(8,128)(2,1)}, s16[4,2,528,128]{3,2,1,0:T(8,128)(2,1)S(1)}, u32[]{:S(2)}, u32[]{:S(2)}) collective-permute-start(s16[4,2,528,128]{3,2,1,0:T(8,128)(2,1)} %get-tuple-element.69), channel_id=1, source_target_pairs={{0,1},{1,0},{2,3},{3,2},{4,5},{5,4},{6,7},{7,6},{8,9},{9,8},{10,11... | collective-permute-start | bytes 3244040 | tf_op jit(solution)/shard_map/ppermute | solution.py:351
  271.5 17.4 %collective-permute-start.14 = (s16[1,2,528,128]{3,2,1,0:T(8,128)(2,1)}, s16[1,2,528,128]{3,2,1,0:T(8,128)(2,1)S(1)}, u32[]{:S(2)}, u32[]{:S(2)}) collective-permute-start(s16[1,2,528,128]{3,2,1,0:T(8,128)(2,1)} %add_parts.16), channel_id=1, source_target_pairs={{0,2},{1,3},{2,4},{3,5},{4,6},{5,7},{6,0},{7,1},{8,10},{9,11},{10,... | collective-permute-start | bytes 811016 | tf_op jit(solution)/shard_map/ppermute | solution.py:398
  274.1 27.8 %collective-permute-start.18 = (s16[1,2,528,128]{3,2,1,0:T(8,128)(2,1)}, s16[1,2,528,128]{3,2,1,0:T(8,128)(2,1)S(1)}, u32[]{:S(2)}, u32[]{:S(2)}) collective-permute-start(s16[1,2,528,128]{3,2,1,0:T(8,128)(2,1)} %add_parts.20), channel_id=1, source_target_pairs={{0,2},{1,3},{2,4},{3,5},{4,6},{5,7},{6,0},{7,1},{8,10},{9,11},{10,... | collective-permute-start | bytes 811016 | tf_op jit(solution)/shard_map/ppermute | solution.py:398
  276.6 31.1 %collective-permute-start.22 = (s16[1,2,528,128]{3,2,1,0:T(8,128)(2,1)}, s16[1,2,528,128]{3,2,1,0:T(8,128)(2,1)S(1)}, u32[]{:S(2)}, u32[]{:S(2)}) collective-permute-start(s16[1,2,528,128]{3,2,1,0:T(8,128)(2,1)} %add_parts.24), channel_id=1, source_target_pairs={{0,2},{1,3},{2,4},{3,5},{4,6},{5,7},{6,0},{7,1},{8,10},{9,11},{10,... | collective-permute-start | bytes 811016 | tf_op jit(solution)/shard_map/ppermute | solution.py:398
  292.3 27.1 %collective-permute-start.15 = (s16[1,2,528,128]{3,2,1,0:T(8,128)(2,1)}, s16[1,2,528,128]{3,2,1,0:T(8,128)(2,1)S(1)}, u32[]{:S(2)}, u32[]{:S(2)}) collective-permute-start(s16[1,2,528,128]{3,2,1,0:T(8,128)(2,1)} %add_parts.17), channel_id=1, source_target_pairs={{0,2},{1,3},{2,4},{3,5},{4,6},{5,7},{6,0},{7,1},{8,10},{9,11},{10,... | collective-permute-start | bytes 811016 | tf_op jit(solution)/shard_map/ppermute | solution.py:398
  305.3 17.6 %collective-permute-start.19 = (s16[1,2,528,128]{3,2,1,0:T(8,128)(2,1)}, s16[1,2,528,128]{3,2,1,0:T(8,128)(2,1)S(1)}, u32[]{:S(2)}, u32[]{:S(2)}) collective-permute-start(s16[1,2,528,128]{3,2,1,0:T(8,128)(2,1)} %add_parts.21), channel_id=1, source_target_pairs={{0,2},{1,3},{2,4},{3,5},{4,6},{5,7},{6,0},{7,1},{8,10},{9,11},{10,... | collective-permute-start | bytes 811016 | tf_op jit(solution)/shard_map/ppermute | solution.py:398
  311.1 15.4 %collective-permute-start.23 = (s16[1,2,528,128]{3,2,1,0:T(8,128)(2,1)}, s16[1,2,528,128]{3,2,1,0:T(8,128)(2,1)S(1)}, u32[]{:S(2)}, u32[]{:S(2)}) collective-permute-start(s16[1,2,528,128]{3,2,1,0:T(8,128)(2,1)} %add_parts.25), channel_id=1, source_target_pairs={{0,2},{1,3},{2,4},{3,5},{4,6},{5,7},{6,0},{7,1},{8,10},{9,11},{10,... | collective-permute-start | bytes 811016 | tf_op jit(solution)/shard_map/ppermute | solution.py:398
  317.1 15.2 %collective-permute-start.26 = (s16[1,2,528,128]{3,2,1,0:T(8,128)(2,1)}, s16[1,2,528,128]{3,2,1,0:T(8,128)(2,1)S(1)}, u32[]{:S(2)}, u32[]{:S(2)}) collective-permute-start(s16[1,2,528,128]{3,2,1,0:T(8,128)(2,1)} %add_parts.28), channel_id=1, source_target_pairs={{0,2},{1,3},{2,4},{3,5},{4,6},{5,7},{6,0},{7,1},{8,10},{9,11},{10,... | collective-permute-start | bytes 811016 | tf_op jit(solution)/shard_map/ppermute | solution.py:398
  322.9 15.2 %collective-permute-start.16 = (s16[1,2,528,128]{3,2,1,0:T(8,128)(2,1)}, s16[1,2,528,128]{3,2,1,0:T(8,128)(2,1)S(1)}, u32[]{:S(2)}, u32[]{:S(2)}) collective-permute-start(s16[1,2,528,128]{3,2,1,0:T(8,128)(2,1)} %add_parts.18), channel_id=1, source_target_pairs={{0,2},{1,3},{2,4},{3,5},{4,6},{5,7},{6,0},{7,1},{8,10},{9,11},{10,... | collective-permute-start | bytes 811016 | tf_op jit(solution)/shard_map/ppermute | solution.py:398
  326.3 15.1 %collective-permute-start.20 = (s16[1,2,528,128]{3,2,1,0:T(8,128)(2,1)}, s16[1,2,528,128]{3,2,1,0:T(8,128)(2,1)S(1)}, u32[]{:S(2)}, u32[]{:S(2)}) collective-permute-start(s16[1,2,528,128]{3,2,1,0:T(8,128)(2,1)} %add_parts.22), channel_id=1, source_target_pairs={{0,2},{1,3},{2,4},{3,5},{4,6},{5,7},{6,0},{7,1},{8,10},{9,11},{10,... | collective-permute-start | bytes 811016 | tf_op jit(solution)/shard_map/ppermute | solution.py:398
  329.9 16.0 %collective-permute-start.24 = (s16[1,2,528,128]{3,2,1,0:T(8,128)(2,1)}, s16[1,2,528,128]{3,2,1,0:T(8,128)(2,1)S(1)}, u32[]{:S(2)}, u32[]{:S(2)}) collective-permute-start(s16[1,2,528,128]{3,2,1,0:T(8,128)(2,1)} %add_parts.26), channel_id=1, source_target_pairs={{0,2},{1,3},{2,4},{3,5},{4,6},{5,7},{6,0},{7,1},{8,10},{9,11},{10,... | collective-permute-start | bytes 811016 | tf_op jit(solution)/shard_map/ppermute | solution.py:398
  335.7 14.6 %collective-permute-start.27 = (s16[1,2,528,128]{3,2,1,0:T(8,128)(2,1)}, s16[1,2,528,128]{3,2,1,0:T(8,128)(2,1)S(1)}, u32[]{:S(2)}, u32[]{:S(2)}) collective-permute-start(s16[1,2,528,128]{3,2,1,0:T(8,128)(2,1)} %add_parts.29), channel_id=1, source_target_pairs={{0,2},{1,3},{2,4},{3,5},{4,6},{5,7},{6,0},{7,1},{8,10},{9,11},{10,... | collective-permute-start | bytes 811016 | tf_op jit(solution)/shard_map/ppermute | solution.py:398
  353.7 23.2 %collective-permute-start.28 = (s16[1,2,528,128]{3,2,1,0:T(8,128)(2,1)}, s16[1,2,528,128]{3,2,1,0:T(8,128)(2,1)S(1)}, u32[]{:S(2)}, u32[]{:S(2)}) collective-permute-start(s16[1,2,528,128]{3,2,1,0:T(8,128)(2,1)} %add_parts.30), channel_id=1, source_target_pairs={{0,2},{1,3},{2,4},{3,5},{4,6},{5,7},{6,0},{7,1},{8,10},{9,11},{10,... | collective-permute-start | bytes 811016 | tf_op jit(solution)/shard_map/ppermute | solution.py:398
  (34 other events, 508.3 us)

commit v3 on v2

v3 whole, which is shorter than its diff:
```python
import functools

import jax
import jax.numpy as jnp
from jax import lax
from jax.experimental import pallas as pl
from jax.experimental.pallas import tpu as pltpu
from jax.sharding import PartitionSpec as P

TILE = 128
ADAPTER_SCALE = 2.0
INNER = 2
PAD = 16
TOP = 32700.0
STEPS = 64.0
TINY = 1e-30
VMEM = 60 * 1024 * 1024
F32 = jnp.float32
BF16 = jnp.bfloat16
NT = (((1,), (1,)), ((), ()))
TN = (((0,), (0,)), ((), ()))


def dot(a, b, dims=(((1,), (0,)), ((), ()))):
    return lax.dot_general(a, b, dims, preferred_element_type=F32)


def split_halves(twice, rank):
    high = twice.astype(BF16).astype(F32)
    lane = lax.broadcasted_iota(jnp.int32, twice.shape, 1)
    return jnp.where(lane < rank, high, twice - high).astype(BF16)


def encode(v):
    most = jnp.max(jnp.abs(v), axis=0, keepdims=True)
    code = jnp.ceil(jnp.log2(jnp.maximum(most, TINY)) * STEPS)
    gain = jnp.exp2(code * (-1.0 / STEPS)) * TOP
    return jnp.round(v * gain).astype(jnp.int32).astype(jnp.int16), code


def step_of(code):
    return jnp.exp2(code.astype(jnp.int32).astype(F32) * (1.0 / STEPS)) * (1.0 / TOP)


def decode(q, code):
    return q.astype(jnp.int32).astype(F32) * step_of(code)


def copy_kernel(in_ref, out_ref):
    out_ref[...] = in_ref[...]


def fill_twice(pair_ref, near_ref, far_ref):
    n, rank = near_ref.shape[:2]
    for k, ref in enumerate((near_ref, far_ref)):
        pair_ref[k * n : (k + 1) * n, :rank, :] = ref[...]
        pair_ref[k * n : (k + 1) * n, rank:, :] = ref[...]


def shrink_kernel(slot_ref, x_ref, near_ref, far_ref, out_ref, down_ref):
    step = pl.program_id(0)
    n = near_ref.shape[0]

    @pl.when(step == 0)
    def _():
        down_ref[:n] = near_ref[...]
        down_ref[n:] = far_ref[...]

    tiles = x_ref.shape[0] // TILE
    for t in range(tiles):
        at = slice(t * TILE, (t + 1) * TILE)
        out_ref[:, at] = dot(down_ref[slot_ref[step * tiles + t]], x_ref[at, :], NT)


def forward_kernel(first, slot_ref, upslot_ref, place_ref, *refs):
    x_ref, w_ref, ndown_ref, fdown_ref, nup_ref, fup_ref, kept_ref = refs[:7]
    *sent_ref, down_ref, up_ref = refs[7:10] if len(refs) == 11 else refs[7:]
    sum_ref = refs[-1] if sent_ref else kept_ref
    step = pl.program_id(0)
    n, rows, cols = sum_ref.shape
    outer = kept_ref.shape[0]
    inner = n // outer
    tiles = rows // TILE
    rank = down_ref.shape[1] // 2

    @pl.when(step == 0)
    def _():
        fill_twice(down_ref, ndown_ref, fdown_ref)
        fill_twice(up_ref, nup_ref, fup_ref)

    base = dot(x_ref[...], w_ref[...])
    for t in range(tiles):
        at = slice(t * TILE, (t + 1) * TILE)
        tile = first + step * tiles + t
        pieces = split_halves(dot(x_ref[at, :], down_ref[slot_ref[tile]], NT), rank)
        total = base[at] + ADAPTER_SCALE * dot(pieces, up_ref[upslot_ref[tile]])
        for j in range(n):
            sum_ref[j, at, :] = total[:, j * cols : (j + 1) * cols]
    if not sent_ref:
        return
    mine = place_ref[1]
    for z in range(outer):
        kept_ref[z] = sum_ref[z * inner + mine]
        put(sent_ref[0].at[z, 0], *encode(sum_ref[z * inner + 1 - mine]))


def gradient_kernel(blocks, slot_ref, upslot_ref, order_ref, *refs):
    cots = refs[:blocks]
    x_ref, nup_ref, fup_ref, shrink_ref = refs[blocks : blocks + 4]
    all_ref, back_ref, ndown_ref, fdown_ref, nsum_ref, fsum_ref, up_ref, cot_ref, gdown_ref, gup_ref = refs[blocks + 4 :]
    step = pl.program_id(0)
    rows = x_ref.shape[0]
    tiles = rows // TILE
    rank = up_ref.shape[1] // 2

    @pl.when(step == 0)
    def _():
        fill_twice(up_ref, nup_ref, fup_ref)
        gdown_ref[...] = jnp.zeros_like(gdown_ref)
        gup_ref[...] = jnp.zeros_like(gup_ref)

    for j, block in enumerate(cots):
        wide = block.shape[1]
        if blocks == 1:
            cot_ref[...] = block[...]
        else:
            cot_ref[:, pl.ds(pl.multiple_of(order_ref[j] * wide, wide), wide)] = block[...]
    all_ref[...] = cot_ref[...]
    for t in range(tiles):
        at = slice(t * TILE, (t + 1) * TILE)
        tile = step * tiles + t
        slot, cot = slot_ref[tile], cot_ref[at, :]
        pieces = split_halves(dot(cot, up_ref[upslot_ref[tile]], NT), rank)
        back_ref[at, :] = pieces
        grad = dot(pieces, x_ref[at, :], TN)
        gdown_ref[slot] += grad[:rank] + grad[rank:]
        shrink = shrink_ref[:, at]
        high = shrink.astype(BF16)
        low = (shrink - high.astype(F32)).astype(BF16)
        gup_ref[slot] += dot(high, cot) + dot(low, cot)

    @pl.when(step == pl.num_programs(0) - 1)
    def _():
        n = ndown_ref.shape[0]
        ndown_ref[...] = gdown_ref[:n]
        fdown_ref[...] = gdown_ref[n:]
        nsum_ref[...] = gup_ref[:n]
        fsum_ref[...] = gup_ref[n:]


def token_kernel(slot_ref, cot_ref, w_ref, near_ref, far_ref, back_ref, after_ref, out_ref, down_ref):
    step = pl.program_id(0)
    tiles = cot_ref.shape[0] // TILE

    @pl.when(step == 0)
    def _():
        fill_twice(down_ref, near_ref, far_ref)

    base = dot(cot_ref[...], w_ref[...], NT)
    for t in range(tiles):
        at = slice(t * TILE, (t + 1) * TILE)
        slot = slot_ref[step * tiles + t]
        out_ref[at, :] = (base[at] + ADAPTER_SCALE * dot(back_ref[at, :], down_ref[slot])).astype(BF16)


def put(ref, q, code):
    rows = q.shape[0]
    ref[:rows, :] = q
    ref[rows:, :] = jnp.broadcast_to(code, (PAD, code.shape[1])).astype(jnp.int32).astype(jnp.int16)


def sum_kernel(coded, place_ref, *refs):
    total = refs[0][0]
    rows = total.shape[0]
    for ref in refs[1 : 1 + coded]:
        total = total + decode(ref[0, 0, :rows, :], ref[0, 0, rows : rows + 1, :])
    out_ref = refs[-1]
    if out_ref.dtype == BF16:
        out_ref[...] = total.astype(BF16)
    else:
        put(out_ref.at[0, 0], *encode(total))


def add_parts(place, block_rows, count, kept, coded, last=False):
    part, pick = kept
    rows, cols = part.shape[1:]
    blocks, held = rows // block_rows, block_rows + PAD

    def coded_spec(pick):
        return pl.BlockSpec((1, 1, held, cols), lambda i, b, p: (pick(i, p), b, 0, 0))

    in_specs = [pl.BlockSpec((1, block_rows, cols), lambda i, b, p: (pick(i, p), b, 0))]
    in_specs += [coded_spec(q) for _, q in coded]
    if last:
        out_shape = jax.ShapeDtypeStruct((rows, cols), BF16)
        out_spec = pl.BlockSpec((block_rows, cols), lambda i, b, p: (b, 0))
    else:
        out_shape = jax.ShapeDtypeStruct((count, blocks, held, cols), jnp.int16)
        out_spec = coded_spec(lambda i, p: i)
    return pl.pallas_call(
        functools.partial(sum_kernel, len(coded)),
        grid_spec=pltpu.PrefetchScalarGridSpec(
            num_scalar_prefetch=1, grid=(count, blocks), in_specs=in_specs, out_specs=out_spec
        ),
        out_shape=out_shape,
        cost_estimate=pl.CostEstimate(flops=0, bytes_accessed=count * rows * cols * 8, transcendentals=0),
        name="add_parts",
    )(place, part, *[a for a, _ in coded])


def pack_kernel(gdown_ref, rdown_ref, gup_ref, rup_ref, out_ref):
    rank, width = gdown_ref.shape[1:]
    own = gup_ref.shape[1]
    groups = gup_ref.shape[2] // width
    q, code = encode(gdown_ref[0] + rdown_ref[0])
    out_ref[0, :rank, :] = q
    tail, codes = [], [code]
    up = gup_ref[0] + rup_ref[0]
    for g in range(groups):
        q, code = encode(up[:, g * width : (g + 1) * width])
        tail.append(q.astype(jnp.int32))
        codes.append(code)
    row = lax.broadcasted_iota(jnp.int32, (PAD - groups * own, width), 0)
    last = jnp.zeros(row.shape, F32)
    for g, code in enumerate(codes):
        last = jnp.where(row == g, code, last)
    out_ref[0, rank:, :] = jnp.concatenate([*tail, last.astype(jnp.int32)], axis=0).astype(jnp.int16)


def unpack_kernel(in_ref, down_ref, up_ref):
    width = in_ref.shape[2]
    own = up_ref.shape[1]
    groups = up_ref.shape[2] // width
    rank = down_ref.shape[1]
    tail = in_ref[0, rank:, :].astype(jnp.int32).astype(F32)
    steps = jnp.exp2(tail[groups * own :] * (1.0 / STEPS)) * (ADAPTER_SCALE / TOP)
    down_ref[0] = in_ref[0, :rank, :].astype(jnp.int32).astype(F32) * steps[:1]
    for g in range(groups):
        up_ref[0, :, g * width : (g + 1) * width] = tail[g * own : (g + 1) * own] * steps[g + 1 : g + 2]


def body(
    tokens, frozen_weight, cotangent, adapter_down, adapter_up, seg_tiles, seg_adapter, owner_slot
):
    rows, width = tokens.shape
    cols = cotangent.shape[1]
    n = lax.axis_size("mp")
    n_data = lax.axis_size("dp")
    _, entire_width, rank = adapter_down.shape
    out_width = adapter_up.shape[2]
    slots = n_data * n
    tile_count = rows // TILE
    inner = INNER
    outer = n // inner
    me = lax.axis_index("mp")
    my_outer, my_inner = me // inner, me % inner
    other = 1 - my_inner
    my_data = lax.axis_index("dp")
    swap = [(i, i ^ 1) for i in range(n)]
    ring = [(i, (i + inner) % n) for i in range(n)]
    cores = [(i, 1 - i) for i in range(n_data)]

    place = jnp.stack([my_outer, my_inner]).astype(jnp.int32)

    block_rows = 4 * TILE
    steps = rows // block_rows
    sizes = [steps // 4, steps // 4, steps - 2 * (steps // 4)]
    starts = [sum(sizes[:c]) for c in range(len(sizes))]
    chunks = len(sizes)
    once = pl.Buffered(1)
    params = pltpu.CompilerParams(vmem_limit_bytes=VMEM)
    held = block_rows + PAD
    tie = lax.optimization_barrier

    ups = [adapter_up]
    for s in range(1, outer):
        ups.append(lax.ppermute(adapter_up, "mp", [(i, (i + s * inner) % n) for i in range(n)]))
    cut = pl.pallas_call(
        copy_kernel,
        grid=(n,),
        in_specs=[pl.BlockSpec((1, rank, width), lambda i: (0, 0, i))],
        out_specs=pl.BlockSpec((1, rank, width), lambda i: (i, 0, 0)),
        out_shape=jax.ShapeDtypeStruct((n, rank, width), BF16),
        name="cut_down",
    )(jnp.swapaxes(adapter_down, 1, 2))

    ends = jnp.cumsum(seg_tiles[0])
    positions = jnp.arange(tile_count, dtype=jnp.int32)
    segment = jnp.sum((positions[:, None] >= ends[None, :]).astype(jnp.int32), axis=1)
    seg_pick = segment[:, None] == jnp.arange(ends.shape[0], dtype=jnp.int32)[None, :]
    tile_adapter = jnp.sum(jnp.where(seg_pick, seg_adapter[:, 0][None, :], 0), axis=1)
    adapt_pick = tile_adapter[:, None] == jnp.arange(slots, dtype=jnp.int32)[None, :]
    tile_slot = jnp.sum(jnp.where(adapt_pick, owner_slot[None, :], 0), axis=1)
    core, owner = (tile_slot // n + my_data) % n_data, tile_slot % n
    tile_slot = core * n + owner
    tile_up = core * n + ((owner + my_inner) % inner) * outer + (my_outer - owner // inner) % outer

    def whole(*shape):
        return pl.BlockSpec(shape, lambda i, *_: (0,) * len(shape), pipeline_mode=once)

    def strip(wide, first=0):
        return pl.BlockSpec((block_rows, wide), lambda i, *_: (first + i, 0))

    def forward(c, sends):
        kept = outer if sends else n
        blocks, start = sizes[c], starts[c]
        chunk_rows = blocks * block_rows
        coded_spec = [pl.BlockSpec((outer, 1, held, cols), lambda i, *_: (0, i, 0, 0))]
        coded_shape = [jax.ShapeDtypeStruct((outer, blocks, held, cols), jnp.int16)]
        return pl.pallas_call(
            functools.partial(forward_kernel, start * (block_rows // TILE)),
            grid_spec=pltpu.PrefetchScalarGridSpec(
                num_scalar_prefetch=3,
                grid=(blocks,),
                in_specs=[
                    strip(width, start),
                    whole(width, out_width),
                    whole(n, rank, width),
                    whole(n, rank, width),
                    whole(n, rank, out_width),
                    whole(n, rank, out_width),
                ],
                out_specs=[
                    pl.BlockSpec((kept, block_rows, cols), lambda i, *_: (0, i, 0)),
                ]
                + coded_spec * sends,
                scratch_shapes=[
                    pltpu.VMEM((slots, 2 * rank, width), BF16),
                    pltpu.VMEM((slots, 2 * rank, out_width), BF16),
                ]
                + [pltpu.VMEM((n, block_rows, cols), F32)] * sends,
            ),
            out_shape=[
                jax.ShapeDtypeStruct((kept, chunk_rows, cols), F32),
            ]
            + coded_shape * sends,
            compiler_params=params,
            cost_estimate=pl.CostEstimate(
                flops=4 * chunk_rows * width * out_width, bytes_accessed=chunk_rows * width * 6, transcendentals=0
            ),
            name="forward",
        )(tile_slot, tile_up, place, tokens, frozen_weight, near_down, far_down, near_up, far_up)

    def swapped(x):
        return lax.ppermute(x, "mp", swap)

    def shifted(x):
        return lax.ppermute(x, "mp", ring)

    def behind(back):
        return lambda i, p: lax.rem(p[0] - back + outer, outer)

    def first(i, p):
        return 0

    def ring_step(s, kept, near, run):
        at = behind(s % outer)
        coded = [(near, at)] + [(r, first) for r in run]
        return add_parts(place, block_rows, 1, (kept, at), coded, last=s == outer)

    def pair_step(s, kept, run):
        at = behind(s)
        pick = (kept, lambda i, p: at(i, p) * inner + i)
        return add_parts(place, block_rows, inner, pick, [(r, lambda i, p: i) for r in run])

    def pair_end(kept, run, got):
        def whose(i, p):
            return p[1] if got else 1 - p[1]

        coded = [(run, whose)] + [(g, first) for g in got]
        return add_parts(place, block_rows, 1, (kept, lambda i, p: p[0] * inner + whose(i, p)), coded, last=bool(got))

    order = []
    for s in range(outer):
        at = ((my_outer - s) % outer) * inner
        order += [at + my_inner, at + other]
    cots = [cotangent, swapped(cotangent)]
    block, cots[-1], ups, cut = tie((shifted(cotangent), cots[-1], ups, cut))
    ups = jnp.concatenate(ups, axis=0)
    near_up = jnp.concatenate([ups, swapped(ups)], axis=0)
    near_down = lax.all_to_all(cut, "mp", split_axis=0, concat_axis=0, tiled=True)
    cots += [block, swapped(block)]
    if outer > 2:
        block = shifted(block)
    block, cots[-1], near_up, near_down = tie((block, cots[-1], near_up, near_down))
    far_up, far_down = (lax.ppermute(a, "dp", cores) for a in (near_up, near_down))
    own = rank // n
    half = rank // inner
    shrink = pl.pallas_call(
        shrink_kernel,
        grid_spec=pltpu.PrefetchScalarGridSpec(
            num_scalar_prefetch=1,
            grid=(steps // 2,),
            in_specs=[
                pl.BlockSpec((2 * block_rows, width), lambda i, s: (i, 0)),
                whole(n, rank, width),
                whole(n, rank, width),
            ],
            out_specs=pl.BlockSpec((rank, 2 * block_rows), lambda i, s: (0, i)),
            scratch_shapes=[pltpu.VMEM((slots, rank, width), BF16)],
        ),
        out_shape=jax.ShapeDtypeStruct((rank, rows), F32),
        compiler_params=params,
        cost_estimate=pl.CostEstimate(flops=0, bytes_accessed=rows * width * 2, transcendentals=0),
        name="shrink",
    )(tile_slot, tokens, near_down, far_down)
    mine = lax.dynamic_slice_in_dim(shrink, my_inner * half, half, 0)
    theirs = swapped(lax.dynamic_slice_in_dim(shrink, other * half, half, 0))
    parts = [forward(c, c < chunks - 1) for c in range(chunks)]
    near, outs = {}, {}
    runs = {c: [] for c in range(chunks)}

    done = {c: 0 for c in range(chunks)}

    def advance(c, through=outer):
        pair = c == chunks - 1
        while done[c] < min(through, outer - pair):
            done[c] += 1
            if pair:
                runs[c] = [shifted(pair_step(done[c], parts[c][0], runs[c]))]
                continue
            total = ring_step(done[c], parts[c][0], near[c], runs[c])
            if done[c] == outer:
                outs[c] = total
            else:
                runs[c] = [shifted(total)]

    last = chunks - 1
    for s in range(2, outer):
        cots += [block, swapped(block)]
        if s < outer - 1:
            block = shifted(block)
        if s == 2:
            block, cots[-1], parts[last], theirs = tie((block, cots[-1], parts[last], theirs))
    mine += theirs
    shrink = [lax.dynamic_slice_in_dim(mine, my_outer * own, own, 0)]
    for s in range(1, outer):
        theirs = lax.dynamic_slice_in_dim(mine, ((my_outer + s) % outer) * own, own, 0)
        shrink.append(lax.ppermute(theirs, "mp", [(i, (i + s * inner) % n) for i in range(n)]))
    advance(last, 1)
    cots[-1], parts[0], parts[1], runs, shrink = tie((cots[-1], parts[0], parts[1], runs, shrink))
    shrink = sum(shrink[1:], shrink[0])
    near[0] = swapped(parts[0][1])
    if cols % 128:
        natural = jnp.stack(cots)[jnp.argsort(jnp.stack(order))]
        cots = [jnp.transpose(natural, (1, 0, 2)).reshape(rows, out_width)]
    cot_all, back, gdown, rdown, gup, rup = pl.pallas_call(
        functools.partial(gradient_kernel, len(cots)),
        grid_spec=pltpu.PrefetchScalarGridSpec(
            num_scalar_prefetch=3,
            grid=(steps,),
            in_specs=[strip(a.shape[1]) for a in cots]
            + [strip(width), whole(n, rank, out_width), whole(n, rank, out_width)]
            + [pl.BlockSpec((own, block_rows), lambda i, *_: (0, i))],
            out_specs=[
                strip(out_width),
                strip(2 * rank),
                whole(n, rank, width),
                whole(n, rank, width),
                whole(n, own, out_width),
                whole(n, own, out_width),
            ],
            scratch_shapes=[
                pltpu.VMEM((slots, 2 * rank, out_width), BF16),
                pltpu.VMEM((block_rows, out_width), BF16),
                pltpu.VMEM((slots, rank, width), F32),
                pltpu.VMEM((slots, own, out_width), F32),
            ],
        ),
        out_shape=[
            jax.ShapeDtypeStruct((rows, out_width), BF16),
            jax.ShapeDtypeStruct((rows, 2 * rank), BF16),
            jax.ShapeDtypeStruct((n, rank, width), F32),
            jax.ShapeDtypeStruct((n, rank, width), F32),
            jax.ShapeDtypeStruct((n, own, out_width), F32),
            jax.ShapeDtypeStruct((n, own, out_width), F32),
        ],
        compiler_params=params,
        cost_estimate=pl.CostEstimate(
            flops=2 * rows * width * out_width, bytes_accessed=rows * (width * 2 + out_width * 4), transcendentals=0
        ),
        name="gradients",
    )(tile_slot, tile_up, jnp.stack(order).astype(jnp.int32), *cots, tokens, near_up, far_up, shrink)
    advance(last, 2)
    near[0], gdown, rdown, gup, rup, runs = tie((near[0], gdown, rdown, gup, rup, runs))
    near[1] = swapped(parts[1][1])
    advance(last)

    rdown = lax.ppermute(rdown, "dp", cores)
    rup = lax.ppermute(rup, "dp", cores)
    packed_rows = rank + PAD
    packed = pl.pallas_call(
        pack_kernel,
        grid=(n,),
        in_specs=[
            pl.BlockSpec((1, rank, width), lambda i: (i, 0, 0)),
            pl.BlockSpec((1, rank, width), lambda i: (i, 0, 0)),
            pl.BlockSpec((1, own, out_width), lambda i: (i, 0, 0)),
            pl.BlockSpec((1, own, out_width), lambda i: (i, 0, 0)),
        ],
        out_specs=pl.BlockSpec((1, packed_rows, width), lambda i: (i, 0, 0)),
        out_shape=jax.ShapeDtypeStruct((n, packed_rows, width), jnp.int16),
        name="pack_gradients",
    )(gdown, rdown, gup, rup)
    landed = lax.all_to_all(packed, "mp", split_axis=0, concat_axis=0, tiled=True)
    down_gradient, up_gradient = pl.pallas_call(
        unpack_kernel,
        grid=(n,),
        in_specs=[pl.BlockSpec((1, packed_rows, width), lambda i: (i, 0, 0))],
        out_specs=[
            pl.BlockSpec((1, rank, width), lambda i: (0, 0, i)),
            pl.BlockSpec((1, own, out_width), lambda i: ((i % inner) * outer + i // inner, 0, 0)),
        ],
        out_shape=[
            jax.ShapeDtypeStruct((1, rank, entire_width), F32),
            jax.ShapeDtypeStruct((n, own, out_width), F32),
        ],
        name="unpack_gradients",
    )(landed)

    token_gradient = pl.pallas_call(
        token_kernel,
        grid_spec=pltpu.PrefetchScalarGridSpec(
            num_scalar_prefetch=1,
            grid=(steps,),
            in_specs=[
                strip(out_width),
                whole(width, out_width),
                whole(n, rank, width),
                whole(n, rank, width),
                strip(2 * rank),
                pl.BlockSpec(memory_space=pl.ANY),
            ],
            out_specs=strip(width),
            scratch_shapes=[pltpu.VMEM((slots, 2 * rank, width), BF16)],
        ),
        out_shape=jax.ShapeDtypeStruct((rows, width), BF16),
        compiler_params=params,
        cost_estimate=pl.CostEstimate(
            flops=3 * rows * width * out_width, bytes_accessed=rows * (width * 2 + out_width * 2), transcendentals=0
        ),
        name="token_gradient",
    )(tile_slot, cot_all, frozen_weight, near_down, far_down, back, packed)
    kept, run = parts[last][0], runs[last][0]
    outs[last] = pair_end(kept, run, [swapped(pair_end(kept, run, []))])
    near, token_gradient = tie((near, token_gradient))
    for c in range(last):
        advance(c)
    output = jnp.concatenate([outs[c] for c in range(chunks)], axis=0)

    up_gradient = up_gradient.reshape(1, rank, out_width)
    return output, token_gradient, jnp.swapaxes(down_gradient, 1, 2), up_gradient


def solution(mesh):
    placed = (
        P(("groups", "dp"), "mp"),
        P("mp", None),
        P(("groups", "dp"), "mp"),
        P(("groups", "dp", "mp"), None, None),
        P(("groups", "dp", "mp"), None, None),
        P(("groups", "dp"), None),
        P(("groups", "dp"), None),
        P("groups"),
    )
    return jax.shard_map(
        body,
        mesh=mesh,
        in_specs=placed,
        out_specs=(
            P(("groups", "dp"), "mp"),
            P(("groups", "dp"), "mp"),
            P(("groups", "dp", "mp"), None, None),
            P(("groups", "dp", "mp"), None, None),
        ),
        check_vma=False,
    )
```

time: 395 us -> 331 us (0.84)
  waiting for transfers between devices: 157 us -> 98.1 us
  starting transfers between devices: 65.8 us -> 54.5 us
  Pallas kernels: 145 us -> 153 us
    ppermute x26, waiting for transfers between devices: 129 us -> 77.2 us  [the longest x9 43 us: swapped(): return lax.ppermute(x, 'mp', swap)]
    ppermute x26, starting transfers between devices: 49.2 us -> 35.7 us  [the longest x12 21.7 us: shifted(): return lax.ppermute(x, 'mp', ring)]
    pallas_call x21 -> x18, Pallas kernels: 89.4 us -> 96.7 us  [the longest x13 49.2 us: add_parts(): pl.pallas_call(functools.partial(sum_kernel, len(coded)), grid_spec=pltpu...]
    ppermute x3, waiting for transfers between devices: 27.9 us -> 20.8 us  [body(): lax.ppermute(adapter_up, 'mp', [(i, (i + s * inner) % n) for i in range(n)])]
    unnamed x72 -> x62, local copies, waits for them, and re-layouts: 17.1 us -> 14.8 us
  transfers between devices with their start and end apart: 33 -> 33, of which waited for: 10 -> 6; matrix products, arithmetic and copies ran while one was open for 2% -> 2% of each run, Pallas kernels for 34% -> 43%
where the time goes in v3:
time: 331 us; the launch traced here: 329 us
  Pallas kernels  153 us (46%)
  waiting for transfers between devices  98.1 us (30%)
  starting transfers between devices  54.5 us (16%)
  local copies, waits for them, and re-layouts  16.7 us (5%)
  other arithmetic  5.85 us (2%)
    pallas_call x13, Pallas kernels, add_parts(): pl.pallas_call(functools.partial(sum_kernel, len(coded)), grid_spec=pltpu...  49.2 us
    ppermute x9, waiting for transfers between devices, swapped(): return lax.ppermute(x, 'mp', swap)  43 us
    pallas_call x3, Pallas kernels, forward(): pl.pallas_call(functools.partial(forward_kernel, start * (block_rows // T...  34.3 us
    pallas_call x1, Pallas kernels, body(): pl.pallas_call(functools.partial(gradient_kernel, len(cots)), grid_spec=p...  27.4 us
    ppermute x3, waiting for transfers between devices, body(): lax.ppermute(theirs, 'mp', [(i, (i + s * inner) % n) for i in range(n)])  22.9 us
    ppermute x12, starting transfers between devices, shifted(): return lax.ppermute(x, 'mp', ring)  21.7 us
    ppermute x3, waiting for transfers between devices, body(): lax.ppermute(adapter_up, 'mp', [(i, (i + s * inner) % n) for i in range(n)])  20.8 us
    pallas_call x1, Pallas kernels, body(): pl.pallas_call(token_kernel, grid_spec=pltpu.PrefetchScalarGridSpec(num_s...  17.2 us
  transfers between devices with their start and end apart: 33, of which 6 were waited for; matrix products, arithmetic and copies ran while one was open for 2% of the time, Pallas kernels for 43%

profile of v3, /device:TPU:0, one launch (start us, length us, event | category | flops | bytes accessed | tf_op | source)
XLA Modules:
  0.0 329.0 jit_solution(3932956747915325307)
XLA Ops:
  0.6 3.1 collective-permute-start
  5.2 2.6 collective-permute-start.3
  8.0 3.6 %collective-permute-start.4 = (bf16[1,64,1024]{2,1,0:T(8,128)(2,1)}, bf16[1,64,1024]{2,1,0:T(8,128)(2,1)S(1)}, u32[]{:S(2)}, u32[]{:S(2)}) collective-permute-start(bf16[1,64,1024]{2,1,0:T(8,128)(2,1)} %param.12), channel_id=1, source_target_pairs={{0,6},{1,7},{2,0},{3,1},{4,2},{5,3},{6,4},{7,5},{8,14},{9,15},{10,... | collective-permute-start | bytes 393224 | tf_op jit(solution)/shard_map/ppermute | solution.py:277
  11.6 5.2 %cut_down.1 = bf16[8,64,1024]{2,1,0:T(8,128)(2,1)} custom-call(bf16[1,64,8192]{2,1,0:T(8,128)(2,1)} %bitcast.15), custom_call_target="tpu_custom_call" | custom-call | tf_op jit(solution)/shard_map/cut_down/pallas_call | solution.py:278
  16.8 20.8 %collective-permute-done.3 = bf16[1,64,1024]{2,1,0:T(8,128)(2,1)S(1)} collective-permute-done((bf16[1,64,1024]{2,1,0:T(8,128)(2,1)}, bf16[1,64,1024]{2,1,0:T(8,128)(2,1)S(1)}, u32[]{:S(2)}, u32[]{:S(2)}) %collective-permute-start.3) | collective-permute-done | bytes 131104 | tf_op jit(solution)/shard_map/ppermute | solution.py:277
  38.7 5.6 %all-to-all-start = ((bf16[8,64,1024]{2,1,0:T(8,128)(2,1)}), bf16[8,64,1024]{2,1,0:T(8,128)(2,1)S(1)}, u32[]{:S(2)}, u32[]{:S(2)}) async-start(bf16[8,64,1024]{2,1,0:T(8,128)(2,1)} %cut_down.1), calls=%async_computation | async-start | bytes 2097152 | tf_op jit(solution)/shard_map/all_to_all | solution.py:381
  48.7 43.0 %collective-permute-done.7 = bf16[4,64,1024]{2,1,0:T(8,128)(2,1)S(1)} collective-permute-done((bf16[4,64,1024]{2,1,0:T(8,128)(2,1)S(1)}, bf16[4,64,1024]{2,1,0:T(8,128)(2,1)S(1)}, u32[]{:S(2)}, u32[]{:S(2)}) %collective-permute-start.7) | collective-permute-done | bytes 524320 | tf_op jit(solution)/shard_map/ppermute | solution.py:345
  100.2 8.1 %shrink.1 = f32[64,4096]{1,0:T(8,128)} custom-call(s32[32]{0:T(128)} %fusion.7.slot_ref, bf16[4096,1024]{1,0:T(8,128)(2,1)} %refs_8_.1, bf16[8,64,1024]{2,1,0:T(8,128)(2,1)} %copy-done.4, bf16[8,64,1024]{2,1,0:T(8,128)(2,1)} %copy-done.9), custom_call_target="tpu_custom_call" | custom-call | bytes 8388608 | tf_op jit(solution)/shard_map/shrink/pallas_call | solution.py:389
  111.9 13.9 %forward.3.refs_0_ = f32[8,2048,128]{2,1,0:T(8,128)} custom-call(s32[32]{0:T(128)} %fusion.7.slot_ref, s32[32]{0:T(128)} %get-tuple-element.96.upslot_ref, s32[2]{0:T(128)} %pad_add_fusion.place_ref, bf16[4096,1024]{1,0:T(8,128)(2,1)} %refs_8_.1, bf16[1024,1024]{1,0:T(8,128)(2,1)} %w_ref.1, bf16[8,64,1024]{2,1,0:T(8,128)(2,1)} %copy-done.4, ...), custom_call_target="tpu_custom_call" | custom-call | flops 8589934592 | bytes 12582912 | tf_op jit(solution)/shard_map/forward/pallas_call | solution.py:310
  125.8 10.2 %forward.5 = (f32[4,1024,128]{2,1,0:T(8,128)}, s16[4,2,528,128]{3,2,1,0:T(8,128)(2,1)}) custom-call(s32[32]{0:T(128)} %fusion.7.slot_ref, s32[32]{0:T(128)} %get-tuple-element.96.upslot_ref, s32[2]{0:T(128)} %pad_add_fusion.place_ref, bf16[4096,1024]{1,0:T(8,128)(2,1)} %refs_8_.1, bf16[1024,1024]{1,0:T(8,128)(2,1)} %w_ref.1, bf16[8,64,1024]{2,1,0:T(8,128)(2,1)} %copy-done.4, ...), custom_call_target="tpu_custom_call" | custom-call | flops 4294967296 | bytes 6291456 | tf_op jit(solution)/shard_map/forward/pallas_call | solution.py:310
  136.6 6.3 %add_parts.13 = s16[2,4,528,128]{3,2,1,0:T(8,128)(2,1)} custom-call(s32[2]{0:T(128)} %pad_add_fusion.place_ref, f32[8,2048,128]{2,1,0:T(8,128)} %forward.3.refs_0_), custom_call_target="tpu_custom_call" | custom-call | bytes 4194304 | tf_op jit(solution)/shard_map/add_parts/pallas_call | solution.py:200
  147.8 10.2 %forward.4 = (f32[4,1024,128]{2,1,0:T(8,128)}, s16[4,2,528,128]{3,2,1,0:T(8,128)(2,1)}) custom-call(s32[32]{0:T(128)} %fusion.7.slot_ref, s32[32]{0:T(128)} %get-tuple-element.96.upslot_ref, s32[2]{0:T(128)} %pad_add_fusion.place_ref, bf16[4096,1024]{1,0:T(8,128)(2,1)} %refs_8_.1, bf16[1024,1024]{1,0:T(8,128)(2,1)} %w_ref.1, bf16[8,64,1024]{2,1,0:T(8,128)(2,1)} %copy-done.4, ...), custom_call_target="tpu_custom_call" | custom-call | flops 4294967296 | bytes 6291456 | tf_op jit(solution)/shard_map/forward/pallas_call | solution.py:310
  157.9 13.9 %collective-permute-done.17 = f32[8,4096]{1,0:T(8,128)S(1)} collective-permute-done((f32[8,4096]{1,0:T(8,128)S(1)}, f32[8,4096]{1,0:T(8,128)S(1)}, u32[]{:S(2)}, u32[]{:S(2)}) %collective-permute-start.17) | collective-permute-done | bytes 131104 | tf_op jit(solution)/shard_map/ppermute | solution.py:439
  171.8 9.1 %collective-permute-done.16 = f32[8,4096]{1,0:T(8,128)S(1)} collective-permute-done((f32[8,4096]{1,0:T(8,128)S(1)}, f32[8,4096]{1,0:T(8,128)S(1)}, u32[]{:S(2)}, u32[]{:S(2)}) %collective-permute-start.16) | collective-permute-done | bytes 131104 | tf_op jit(solution)/shard_map/ppermute | solution.py:439
  182.5 6.6 %add_parts.14 = s16[2,4,528,128]{3,2,1,0:T(8,128)(2,1)} custom-call(s32[2]{0:T(128)} %pad_add_fusion.place_ref, f32[8,2048,128]{2,1,0:T(8,128)} %forward.3.refs_0_, s16[2,4,528,128]{3,2,1,0:T(8,128)(2,1)} %copy-done.7), custom_call_target="tpu_custom_call" | custom-call | bytes 4194304 | tf_op jit(solution)/shard_map/add_parts/pallas_call | solution.py:200
  192.2 27.4 %gradients.1 = (bf16[4096,1024]{1,0:T(8,128)(2,1)}, bf16[4096,128]{1,0:T(8,128)(2,1)}, f32[8,64,1024]{2,1,0:T(8,128)}, f32[8,64,1024]{2,1,0:T(8,128)}, f32[8,8,1024]{2,1,0:T(8,128)}, /*index=5*/f32[8,8,1024]{2,1,0:T(8,128)}) custom-call(s32[32]{0:T(128)} %fusion.7.slot_ref, s32[32]{0:T(128)} %get-tuple-element.96.upslot_ref, s32[8]{0:T(128)} %stack.47.order_ref, ...), custom_call_target="tpu_custom_call" | custom-call | flops 8589934592 | bytes 25165824 | tf_op jit(solution)/shard_map/gradients/pallas_call | solution.py:447
  220.7 6.6 %add_parts.23 = s16[2,4,528,128]{3,2,1,0:T(8,128)(2,1)} custom-call(s32[2]{0:T(128)} %pad_add_fusion.place_ref, f32[8,2048,128]{2,1,0:T(8,128)} %forward.3.refs_0_, s16[2,4,528,128]{3,2,1,0:T(8,128)(2,1)} %copy-done.8), custom_call_target="tpu_custom_call" | custom-call | bytes 4194304 | tf_op jit(solution)/shard_map/add_parts/pallas_call | solution.py:200
  227.7 6.1 %pack_gradients.1.after_ref = s16[8,80,1024]{2,1,0:T(8,128)(2,1)} custom-call(f32[8,64,1024]{2,1,0:T(8,128)} %get-tuple-element.85.gdown_ref, f32[8,64,1024]{2,1,0:T(8,128)} %collective-permute-done.21.rdown_ref, f32[8,8,1024]{2,1,0:T(8,128)} %get-tuple-element.87.gup_ref, f32[8,8,1024]{2,1,0:T(8,128)} %collective-permute-done.22.rup_ref), custom_call_target="tpu_custom_call" | custom-call | tf_op jit(solution)/shard_map/pack_gradients/pallas_call | solution.py:492
  233.8 6.2 %all-to-all-start.1 = ((s16[8,80,1024]{2,1,0:T(8,128)(2,1)}), s16[8,80,1024]{2,1,0:T(8,128)(2,1)S(1)}, u32[]{:S(2)}, u32[]{:S(2)}) async-start(s16[8,80,1024]{2,1,0:T(8,128)(2,1)} %pack_gradients.1.after_ref), calls=%async_computation.1 | async-start | bytes 2621440 | tf_op jit(solution)/shard_map/all_to_all | solution.py:505
  240.0 17.2 %token_gradient.1 = bf16[4096,1024]{1,0:T(8,128)(2,1)} custom-call(s32[32]{0:T(128)} %fusion.7.slot_ref, bf16[4096,1024]{1,0:T(8,128)(2,1)} %get-tuple-element.83.cot_ref, bf16[1024,1024]{1,0:T(8,128)(2,1)} %w_ref.1, bf16[8,64,1024]{2,1,0:T(8,128)(2,1)} %copy-done.4, bf16[8,64,1024]{2,1,0:T(8,128)(2,1)} %copy-done.9, ...), custom_call_target="tpu_custom_call" | custom-call | flops 12884901888 | bytes 16777216 | tf_op jit(solution)/shard_map/token_gradient/pallas_call | solution.py:521
  262.8 2.6 add_parts.15
  267.9 4.2 %add_parts.24 = s16[1,4,528,128]{3,2,1,0:T(8,128)(2,1)} custom-call(s32[2]{0:T(128)} %pad_add_fusion.place_ref, f32[8,2048,128]{2,1,0:T(8,128)} %forward.3.refs_0_, s16[2,4,528,128]{3,2,1,0:T(8,128)(2,1)} %copy-done.3), custom_call_target="tpu_custom_call" | custom-call | bytes 2097152 | tf_op jit(solution)/shard_map/add_parts/pallas_call | solution.py:200
  273.5 9.7 %collective-permute-done.26.refs_2_ = s16[1,2,528,128]{3,2,1,0:T(8,128)(2,1)S(1)} collective-permute-done((s16[1,2,528,128]{3,2,1,0:T(8,128)(2,1)}, s16[1,2,528,128]{3,2,1,0:T(8,128)(2,1)S(1)}, u32[]{:S(2)}, u32[]{:S(2)}) %collective-permute-start.26) | collective-permute-done | bytes 270368 | tf_op jit(solution)/shard_map/ppermute | solution.py:348
  283.9 2.7 add_parts.20
  286.6 3.7 %collective-permute-start.27 = (s16[1,2,528,128]{3,2,1,0:T(8,128)(2,1)}, s16[1,2,528,128]{3,2,1,0:T(8,128)(2,1)S(1)}, u32[]{:S(2)}, u32[]{:S(2)}) collective-permute-start(s16[1,2,528,128]{3,2,1,0:T(8,128)(2,1)} %add_parts.20), channel_id=1, source_target_pairs={{0,2},{1,3},{2,4},{3,5},{4,6},{5,7},{6,0},{7,1},{8,10},{9,11},{10,... | collective-permute-start | bytes 811016 | tf_op jit(solution)/shard_map/ppermute | solution.py:348
  291.0 2.7 add_parts.16
  296.8 2.7 add_parts.21
  303.6 2.7 add_parts.17
  309.3 4.2 %add_parts.25 = bf16[2048,128]{1,0:T(8,128)(2,1)} custom-call(s32[2]{0:T(128)} %pad_add_fusion.place_ref, f32[8,2048,128]{2,1,0:T(8,128)} %forward.3.refs_0_, s16[2,4,528,128]{3,2,1,0:T(8,128)(2,1)} %copy-done.3, s16[1,4,528,128]{3,2,1,0:T(8,128)(2,1)} %copy-done.11), custom_call_target="tpu_custom_call" | custom-call | bytes 2097152 | tf_op jit(solution)/shard_map/add_parts/pallas_call | solution.py:200
  314.3 2.7 add_parts.22
  317.7 2.7 add_parts.18
  323.4 5.6 %unpack_gradients.1 = (f32[1,64,8192]{2,1,0:T(8,128)}, f32[8,8,1024]{2,1,0:T(8,128)}) custom-call(s16[8,80,1024]{2,1,0:T(8,128)(2,1)} %copy-done.2), custom_call_target="tpu_custom_call" | custom-call | tf_op jit(solution)/shard_map/unpack_gradients/pallas_call | solution.py:506
  (135 shorter events, 56.5 us)
Async XLA Ops:
  0.6 37.0 %collective-permute-start = (bf16[4096,128]{1,0:T(8,128)(2,1)}, bf16[4096,128]{1,0:T(8,128)(2,1)S(1)}, u32[]{:S(2)}, u32[]{:S(2)}) collective-permute-start(bf16[4096,128]{1,0:T(8,128)(2,1)} %refs_0_.7), channel_id=1, source_target_pairs={{0,2},{1,3},{2,4},{3,5},{4,6},{5,7},{6,0},{7,1},{8,10},{9,11},{10,... | collective-permute-start | bytes 3145736 | tf_op jit(solution)/shard_map/ppermute | solution.py:348
  3.7 34.0 %collective-permute-start.1 = (bf16[4096,128]{1,0:T(8,128)(2,1)}, bf16[4096,128]{1,0:T(8,128)(2,1)S(1)}, u32[]{:S(2)}, u32[]{:S(2)}) collective-permute-start(bf16[4096,128]{1,0:T(8,128)(2,1)} %refs_0_.7), channel_id=1, source_target_pairs={{0,1},{1,0},{2,3},{3,2},{4,5},{5,4},{6,7},{7,6},{8,9},{9,8},{10,11... | collective-permute-start | bytes 3145736 | tf_op jit(solution)/shard_map/ppermute | solution.py:345
  5.2 32.4 %collective-permute-start.3 = (bf16[1,64,1024]{2,1,0:T(8,128)(2,1)}, bf16[1,64,1024]{2,1,0:T(8,128)(2,1)S(1)}, u32[]{:S(2)}, u32[]{:S(2)}) collective-permute-start(bf16[1,64,1024]{2,1,0:T(8,128)(2,1)} %param.12), channel_id=1, source_target_pairs={{0,4},{1,5},{2,6},{3,7},{4,0},{5,1},{6,2},{7,3},{8,12},{9,13},{10,... | collective-permute-start | bytes 393224 | tf_op jit(solution)/shard_map/ppermute | solution.py:277
  7.8 29.9 %collective-permute-start.2 = (bf16[1,64,1024]{2,1,0:T(8,128)(2,1)}, bf16[1,64,1024]{2,1,0:T(8,128)(2,1)S(1)}, u32[]{:S(2)}, u32[]{:S(2)}) collective-permute-start(bf16[1,64,1024]{2,1,0:T(8,128)(2,1)} %param.12), channel_id=1, source_target_pairs={{0,2},{1,3},{2,4},{3,5},{4,6},{5,7},{6,0},{7,1},{8,10},{9,11},{10,... | collective-permute-start | bytes 393224 | tf_op jit(solution)/shard_map/ppermute | solution.py:277
  8.0 29.6 %collective-permute-start.4 = (bf16[1,64,1024]{2,1,0:T(8,128)(2,1)}, bf16[1,64,1024]{2,1,0:T(8,128)(2,1)S(1)}, u32[]{:S(2)}, u32[]{:S(2)}) collective-permute-start(bf16[1,64,1024]{2,1,0:T(8,128)(2,1)} %param.12), channel_id=1, source_target_pairs={{0,6},{1,7},{2,0},{3,1},{4,2},{5,3},{6,4},{7,5},{8,14},{9,15},{10,... | collective-permute-start | bytes 393224 | tf_op jit(solution)/shard_map/ppermute | solution.py:277
  38.7 55.0 %all-to-all-start = ((bf16[8,64,1024]{2,1,0:T(8,128)(2,1)}), bf16[8,64,1024]{2,1,0:T(8,128)(2,1)S(1)}, u32[]{:S(2)}, u32[]{:S(2)}) async-start(bf16[8,64,1024]{2,1,0:T(8,128)(2,1)} %cut_down.1), calls=%async_computation | async-start | bytes 2097152 | tf_op jit(solution)/shard_map/all_to_all | solution.py:381
  44.4 47.4 %collective-permute-start.6 = (bf16[4096,128]{1,0:T(8,128)(2,1)S(1)}, bf16[4096,128]{1,0:T(8,128)(2,1)S(1)}, u32[]{:S(2)}, u32[]{:S(2)}) collective-permute-start(bf16[4096,128]{1,0:T(8,128)(2,1)S(1)} %collective-permute-done.refs_2_), channel_id=1, source_target_pairs={{0,1},{1,0},{2,3},{3,2},{4,5},{5,4},{6,7},{7,6},{8,9},{9,8},{10,11... | collective-permute-start | bytes 3145736 | tf_op jit(solution)/shard_map/ppermute | solution.py:345
  46.4 47.2 %collective-permute-start.5 = (bf16[4096,128]{1,0:T(8,128)(2,1)S(1)}, bf16[4096,128]{1,0:T(8,128)(2,1)}, u32[]{:S(2)}, u32[]{:S(2)}) collective-permute-start(bf16[4096,128]{1,0:T(8,128)(2,1)S(1)} %collective-permute-done.refs_2_), channel_id=1, source_target_pairs={{0,2},{1,3},{2,4},{3,5},{4,6},{5,7},{6,0},{7,1},{8,10},{9,11},{10,... | collective-permute-start | bytes 3145736 | tf_op jit(solution)/shard_map/ppermute | solution.py:348
  48.0 43.7 %collective-permute-start.7 = (bf16[4,64,1024]{2,1,0:T(8,128)(2,1)S(1)}, bf16[4,64,1024]{2,1,0:T(8,128)(2,1)S(1)}, u32[]{:S(2)}, u32[]{:S(2)}) collective-permute-start(bf16[4,64,1024]{2,1,0:T(8,128)(2,1)S(1)} %pad_maximum_fusion.1), channel_id=1, source_target_pairs={{0,1},{1,0},{2,3},{3,2},{4,5},{5,4},{6,7},{7,6},{8,9},{9,8},{10,11... | collective-permute-start | bytes 1572872 | tf_op jit(solution)/shard_map/ppermute | solution.py:345
  94.2 16.6 %collective-permute-start.11 = (bf16[8,64,1024]{2,1,0:T(8,128)(2,1)}, bf16[8,64,1024]{2,1,0:T(8,128)(2,1)S(1)}, u32[]{:S(2)}, u32[]{:S(2)}) collective-permute-start(bf16[8,64,1024]{2,1,0:T(8,128)(2,1)} %copy-done.21), channel_id=1, source_target_pairs={{0,8},{8,0},{1,9},{9,1},{2,10},{10,2},{3,11},{11,3},{4,12},{12,4},... | collective-permute-start | bytes 3145736 | tf_op jit(solution)/shard_map/ppermute | solution.py:386
  97.1 38.9 %collective-permute-start.9 = (bf16[4096,128]{1,0:T(8,128)(2,1)}, bf16[4096,128]{1,0:T(8,128)(2,1)}, u32[]{:S(2)}, u32[]{:S(2)}) collective-permute-start(bf16[4096,128]{1,0:T(8,128)(2,1)} %collective-permute-done.5.refs_4_), channel_id=1, source_target_pairs={{0,1},{1,0},{2,3},{3,2},{4,5},{5,4},{6,7},{7,6},{8,9},{9,8},{10,11... | collective-permute-start | bytes 3145736 | tf_op jit(solution)/shard_map/ppermute | solution.py:345
  97.4 38.6 %collective-permute-start.8 = (bf16[4096,128]{1,0:T(8,128)(2,1)}, bf16[4096,128]{1,0:T(8,128)(2,1)}, u32[]{:S(2)}, u32[]{:S(2)}) collective-permute-start(bf16[4096,128]{1,0:T(8,128)(2,1)} %collective-permute-done.5.refs_4_), channel_id=1, source_target_pairs={{0,2},{1,3},{2,4},{3,5},{4,6},{5,7},{6,0},{7,1},{8,10},{9,11},{10,... | collective-permute-start | bytes 3145736 | tf_op jit(solution)/shard_map/ppermute | solution.py:348
  109.3 26.7 %collective-permute-start.12 = (f32[32,4096]{1,0:T(8,128)S(1)}, f32[32,4096]{1,0:T(8,128)S(1)}, u32[]{:S(2)}, u32[]{:S(2)}) collective-permute-start(f32[32,4096]{1,0:T(8,128)S(1)} %constant_dynamic-slice_fusion.4), channel_id=1, source_target_pairs={{0,1},{1,0},{2,3},{3,2},{4,5},{5,4},{6,7},{7,6},{8,9},{9,8},{10,11... | collective-permute-start | bytes 1572872 | tf_op jit(solution)/shard_map/ppermute | solution.py:345
  136.0 44.9 %collective-permute-start.13 = (bf16[4096,128]{1,0:T(8,128)(2,1)}, bf16[4096,128]{1,0:T(8,128)(2,1)}, u32[]{:S(2)}, u32[]{:S(2)}) collective-permute-start(bf16[4096,128]{1,0:T(8,128)(2,1)} %collective-permute-done.8.refs_6_), channel_id=1, source_target_pairs={{0,1},{1,0},{2,3},{3,2},{4,5},{5,4},{6,7},{7,6},{8,9},{9,8},{10,11... | collective-permute-start | bytes 3145736 | tf_op jit(solution)/shard_map/ppermute | solution.py:345
  142.9 37.9 %collective-permute-start.14 = (s16[2,4,528,128]{3,2,1,0:T(8,128)(2,1)}, s16[2,4,528,128]{3,2,1,0:T(8,128)(2,1)S(1)}, u32[]{:S(2)}, u32[]{:S(2)}) collective-permute-start(s16[2,4,528,128]{3,2,1,0:T(8,128)(2,1)} %add_parts.13), channel_id=1, source_target_pairs={{0,2},{1,3},{2,4},{3,5},{4,6},{5,7},{6,0},{7,1},{8,10},{9,11},{10,... | collective-permute-start | bytes 3244040 | tf_op jit(solution)/shard_map/ppermute | solution.py:348
  144.5 27.3 %collective-permute-start.17 = (f32[8,4096]{1,0:T(8,128)S(1)}, f32[8,4096]{1,0:T(8,128)S(1)}, u32[]{:S(2)}, u32[]{:S(2)}) collective-permute-start(f32[8,4096]{1,0:T(8,128)S(1)} %get-tuple-element.98), channel_id=1, source_target_pairs={{0,6},{1,7},{2,0},{3,1},{4,2},{5,3},{6,4},{7,5},{8,14},{9,15},{10,... | collective-permute-start | bytes 393224 | tf_op jit(solution)/shard_map/ppermute | solution.py:439
  146.9 33.9 %collective-permute-start.16 = (f32[8,4096]{1,0:T(8,128)S(1)}, f32[8,4096]{1,0:T(8,128)S(1)}, u32[]{:S(2)}, u32[]{:S(2)}) collective-permute-start(f32[8,4096]{1,0:T(8,128)S(1)} %get-tuple-element.99), channel_id=1, source_target_pairs={{0,4},{1,5},{2,6},{3,7},{4,0},{5,1},{6,2},{7,3},{8,12},{9,13},{10,... | collective-permute-start | bytes 393224 | tf_op jit(solution)/shard_map/ppermute | solution.py:439
  147.2 33.6 %collective-permute-start.15 = (f32[8,4096]{1,0:T(8,128)S(1)}, f32[8,4096]{1,0:T(8,128)S(1)}, u32[]{:S(2)}, u32[]{:S(2)}) collective-permute-start(f32[8,4096]{1,0:T(8,128)S(1)} %get-tuple-element.100), channel_id=1, source_target_pairs={{0,2},{1,3},{2,4},{3,5},{4,6},{5,7},{6,0},{7,1},{8,10},{9,11},{10,... | collective-permute-start | bytes 393224 | tf_op jit(solution)/shard_map/ppermute | solution.py:439
  189.1 30.5 %collective-permute-start.19 = (s16[2,4,528,128]{3,2,1,0:T(8,128)(2,1)}, s16[2,4,528,128]{3,2,1,0:T(8,128)(2,1)S(1)}, u32[]{:S(2)}, u32[]{:S(2)}) collective-permute-start(s16[2,4,528,128]{3,2,1,0:T(8,128)(2,1)} %add_parts.14), channel_id=1, source_target_pairs={{0,2},{1,3},{2,4},{3,5},{4,6},{5,7},{6,0},{7,1},{8,10},{9,11},{10,... | collective-permute-start | bytes 3244040 | tf_op jit(solution)/shard_map/ppermute | solution.py:348
  189.1 30.5 %collective-permute-start.18 = (s16[4,2,528,128]{3,2,1,0:T(8,128)(2,1)}, s16[4,2,528,128]{3,2,1,0:T(8,128)(2,1)S(1)}, u32[]{:S(2)}, u32[]{:S(2)}) collective-permute-start(s16[4,2,528,128]{3,2,1,0:T(8,128)(2,1)} %get-tuple-element.67), channel_id=1, source_target_pairs={{0,1},{1,0},{2,3},{3,2},{4,5},{5,4},{6,7},{7,6},{8,9},{9,8},{10,11... | collective-permute-start | bytes 3244040 | tf_op jit(solution)/shard_map/ppermute | solution.py:345
  219.6 8.1 %collective-permute-start.21 = (f32[8,64,1024]{2,1,0:T(8,128)}, f32[8,64,1024]{2,1,0:T(8,128)}, u32[]{:S(2)}, u32[]{:S(2)}) collective-permute-start(f32[8,64,1024]{2,1,0:T(8,128)} %get-tuple-element.86), channel_id=1, source_target_pairs={{0,8},{8,0},{1,9},{9,1},{2,10},{10,2},{3,11},{11,3},{4,12},{12,4},... | collective-permute-start | bytes 6291464 | tf_op jit(solution)/shard_map/ppermute | solution.py:489
  219.7 8.0 %collective-permute-start.22 = (f32[8,8,1024]{2,1,0:T(8,128)}, f32[8,8,1024]{2,1,0:T(8,128)}, u32[]{:S(2)}, u32[]{:S(2)}) collective-permute-start(f32[8,8,1024]{2,1,0:T(8,128)} %get-tuple-element.88), channel_id=1, source_target_pairs={{0,8},{8,0},{1,9},{9,1},{2,10},{10,2},{3,11},{11,3},{4,12},{12,4},... | collective-permute-start | bytes 786440 | tf_op jit(solution)/shard_map/ppermute | solution.py:490
  220.2 37.0 %collective-permute-start.20 = (s16[4,2,528,128]{3,2,1,0:T(8,128)(2,1)}, s16[4,2,528,128]{3,2,1,0:T(8,128)(2,1)S(1)}, u32[]{:S(2)}, u32[]{:S(2)}) collective-permute-start(s16[4,2,528,128]{3,2,1,0:T(8,128)(2,1)} %get-tuple-element.82), channel_id=1, source_target_pairs={{0,1},{1,0},{2,3},{3,2},{4,5},{5,4},{6,7},{7,6},{8,9},{9,8},{10,11... | collective-permute-start | bytes 3244040 | tf_op jit(solution)/shard_map/ppermute | solution.py:345
  227.3 39.6 %collective-permute-start.29 = (s16[2,4,528,128]{3,2,1,0:T(8,128)(2,1)}, s16[2,4,528,128]{3,2,1,0:T(8,128)(2,1)S(1)}, u32[]{:S(2)}, u32[]{:S(2)}) collective-permute-start(s16[2,4,528,128]{3,2,1,0:T(8,128)(2,1)} %add_parts.23), channel_id=1, source_target_pairs={{0,2},{1,3},{2,4},{3,5},{4,6},{5,7},{6,0},{7,1},{8,10},{9,11},{10,... | collective-permute-start | bytes 3244040 | tf_op jit(solution)/shard_map/ppermute | solution.py:348
  233.8 88.5 %all-to-all-start.1 = ((s16[8,80,1024]{2,1,0:T(8,128)(2,1)}), s16[8,80,1024]{2,1,0:T(8,128)(2,1)S(1)}, u32[]{:S(2)}, u32[]{:S(2)}) async-start(s16[8,80,1024]{2,1,0:T(8,128)(2,1)} %pack_gradients.1.after_ref), calls=%async_computation.1 | async-start | bytes 2621440 | tf_op jit(solution)/shard_map/all_to_all | solution.py:505
  260.8 22.4 %collective-permute-start.26 = (s16[1,2,528,128]{3,2,1,0:T(8,128)(2,1)}, s16[1,2,528,128]{3,2,1,0:T(8,128)(2,1)S(1)}, u32[]{:S(2)}, u32[]{:S(2)}) collective-permute-start(s16[1,2,528,128]{3,2,1,0:T(8,128)(2,1)} %add_parts.19), channel_id=1, source_target_pairs={{0,2},{1,3},{2,4},{3,5},{4,6},{5,7},{6,0},{7,1},{8,10},{9,11},{10,... | collective-permute-start | bytes 811016 | tf_op jit(solution)/shard_map/ppermute | solution.py:348
  265.4 24.9 %collective-permute-start.23 = (s16[1,2,528,128]{3,2,1,0:T(8,128)(2,1)}, s16[1,2,528,128]{3,2,1,0:T(8,128)(2,1)S(1)}, u32[]{:S(2)}, u32[]{:S(2)}) collective-permute-start(s16[1,2,528,128]{3,2,1,0:T(8,128)(2,1)} %add_parts.15), channel_id=1, source_target_pairs={{0,2},{1,3},{2,4},{3,5},{4,6},{5,7},{6,0},{7,1},{8,10},{9,11},{10,... | collective-permute-start | bytes 811016 | tf_op jit(solution)/shard_map/ppermute | solution.py:348
  272.1 36.5 %collective-permute-start.30 = (s16[1,4,528,128]{3,2,1,0:T(8,128)(2,1)}, s16[1,4,528,128]{3,2,1,0:T(8,128)(2,1)S(1)}, u32[]{:S(2)}, u32[]{:S(2)}) collective-permute-start(s16[1,4,528,128]{3,2,1,0:T(8,128)(2,1)} %add_parts.24), channel_id=1, source_target_pairs={{0,1},{1,0},{2,3},{3,2},{4,5},{5,4},{6,7},{7,6},{8,9},{9,8},{10,11... | collective-permute-start | bytes 1622024 | tf_op jit(solution)/shard_map/ppermute | solution.py:345
  286.6 9.5 %collective-permute-start.27 = (s16[1,2,528,128]{3,2,1,0:T(8,128)(2,1)}, s16[1,2,528,128]{3,2,1,0:T(8,128)(2,1)S(1)}, u32[]{:S(2)}, u32[]{:S(2)}) collective-permute-start(s16[1,2,528,128]{3,2,1,0:T(8,128)(2,1)} %add_parts.20), channel_id=1, source_target_pairs={{0,2},{1,3},{2,4},{3,5},{4,6},{5,7},{6,0},{7,1},{8,10},{9,11},{10,... | collective-permute-start | bytes 811016 | tf_op jit(solution)/shard_map/ppermute | solution.py:348
  293.7 9.2 %collective-permute-start.24 = (s16[1,2,528,128]{3,2,1,0:T(8,128)(2,1)}, s16[1,2,528,128]{3,2,1,0:T(8,128)(2,1)S(1)}, u32[]{:S(2)}, u32[]{:S(2)}) collective-permute-start(s16[1,2,528,128]{3,2,1,0:T(8,128)(2,1)} %add_parts.16), channel_id=1, source_target_pairs={{0,2},{1,3},{2,4},{3,5},{4,6},{5,7},{6,0},{7,1},{8,10},{9,11},{10,... | collective-permute-start | bytes 811016 | tf_op jit(solution)/shard_map/ppermute | solution.py:348
  299.5 14.1 %collective-permute-start.28 = (s16[1,2,528,128]{3,2,1,0:T(8,128)(2,1)}, s16[1,2,528,128]{3,2,1,0:T(8,128)(2,1)S(1)}, u32[]{:S(2)}, u32[]{:S(2)}) collective-permute-start(s16[1,2,528,128]{3,2,1,0:T(8,128)(2,1)} %add_parts.21), channel_id=1, source_target_pairs={{0,2},{1,3},{2,4},{3,5},{4,6},{5,7},{6,0},{7,1},{8,10},{9,11},{10,... | collective-permute-start | bytes 811016 | tf_op jit(solution)/shard_map/ppermute | solution.py:348
  306.3 10.7 %collective-permute-start.25 = (s16[1,2,528,128]{3,2,1,0:T(8,128)(2,1)}, s16[1,2,528,128]{3,2,1,0:T(8,128)(2,1)S(1)}, u32[]{:S(2)}, u32[]{:S(2)}) collective-permute-start(s16[1,2,528,128]{3,2,1,0:T(8,128)(2,1)} %add_parts.17), channel_id=1, source_target_pairs={{0,2},{1,3},{2,4},{3,5},{4,6},{5,7},{6,0},{7,1},{8,10},{9,11},{10,... | collective-permute-start | bytes 811016 | tf_op jit(solution)/shard_map/ppermute | solution.py:348
  (30 other events, 248.6 us)

commit v4 on v3

--- a/solution.py
+++ b/solution.py
@@ -57,25 +57,9 @@
         pair_ref[k * n : (k + 1) * n, rank:, :] = ref[...]
 
 
-def shrink_kernel(slot_ref, x_ref, near_ref, far_ref, out_ref, down_ref):
-    step = pl.program_id(0)
-    n = near_ref.shape[0]
-
-    @pl.when(step == 0)
-    def _():
-        down_ref[:n] = near_ref[...]
-        down_ref[n:] = far_ref[...]
-
-    tiles = x_ref.shape[0] // TILE
-    for t in range(tiles):
-        at = slice(t * TILE, (t + 1) * TILE)
-        out_ref[:, at] = dot(down_ref[slot_ref[step * tiles + t]], x_ref[at, :], NT)
-
-
 def forward_kernel(first, slot_ref, upslot_ref, place_ref, *refs):
-    x_ref, w_ref, ndown_ref, fdown_ref, nup_ref, fup_ref, kept_ref = refs[:7]
-    *sent_ref, down_ref, up_ref = refs[7:10] if len(refs) == 11 else refs[7:]
-    sum_ref = refs[-1] if sent_ref else kept_ref
+    x_ref, w_ref, ndown_ref, fdown_ref, nup_ref, fup_ref, shrink_ref, kept_ref = refs[:8]
+    *sent_refs, down_ref, up_ref, sum_ref = refs[8:] if len(refs) > 10 else (*refs[8:], kept_ref)
     step = pl.program_id(0)
     n, rows, cols = sum_ref.shape
     outer = kept_ref.shape[0]
@@ -92,22 +76,29 @@
     for t in range(tiles):
         at = slice(t * TILE, (t + 1) * TILE)
         tile = first + step * tiles + t
-        pieces = split_halves(dot(x_ref[at, :], down_ref[slot_ref[tile]], NT), rank)
+        shrink = dot(x_ref[at, :], down_ref[slot_ref[tile]], NT)
+        shrink_ref[:, at] = shrink.T[:rank]
+        pieces = split_halves(shrink, rank)
         total = base[at] + ADAPTER_SCALE * dot(pieces, up_ref[upslot_ref[tile]])
         for j in range(n):
             sum_ref[j, at, :] = total[:, j * cols : (j + 1) * cols]
-    if not sent_ref:
+    if not sent_refs:
         return
     mine = place_ref[1]
     for z in range(outer):
         kept_ref[z] = sum_ref[z * inner + mine]
-        put(sent_ref[0].at[z, 0], *encode(sum_ref[z * inner + 1 - mine]))
+    each = pl.num_programs(0) // len(sent_refs)
+    for c, sent_ref in enumerate(sent_refs):
+
+        @pl.when(step // each == c)
+        def _(sent_ref=sent_ref):
+            for z in range(outer):
+                put(sent_ref.at[z, 0], *encode(sum_ref[z * inner + 1 - mine]))
 
 
 def gradient_kernel(blocks, slot_ref, upslot_ref, order_ref, *refs):
     cots = refs[:blocks]
-    x_ref, nup_ref, fup_ref, shrink_ref = refs[blocks : blocks + 4]
-    all_ref, back_ref, ndown_ref, fdown_ref, nsum_ref, fsum_ref, up_ref, cot_ref, gdown_ref, gup_ref = refs[blocks + 4 :]
+    x_ref, nup_ref, fup_ref, all_ref, back_ref, near_ref, far_ref, up_ref, cot_ref, sum_ref = refs[blocks:]
     step = pl.program_id(0)
     rows = x_ref.shape[0]
     tiles = rows // TILE
@@ -116,8 +107,7 @@
     @pl.when(step == 0)
     def _():
         fill_twice(up_ref, nup_ref, fup_ref)
-        gdown_ref[...] = jnp.zeros_like(gdown_ref)
-        gup_ref[...] = jnp.zeros_like(gup_ref)
+        sum_ref[...] = jnp.zeros_like(sum_ref)
 
     for j, block in enumerate(cots):
         wide = block.shape[1]
@@ -133,22 +123,44 @@
         pieces = split_halves(dot(cot, up_ref[upslot_ref[tile]], NT), rank)
         back_ref[at, :] = pieces
         grad = dot(pieces, x_ref[at, :], TN)
-        gdown_ref[slot] += grad[:rank] + grad[rank:]
-        shrink = shrink_ref[:, at]
-        high = shrink.astype(BF16)
-        low = (shrink - high.astype(F32)).astype(BF16)
-        gup_ref[slot] += dot(high, cot) + dot(low, cot)
+        sum_ref[slot] += grad[:rank] + grad[rank:]
 
     @pl.when(step == pl.num_programs(0) - 1)
     def _():
-        n = ndown_ref.shape[0]
-        ndown_ref[...] = gdown_ref[:n]
-        fdown_ref[...] = gdown_ref[n:]
-        nsum_ref[...] = gup_ref[:n]
-        fsum_ref[...] = gup_ref[n:]
-
-
-def token_kernel(slot_ref, cot_ref, w_ref, near_ref, far_ref, back_ref, after_ref, out_ref, down_ref):
+        n = near_ref.shape[0]
+        near_ref[...] = sum_ref[:n]
+        far_ref[...] = sum_ref[n:]
+
+
+def up_kernel(slot_ref, shrink_ref, cot_ref, near_ref, far_ref, sum_ref):
+    step = pl.program_id(0)
+    own, rows = shrink_ref.shape
+    tiles = rows // TILE
+
+    @pl.when(step == 0)
+    def _():
+        sum_ref[...] = jnp.zeros_like(sum_ref)
+
+    for t in range(tiles):
+        at = slice(t * TILE, (t + 1) * TILE)
+        slot, cot = slot_ref[step * tiles + t], cot_ref[at, :]
+        shrink = shrink_ref[:, at]
+        high = shrink.astype(BF16).astype(F32)
+        low = shrink - high
+        if own % 8:
+            sum_ref[slot] += dot(high.astype(BF16), cot) + dot(low.astype(BF16), cot)
+        else:
+            grad = dot(jnp.concatenate([high, low], axis=0).astype(BF16), cot)
+            sum_ref[slot] += grad[:own] + grad[own:]
+
+    @pl.when(step == pl.num_programs(0) - 1)
+    def _():
+        n = near_ref.shape[0]
+        near_ref[...] = sum_ref[:n]
+        far_ref[...] = sum_ref[n:]
+
+
+def token_kernel(slot_ref, cot_ref, w_ref, near_ref, far_ref, back_ref, out_ref, down_ref):
     step = pl.program_id(0)
     tiles = cot_ref.shape[0] // TILE
 
@@ -181,15 +193,16 @@
         put(out_ref.at[0, 0], *encode(total))
 
 
-def add_parts(place, block_rows, count, kept, coded, last=False):
+def add_parts(place, block_rows, count, kept, coded, first=0, blocks=None, last=False):
     part, pick = kept
     rows, cols = part.shape[1:]
-    blocks, held = rows // block_rows, block_rows + PAD
+    blocks, held = blocks or rows // block_rows, block_rows + PAD
+    rows = blocks * block_rows
 
     def coded_spec(pick):
         return pl.BlockSpec((1, 1, held, cols), lambda i, b, p: (pick(i, p), b, 0, 0))
 
-    in_specs = [pl.BlockSpec((1, block_rows, cols), lambda i, b, p: (pick(i, p), b, 0))]
+    in_specs = [pl.BlockSpec((1, block_rows, cols), lambda i, b, p: (pick(i, p), first + b, 0))]
     in_specs += [coded_spec(q) for _, q in coded]
     if last:
         out_shape = jax.ShapeDtypeStruct((rows, cols), BF16)
@@ -262,11 +275,10 @@
 
     place = jnp.stack([my_outer, my_inner]).astype(jnp.int32)
 
-    block_rows = 4 * TILE
+    block_rows = 8 * TILE
     steps = rows // block_rows
-    sizes = [steps // 4, steps // 4, steps - 2 * (steps // 4)]
-    starts = [sum(sizes[:c]) for c in range(len(sizes))]
-    chunks = len(sizes)
+    each = steps // 4
+    last = 2
     once = pl.Buffered(1)
     params = pltpu.CompilerParams(vmem_limit_bytes=VMEM)
     held = block_rows + PAD
@@ -301,17 +313,18 @@
     def strip(wide, first=0):
         return pl.BlockSpec((block_rows, wide), lambda i, *_: (first + i, 0))
 
-    def forward(c, sends):
-        kept = outer if sends else n
-        blocks, start = sizes[c], starts[c]
-        chunk_rows = blocks * block_rows
-        coded_spec = [pl.BlockSpec((outer, 1, held, cols), lambda i, *_: (0, i, 0, 0))]
-        coded_shape = [jax.ShapeDtypeStruct((outer, blocks, held, cols), jnp.int16)]
+    def forward(start, count, chunks):
+        kept = outer if chunks else n
+        each = count // max(chunks, 1)
+        coded_specs = [
+            pl.BlockSpec((outer, 1, held, cols), lambda i, *_, c=c: (0, jnp.clip(i - c * each, 0, each - 1), 0, 0))
+            for c in range(chunks)
+        ]
         return pl.pallas_call(
             functools.partial(forward_kernel, start * (block_rows // TILE)),
             grid_spec=pltpu.PrefetchScalarGridSpec(
                 num_scalar_prefetch=3,
-                grid=(blocks,),
+                grid=(count,),
                 in_specs=[
                     strip(width, start),
                     whole(width, out_width),
@@ -321,22 +334,26 @@
                     whole(n, rank, out_width),
                 ],
                 out_specs=[
+                    pl.BlockSpec((rank, block_rows), lambda i, *_: (0, i)),
                     pl.BlockSpec((kept, block_rows, cols), lambda i, *_: (0, i, 0)),
-                ]
-                + coded_spec * sends,
+                    *coded_specs,
+                ],
                 scratch_shapes=[
                     pltpu.VMEM((slots, 2 * rank, width), BF16),
                     pltpu.VMEM((slots, 2 * rank, out_width), BF16),
                 ]
-                + [pltpu.VMEM((n, block_rows, cols), F32)] * sends,
+                + [pltpu.VMEM((n, block_rows, cols), F32)] * (chunks > 0),
             ),
             out_shape=[
-                jax.ShapeDtypeStruct((kept, chunk_rows, cols), F32),
-            ]
-            + coded_shape * sends,
+                jax.ShapeDtypeStruct((rank, count * block_rows), F32),
+                jax.ShapeDtypeStruct((kept, count * block_rows, cols), F32),
+                *[jax.ShapeDtypeStruct((outer, each, held, cols), jnp.int16)] * chunks,
+            ],
             compiler_params=params,
             cost_estimate=pl.CostEstimate(
-                flops=4 * chunk_rows * width * out_width, bytes_accessed=chunk_rows * width * 6, transcendentals=0
+                flops=4 * count * block_rows * width * out_width,
+                bytes_accessed=count * block_rows * width * 6,
+                transcendentals=0,
             ),
             name="forward",
         )(tile_slot, tile_up, place, tokens, frozen_weight, near_down, far_down, near_up, far_up)
@@ -353,10 +370,10 @@
     def first(i, p):
         return 0
 
-    def ring_step(s, kept, near, run):
+    def ring_step(s, kept, near, run, c):
         at = behind(s % outer)
         coded = [(near, at)] + [(r, first) for r in run]
-        return add_parts(place, block_rows, 1, (kept, at), coded, last=s == outer)
+        return add_parts(place, block_rows, 1, (kept, at), coded, c * each, each, last=s == outer)
 
     def pair_step(s, kept, run):
         at = behind(s)
@@ -386,85 +403,64 @@
     far_up, far_down = (lax.ppermute(a, "dp", cores) for a in (near_up, near_down))
     own = rank // n
     half = rank // inner
-    shrink = pl.pallas_call(
-        shrink_kernel,
-        grid_spec=pltpu.PrefetchScalarGridSpec(
-            num_scalar_prefetch=1,
-            grid=(steps // 2,),
-            in_specs=[
-                pl.BlockSpec((2 * block_rows, width), lambda i, s: (i, 0)),
-                whole(n, rank, width),
-                whole(n, rank, width),
-            ],
-            out_specs=pl.BlockSpec((rank, 2 * block_rows), lambda i, s: (0, i)),
-            scratch_shapes=[pltpu.VMEM((slots, rank, width), BF16)],
-        ),
-        out_shape=jax.ShapeDtypeStruct((rank, rows), F32),
-        compiler_params=params,
-        cost_estimate=pl.CostEstimate(flops=0, bytes_accessed=rows * width * 2, transcendentals=0),
-        name="shrink",
-    )(tile_slot, tokens, near_down, far_down)
-    mine = lax.dynamic_slice_in_dim(shrink, my_inner * half, half, 0)
-    theirs = swapped(lax.dynamic_slice_in_dim(shrink, other * half, half, 0))
-    parts = [forward(c, c < chunks - 1) for c in range(chunks)]
-    near, outs = {}, {}
-    runs = {c: [] for c in range(chunks)}
-
-    done = {c: 0 for c in range(chunks)}
-
-    def advance(c, through=outer):
-        pair = c == chunks - 1
-        while done[c] < min(through, outer - pair):
+    late_shrink, pair = forward(2 * each, steps - 2 * each, 0)
+    shrink, kept, *sents = forward(0, 2 * each, 2)
+    near, outs, runs, sums, done = {}, {}, [()] * 3, [()] * 3, [0] * 3
+
+    def add(*chunks):
+        for c in chunks:
             done[c] += 1
-            if pair:
-                runs[c] = [shifted(pair_step(done[c], parts[c][0], runs[c]))]
-                continue
-            total = ring_step(done[c], parts[c][0], near[c], runs[c])
-            if done[c] == outer:
-                outs[c] = total
+            if c == last:
+                sums[c] = pair_step(done[c], pair, runs[c])
             else:
-                runs[c] = [shifted(total)]
-
-    last = chunks - 1
+                sums[c] = ring_step(done[c], kept, near[c], runs[c], c)
+
+    def send(*chunks):
+        for c in chunks:
+            runs[c] = (shifted(sums[c]),)
+
     for s in range(2, outer):
         cots += [block, swapped(block)]
         if s < outer - 1:
             block = shifted(block)
         if s == 2:
-            block, cots[-1], parts[last], theirs = tie((block, cots[-1], parts[last], theirs))
-    mine += theirs
+            add(last)
+            block, cots[-1], sums[last] = tie((block, cots[-1], sums[last]))
+    send(last)
+    cots[-1], kept, sents, runs, shrink = tie((cots[-1], kept, sents, runs, shrink))
+
+    shrink = jnp.concatenate([shrink, late_shrink], axis=1)
+    theirs = swapped(lax.dynamic_slice_in_dim(shrink, other * half, half, 0))
+    add(last)
+    mine = lax.dynamic_slice_in_dim(shrink, my_inner * half, half, 0) + theirs
+    send(last)
+    cots[-1], mine = tie((cots[-1], mine))
     shrink = [lax.dynamic_slice_in_dim(mine, my_outer * own, own, 0)]
     for s in range(1, outer):
         theirs = lax.dynamic_slice_in_dim(mine, ((my_outer + s) % outer) * own, own, 0)
         shrink.append(lax.ppermute(theirs, "mp", [(i, (i + s * inner) % n) for i in range(n)]))
-    advance(last, 1)
-    cots[-1], parts[0], parts[1], runs, shrink = tie((cots[-1], parts[0], parts[1], runs, shrink))
-    shrink = sum(shrink[1:], shrink[0])
-    near[0] = swapped(parts[0][1])
+    near[0] = swapped(sents[0])
+
     if cols % 128:
         natural = jnp.stack(cots)[jnp.argsort(jnp.stack(order))]
         cots = [jnp.transpose(natural, (1, 0, 2)).reshape(rows, out_width)]
-    cot_all, back, gdown, rdown, gup, rup = pl.pallas_call(
+    cot_all, back, gdown, rdown = pl.pallas_call(
         functools.partial(gradient_kernel, len(cots)),
         grid_spec=pltpu.PrefetchScalarGridSpec(
             num_scalar_prefetch=3,
             grid=(steps,),
             in_specs=[strip(a.shape[1]) for a in cots]
-            + [strip(width), whole(n, rank, out_width), whole(n, rank, out_width)]
-            + [pl.BlockSpec((own, block_rows), lambda i, *_: (0, i))],
+            + [strip(width), whole(n, rank, out_width), whole(n, rank, out_width)],
             out_specs=[
                 strip(out_width),
                 strip(2 * rank),
                 whole(n, rank, width),
                 whole(n, rank, width),
-                whole(n, own, out_width),
-                whole(n, own, out_width),
             ],
             scratch_shapes=[
                 pltpu.VMEM((slots, 2 * rank, out_width), BF16),
                 pltpu.VMEM((block_rows, out_width), BF16),
                 pltpu.VMEM((slots, rank, width), F32),
-                pltpu.VMEM((slots, own, out_width), F32),
             ],
         ),
         out_shape=[
@@ -472,20 +468,40 @@
             jax.ShapeDtypeStruct((rows, 2 * rank), BF16),
             jax.ShapeDtypeStruct((n, rank, width), F32),
             jax.ShapeDtypeStruct((n, rank, width), F32),
-            jax.ShapeDtypeStruct((n, own, out_width), F32),
-            jax.ShapeDtypeStruct((n, own, out_width), F32),
         ],
         compiler_params=params,
         cost_estimate=pl.CostEstimate(
             flops=2 * rows * width * out_width, bytes_accessed=rows * (width * 2 + out_width * 4), transcendentals=0
         ),
         name="gradients",
-    )(tile_slot, tile_up, jnp.stack(order).astype(jnp.int32), *cots, tokens, near_up, far_up, shrink)
-    advance(last, 2)
-    near[0], gdown, rdown, gup, rup, runs = tie((near[0], gdown, rdown, gup, rup, runs))
-    near[1] = swapped(parts[1][1])
-    advance(last)
-
+    )(tile_slot, tile_up, jnp.stack(order).astype(jnp.int32), *cots, tokens, near_up, far_up)
+    near[0], gdown, rdown, runs, shrink = tie((near[0], gdown, rdown, runs, shrink))
+    shrink = sum(shrink[1:], shrink[0])
+    near[1] = swapped(sents[1])
+    add(0)
+    sums, near[0] = tie((sums, near[0]))
+    send(0)
+    while done[last] < outer - 1:
+        add(last)
+        send(last)
+
+    gup, rup = pl.pallas_call(
+        up_kernel,
+        grid_spec=pltpu.PrefetchScalarGridSpec(
+            num_scalar_prefetch=1,
+            grid=(steps,),
+            in_specs=[pl.BlockSpec((own, block_rows), lambda i, s: (0, i)), strip(out_width)],
+            out_specs=[whole(n, own, out_width), whole(n, own, out_width)],
+            scratch_shapes=[pltpu.VMEM((slots, own, out_width), F32)],
+        ),
+        out_shape=[
+            jax.ShapeDtypeStruct((n, own, out_width), F32),
+            jax.ShapeDtypeStruct((n, own, out_width), F32),
+        ],
+        compiler_params=params,
+        cost_estimate=pl.CostEstimate(flops=0, bytes_accessed=rows * out_width * 2, transcendentals=0),
+        name="up_gradient",
+    )(tile_slot, shrink, cot_all)
     rdown = lax.ppermute(rdown, "dp", cores)
     rup = lax.ppermute(rup, "dp", cores)
     packed_rows = rank + PAD
@@ -502,6 +518,10 @@
         out_shape=jax.ShapeDtypeStruct((n, packed_rows, width), jnp.int16),
         name="pack_gradients",
     )(gdown, rdown, gup, rup)
+    near, packed = tie((near, packed))
+    add(1)
+    send(1)
+    runs, packed = tie((runs, packed))
     landed = lax.all_to_all(packed, "mp", split_axis=0, concat_axis=0, tiled=True)
     down_gradient, up_gradient = pl.pallas_call(
         unpack_kernel,
@@ -529,7 +549,6 @@
                 whole(n, rank, width),
                 whole(n, rank, width),
                 strip(2 * rank),
-                pl.BlockSpec(memory_space=pl.ANY),
             ],
             out_specs=strip(width),
             scratch_shapes=[pltpu.VMEM((slots, 2 * rank, width), BF16)],
@@ -540,13 +559,23 @@
             flops=3 * rows * width * out_width, bytes_accessed=rows * (width * 2 + out_width * 2), transcendentals=0
         ),
         name="token_gradient",
-    )(tile_slot, cot_all, frozen_weight, near_down, far_down, back, packed)
-    kept, run = parts[last][0], runs[last][0]
-    outs[last] = pair_end(kept, run, [swapped(pair_end(kept, run, []))])
-    near, token_gradient = tie((near, token_gradient))
-    for c in range(last):
-        advance(c)
-    output = jnp.concatenate([outs[c] for c in range(chunks)], axis=0)
+    )(tile_slot, cot_all, frozen_weight, near_down, far_down, back)
+    run = runs[last][0]
+    outs[last] = pair_end(pair, run, [swapped(pair_end(pair, run, []))])
+    add(0)
+    send(0)
+    runs, outs, token_gradient = tie((runs, outs, token_gradient))
+    for c in (1, 0):
+        add(c)
+        send(c)
+    runs, down_gradient, up_gradient = tie((runs, down_gradient, up_gradient))
+    while done[1] < outer:
+        for c in (1, 0):
+            if done[c] < outer:
+                add(c)
+                if done[c] < outer:
+                    send(c)
+    output = jnp.concatenate([sums[0], sums[1], outs[last]], axis=0)
 
     up_gradient = up_gradient.reshape(1, rank, out_width)
     return output, token_gradient, jnp.swapaxes(down_gradient, 1, 2), up_gradient

time: 331 us -> 311 us (0.940)
  Pallas kernels: 153 us -> 130 us
  waiting for transfers between devices: 98.1 us -> 109 us
  local copies, waits for them, and re-layouts: 16.7 us -> 10.6 us
    ppermute x3, waiting for transfers between devices: 22.9 us -> 1.33 us  [body(): lax.ppermute(theirs, 'mp', [(i, (i + s * inner) % n) for i in range(n)])]
    ppermute x9, waiting for transfers between devices: 43 us -> 59.5 us  [swapped(): return lax.ppermute(x, 'mp', swap)]
    ppermute x12, waiting for transfers between devices: 11.3 us -> 26.1 us  [shifted(): return lax.ppermute(x, 'mp', ring)]
    pallas_call x1, Pallas kernels: 27.4 us -> 18.6 us  [body(): pl.pallas_call(functools.partial(gradient_kernel, len(cots)), grid_spec=p...]
    pallas_call x13, Pallas kernels: 49.2 us -> 41.8 us  [add_parts(): pl.pallas_call(functools.partial(sum_kernel, len(coded)), grid_spec=pltpu...]
    unnamed x62 -> x61, local copies, waits for them, and re-layouts: 14.8 us -> 8.85 us
    pallas_call x3 -> x2, Pallas kernels: 34.3 us -> 29.2 us  [forward(): pl.pallas_call(functools.partial(forward_kernel, start * (block_rows // T...]
  transfers between devices with their start and end apart: 33 -> 33, of which waited for: 6 -> 13; matrix products, arithmetic and copies ran while one was open for 2% -> 2% of each run, Pallas kernels for 43% -> 40%
where the time goes in v4:
time: 311 us; the launch traced here: 309 us
  Pallas kernels  130 us (42%)
  waiting for transfers between devices  109 us (35%)
  starting transfers between devices  52.5 us (17%)
  local copies, waits for them, and re-layouts  10.6 us (3%)
  other arithmetic  7.04 us (2%)
    ppermute x9, waiting for transfers between devices, swapped(): return lax.ppermute(x, 'mp', swap)  59.5 us
    pallas_call x13, Pallas kernels, add_parts(): pl.pallas_call(functools.partial(sum_kernel, len(coded)), grid_spec=pltpu...  41.8 us
    pallas_call x2, Pallas kernels, forward(): pl.pallas_call(functools.partial(forward_kernel, start * (block_rows // T...  29.2 us
    ppermute x12, waiting for transfers between devices, shifted(): return lax.ppermute(x, 'mp', ring)  26.1 us
    ppermute x12, starting transfers between devices, shifted(): return lax.ppermute(x, 'mp', ring)  22.4 us
    ppermute x3, waiting for transfers between devices, body(): lax.ppermute(adapter_up, 'mp', [(i, (i + s * inner) % n) for i in range(n)])  21.7 us
    pallas_call x1, Pallas kernels, body(): pl.pallas_call(functools.partial(gradient_kernel, len(cots)), grid_spec=p...  18.6 us
    pallas_call x1, Pallas kernels, body(): pl.pallas_call(token_kernel, grid_spec=pltpu.PrefetchScalarGridSpec(num_s...  16.9 us
  transfers between devices with their start and end apart: 33, of which 13 were waited for; matrix products, arithmetic and copies ran while one was open for 2% of the time, Pallas kernels for 40%

profile of v4, /device:TPU:0, one launch (start us, length us, event | category | flops | bytes accessed | tf_op | source)
XLA Modules:
  0.0 309.4 jit_solution(5451313197908994295)
XLA Ops:
  0.6 3.1 collective-permute-start
  10.7 5.2 %cut_down.1 = bf16[8,64,1024]{2,1,0:T(8,128)(2,1)} custom-call(bf16[1,64,8192]{2,1,0:T(8,128)(2,1)} %bitcast.15), custom_call_target="tpu_custom_call" | custom-call | tf_op jit(solution)/shard_map/cut_down/pallas_call | solution.py:290
  15.9 16.9 %collective-permute-done.2 = bf16[1,64,1024]{2,1,0:T(8,128)(2,1)S(1)} collective-permute-done((bf16[1,64,1024]{2,1,0:T(8,128)(2,1)}, bf16[1,64,1024]{2,1,0:T(8,128)(2,1)S(1)}, u32[]{:S(2)}, u32[]{:S(2)}) %collective-permute-start.2) | collective-permute-done | bytes 131104 | tf_op jit(solution)/shard_map/ppermute | solution.py:289
  32.9 4.8 %collective-permute-done.3 = bf16[1,64,1024]{2,1,0:T(8,128)(2,1)S(1)} collective-permute-done((bf16[1,64,1024]{2,1,0:T(8,128)(2,1)}, bf16[1,64,1024]{2,1,0:T(8,128)(2,1)S(1)}, u32[]{:S(2)}, u32[]{:S(2)}) %collective-permute-start.3) | collective-permute-done | bytes 131104 | tf_op jit(solution)/shard_map/ppermute | solution.py:289
  38.7 6.5 %all-to-all-start = ((bf16[8,64,1024]{2,1,0:T(8,128)(2,1)}), bf16[8,64,1024]{2,1,0:T(8,128)(2,1)S(1)}, u32[]{:S(2)}, u32[]{:S(2)}) async-start(bf16[8,64,1024]{2,1,0:T(8,128)(2,1)} %cut_down.1), calls=%async_computation | async-start | bytes 2097152 | tf_op jit(solution)/shard_map/all_to_all | solution.py:398
  49.5 42.3 %collective-permute-done.7 = bf16[4,64,1024]{2,1,0:T(8,128)(2,1)S(1)} collective-permute-done((bf16[4,64,1024]{2,1,0:T(8,128)(2,1)S(1)}, bf16[4,64,1024]{2,1,0:T(8,128)(2,1)S(1)}, u32[]{:S(2)}, u32[]{:S(2)}) %collective-permute-start.7) | collective-permute-done | bytes 524320 | tf_op jit(solution)/shard_map/ppermute | solution.py:362
  97.8 14.0 %forward.2 = (f32[64,2048]{1,0:T(8,128)}, f32[8,2048,128]{2,1,0:T(8,128)}) custom-call(s32[32]{0:T(128)} %fusion.7.slot_ref, s32[32]{0:T(128)} %get-tuple-element.126.upslot_ref, s32[2]{0:T(128)} %pad_add_fusion.place_ref, bf16[4096,1024]{1,0:T(8,128)(2,1)} %refs_8_.1, bf16[1024,1024]{1,0:T(8,128)(2,1)} %w_ref.1, bf16[8,64,1024]{2,1,0:T(8,128)(2,1)} %copy-done.7, ...), custom_call_target="tpu_custom_call" | custom-call | flops 8589934592 | bytes 12582912 | tf_op jit(solution)/shard_map/forward/pallas_call | solution.py:323
  111.7 4.5 %add_parts.13 = s16[2,2,1040,128]{3,2,1,0:T(8,128)(2,1)} custom-call(s32[2]{0:T(128)} %pad_add_fusion.place_ref, f32[8,2048,128]{2,1,0:T(8,128)} %get-tuple-element.74.refs_0_), custom_call_target="tpu_custom_call" | custom-call | bytes 4194304 | tf_op jit(solution)/shard_map/add_parts/pallas_call | solution.py:213
  116.2 5.7 %collective-permute-done.8.refs_6_ = bf16[4096,128]{1,0:T(8,128)(2,1)} collective-permute-done((bf16[4096,128]{1,0:T(8,128)(2,1)}, bf16[4096,128]{1,0:T(8,128)(2,1)}, u32[]{:S(2)}, u32[]{:S(2)}) %collective-permute-start.8) | collective-permute-done | bytes 1048608 | tf_op jit(solution)/shard_map/ppermute | solution.py:365
  123.2 15.2 %forward.3 = (f32[64,2048]{1,0:T(8,128)}, f32[4,2048,128]{2,1,0:T(8,128)}, s16[4,1,1040,128]{3,2,1,0:T(8,128)(2,1)}, s16[4,1,1040,128]{3,2,1,0:T(8,128)(2,1)}) custom-call(s32[32]{0:T(128)} %fusion.7.slot_ref, s32[32]{0:T(128)} %get-tuple-element.126.upslot_ref, s32[2]{0:T(128)} %pad_add_fusion.place_ref, bf16[4096,1024]{1,0:T(8,128)(2,1)} %refs_8_.1, ...), custom_call_target="tpu_custom_call" | custom-call | flops 8589934592 | bytes 12582912 | tf_op jit(solution)/shard_map/forward/pallas_call | solution.py:323
  138.4 8.1 %collective-permute-done.12.refs_7_ = bf16[4096,128]{1,0:T(8,128)(2,1)S(1)} collective-permute-done((bf16[4096,128]{1,0:T(8,128)(2,1)}, bf16[4096,128]{1,0:T(8,128)(2,1)S(1)}, u32[]{:S(2)}, u32[]{:S(2)}) %collective-permute-start.12) | collective-permute-done | bytes 1048608 | tf_op jit(solution)/shard_map/ppermute | solution.py:362
  152.4 4.7 %add_parts.14 = s16[2,2,1040,128]{3,2,1,0:T(8,128)(2,1)} custom-call(s32[2]{0:T(128)} %pad_add_fusion.place_ref, f32[8,2048,128]{2,1,0:T(8,128)} %get-tuple-element.74.refs_0_, s16[2,2,1040,128]{3,2,1,0:T(8,128)(2,1)} %copy-done.5), custom_call_target="tpu_custom_call" | custom-call | bytes 4194304 | tf_op jit(solution)/shard_map/add_parts/pallas_call | solution.py:213
  158.4 7.7 %collective-permute-done.15 = f32[32,4096]{1,0:T(8,128)} collective-permute-done((f32[32,4096]{1,0:T(8,128)}, f32[32,4096]{1,0:T(8,128)}, u32[]{:S(2)}, u32[]{:S(2)}) %collective-permute-start.15) | collective-permute-done | bytes 524320 | tf_op jit(solution)/shard_map/ppermute | solution.py:362
  171.1 18.6 %gradients.1 = (bf16[4096,1024]{1,0:T(8,128)(2,1)}, bf16[4096,128]{1,0:T(8,128)(2,1)}, f32[8,64,1024]{2,1,0:T(8,128)}, f32[8,64,1024]{2,1,0:T(8,128)}) custom-call(s32[32]{0:T(128)} %fusion.7.slot_ref, s32[32]{0:T(128)} %get-tuple-element.126.upslot_ref, s32[8]{0:T(128)} %stack.47.order_ref, bf16[4096,128]{1,0:T(8,128)(2,1)} %refs_0_.5, ...), custom_call_target="tpu_custom_call" | custom-call | flops 8589934592 | bytes 25165824 | tf_op jit(solution)/shard_map/gradients/pallas_call | solution.py:447
  193.4 4.7 %add_parts.17 = s16[2,2,1040,128]{3,2,1,0:T(8,128)(2,1)} custom-call(s32[2]{0:T(128)} %pad_add_fusion.place_ref, f32[8,2048,128]{2,1,0:T(8,128)} %get-tuple-element.74.refs_0_, s16[2,2,1040,128]{3,2,1,0:T(8,128)(2,1)} %copy-done.6), custom_call_target="tpu_custom_call" | custom-call | bytes 4194304 | tf_op jit(solution)/shard_map/add_parts/pallas_call | solution.py:213
  198.1 3.3 %collective-permute-start.25 = (s16[2,2,1040,128]{3,2,1,0:T(8,128)(2,1)}, s16[2,2,1040,128]{3,2,1,0:T(8,128)(2,1)S(1)}, u32[]{:S(2)}, u32[]{:S(2)}) collective-permute-start(s16[2,2,1040,128]{3,2,1,0:T(8,128)(2,1)} %add_parts.17), channel_id=1, source_target_pairs={{0,2},{1,3},{2,4},{3,5},{4,6},{5,7},{6,0},{7,1},{8,10},{9,11},{10,... | collective-permute-start | bytes 3194888 | tf_op jit(solution)/shard_map/ppermute | solution.py:365
  203.0 6.3 %up_gradient.1 = (f32[8,8,1024]{2,1,0:T(8,128)}, f32[8,8,1024]{2,1,0:T(8,128)}) custom-call(s32[32]{0:T(128)} %fusion.7.slot_ref, f32[8,4096]{1,0:T(8,128)} %add_add_fusion.shrink_ref, bf16[4096,1024]{1,0:T(8,128)(2,1)} %get-tuple-element.103.cot_ref), custom_call_target="tpu_custom_call" | custom-call | bytes 8388608 | tf_op jit(solution)/shard_map/up_gradient/pallas_call | solution.py:488
  212.9 6.1 %pack_gradients.1 = s16[8,80,1024]{2,1,0:T(8,128)(2,1)} custom-call(f32[8,64,1024]{2,1,0:T(8,128)} %get-tuple-element.97.gdown_ref, f32[8,64,1024]{2,1,0:T(8,128)} %collective-permute-done.21.rdown_ref, f32[8,8,1024]{2,1,0:T(8,128)} %get-tuple-element.104.gup_ref, f32[8,8,1024]{2,1,0:T(8,128)} %copy-done.18), custom_call_target="tpu_custom_call" | custom-call | tf_op jit(solution)/shard_map/pack_gradients/pallas_call | solution.py:508
  225.1 7.1 %collective-permute-done.23.refs_2_ = s16[1,1,1040,128]{3,2,1,0:T(8,128)(2,1)S(1)} collective-permute-done((s16[1,1,1040,128]{3,2,1,0:T(8,128)(2,1)}, s16[1,1,1040,128]{3,2,1,0:T(8,128)(2,1)S(1)}, u32[]{:S(2)}, u32[]{:S(2)}) %collective-permute-start.23) | collective-permute-done | bytes 266272 | tf_op jit(solution)/shard_map/ppermute | solution.py:365
  232.2 4.9 %collective-permute-done.24.refs_2_ = s16[1,1,1040,128]{3,2,1,0:T(8,128)(2,1)S(1)} collective-permute-done((s16[1,1,1040,128]{3,2,1,0:T(8,128)(2,1)}, s16[1,1,1040,128]{3,2,1,0:T(8,128)(2,1)S(1)}, u32[]{:S(2)}, u32[]{:S(2)}) %collective-permute-start.24) | collective-permute-done | bytes 266272 | tf_op jit(solution)/shard_map/ppermute | solution.py:365
  237.1 3.6 %all-to-all-start.1 = ((s16[8,80,1024]{2,1,0:T(8,128)(2,1)}), s16[8,80,1024]{2,1,0:T(8,128)(2,1)S(1)}, u32[]{:S(2)}, u32[]{:S(2)}) async-start(s16[8,80,1024]{2,1,0:T(8,128)(2,1)} %pack_gradients.1), calls=%async_computation.1 | async-start | bytes 2621440 | tf_op jit(solution)/shard_map/all_to_all | solution.py:525
  240.7 2.9 add_parts.19
  245.6 2.8 add_parts.18
  249.9 16.9 %token_gradient.1 = bf16[4096,1024]{1,0:T(8,128)(2,1)} custom-call(s32[32]{0:T(128)} %fusion.7.slot_ref, bf16[4096,1024]{1,0:T(8,128)(2,1)} %get-tuple-element.103.cot_ref, bf16[1024,1024]{1,0:T(8,128)(2,1)} %w_ref.1, bf16[8,64,1024]{2,1,0:T(8,128)(2,1)} %copy-done.7, bf16[8,64,1024]{2,1,0:T(8,128)(2,1)} %collective-permute-done.10.refs_3_.far_ref, ...), custom_call_target="tpu_custom_call" | custom-call | flops 12884901888 | bytes 16777216 | tf_op jit(solution)/shard_map/token_gradient/pallas_call | solution.py:541
  269.0 3.1 add_parts.20
  272.0 2.8 add_parts.22
  274.8 4.0 %collective-permute-start.29 = (s16[1,1,1040,128]{3,2,1,0:T(8,128)(2,1)}, s16[1,1,1040,128]{3,2,1,0:T(8,128)(2,1)S(1)}, u32[]{:S(2)}, u32[]{:S(2)}) collective-permute-start(s16[1,1,1040,128]{3,2,1,0:T(8,128)(2,1)} %add_parts.22), channel_id=1, source_target_pairs={{0,2},{1,3},{2,4},{3,5},{4,6},{5,7},{6,0},{7,1},{8,10},{9,11},{10,... | collective-permute-start | bytes 798728 | tf_op jit(solution)/shard_map/ppermute | solution.py:365
  278.9 2.8 add_parts.21
  285.1 5.6 %unpack_gradients.1 = (f32[1,64,8192]{2,1,0:T(8,128)}, f32[8,8,1024]{2,1,0:T(8,128)}) custom-call(s16[8,80,1024]{2,1,0:T(8,128)(2,1)} %copy-done.2), custom_call_target="tpu_custom_call" | custom-call | tf_op jit(solution)/shard_map/unpack_gradients/pallas_call | solution.py:526
  291.7 2.8 add_parts.24
  295.9 2.7 add_parts.23
  298.6 5.4 %collective-permute-done.30.refs_2_ = s16[1,1,1040,128]{3,2,1,0:T(8,128)(2,1)S(1)} collective-permute-done((s16[1,1,1040,128]{3,2,1,0:T(8,128)(2,1)}, s16[1,1,1040,128]{3,2,1,0:T(8,128)(2,1)S(1)}, u32[]{:S(2)}, u32[]{:S(2)}) %collective-permute-start.30) | collective-permute-done | bytes 266272 | tf_op jit(solution)/shard_map/ppermute | solution.py:365
  (134 shorter events, 63.4 us)
Async XLA Ops:
  0.6 37.0 %collective-permute-start = (bf16[4096,128]{1,0:T(8,128)(2,1)}, bf16[4096,128]{1,0:T(8,128)(2,1)}, u32[]{:S(2)}, u32[]{:S(2)}) collective-permute-start(bf16[4096,128]{1,0:T(8,128)(2,1)} %refs_0_.5), channel_id=1, source_target_pairs={{0,2},{1,3},{2,4},{3,5},{4,6},{5,7},{6,0},{7,1},{8,10},{9,11},{10,... | collective-permute-start | bytes 3145736 | tf_op jit(solution)/shard_map/ppermute | solution.py:365
  3.7 34.0 %collective-permute-start.1 = (bf16[4096,128]{1,0:T(8,128)(2,1)}, bf16[4096,128]{1,0:T(8,128)(2,1)S(1)}, u32[]{:S(2)}, u32[]{:S(2)}) collective-permute-start(bf16[4096,128]{1,0:T(8,128)(2,1)} %refs_0_.5), channel_id=1, source_target_pairs={{0,1},{1,0},{2,3},{3,2},{4,5},{5,4},{6,7},{7,6},{8,9},{9,8},{10,11... | collective-permute-start | bytes 3145736 | tf_op jit(solution)/shard_map/ppermute | solution.py:362
  5.2 27.7 %collective-permute-start.2 = (bf16[1,64,1024]{2,1,0:T(8,128)(2,1)}, bf16[1,64,1024]{2,1,0:T(8,128)(2,1)S(1)}, u32[]{:S(2)}, u32[]{:S(2)}) collective-permute-start(bf16[1,64,1024]{2,1,0:T(8,128)(2,1)} %param.12), channel_id=1, source_target_pairs={{0,2},{1,3},{2,4},{3,5},{4,6},{5,7},{6,0},{7,1},{8,10},{9,11},{10,... | collective-permute-start | bytes 393224 | tf_op jit(solution)/shard_map/ppermute | solution.py:289
  6.8 30.9 %collective-permute-start.3 = (bf16[1,64,1024]{2,1,0:T(8,128)(2,1)}, bf16[1,64,1024]{2,1,0:T(8,128)(2,1)S(1)}, u32[]{:S(2)}, u32[]{:S(2)}) collective-permute-start(bf16[1,64,1024]{2,1,0:T(8,128)(2,1)} %param.12), channel_id=1, source_target_pairs={{0,4},{1,5},{2,6},{3,7},{4,0},{5,1},{6,2},{7,3},{8,12},{9,13},{10,... | collective-permute-start | bytes 393224 | tf_op jit(solution)/shard_map/ppermute | solution.py:289
  8.0 29.6 %collective-permute-start.4 = (bf16[1,64,1024]{2,1,0:T(8,128)(2,1)}, bf16[1,64,1024]{2,1,0:T(8,128)(2,1)S(1)}, u32[]{:S(2)}, u32[]{:S(2)}) collective-permute-start(bf16[1,64,1024]{2,1,0:T(8,128)(2,1)} %param.12), channel_id=1, source_target_pairs={{0,6},{1,7},{2,0},{3,1},{4,2},{5,3},{6,4},{7,5},{8,14},{9,15},{10,... | collective-permute-start | bytes 393224 | tf_op jit(solution)/shard_map/ppermute | solution.py:289
  38.7 54.2 %all-to-all-start = ((bf16[8,64,1024]{2,1,0:T(8,128)(2,1)}), bf16[8,64,1024]{2,1,0:T(8,128)(2,1)S(1)}, u32[]{:S(2)}, u32[]{:S(2)}) async-start(bf16[8,64,1024]{2,1,0:T(8,128)(2,1)} %cut_down.1), calls=%async_computation | async-start | bytes 2097152 | tf_op jit(solution)/shard_map/all_to_all | solution.py:398
  45.2 46.6 %collective-permute-start.5 = (bf16[4096,128]{1,0:T(8,128)(2,1)}, bf16[4096,128]{1,0:T(8,128)(2,1)S(1)}, u32[]{:S(2)}, u32[]{:S(2)}) collective-permute-start(bf16[4096,128]{1,0:T(8,128)(2,1)} %collective-permute-done.refs_2_), channel_id=1, source_target_pairs={{0,2},{1,3},{2,4},{3,5},{4,6},{5,7},{6,0},{7,1},{8,10},{9,11},{10,... | collective-permute-start | bytes 3145736 | tf_op jit(solution)/shard_map/ppermute | solution.py:365
  47.3 45.6 %collective-permute-start.6 = (bf16[4096,128]{1,0:T(8,128)(2,1)}, bf16[4096,128]{1,0:T(8,128)(2,1)}, u32[]{:S(2)}, u32[]{:S(2)}) collective-permute-start(bf16[4096,128]{1,0:T(8,128)(2,1)} %collective-permute-done.refs_2_), channel_id=1, source_target_pairs={{0,1},{1,0},{2,3},{3,2},{4,5},{5,4},{6,7},{7,6},{8,9},{9,8},{10,11... | collective-permute-start | bytes 3145736 | tf_op jit(solution)/shard_map/ppermute | solution.py:362
  48.8 43.0 %collective-permute-start.7 = (bf16[4,64,1024]{2,1,0:T(8,128)(2,1)S(1)}, bf16[4,64,1024]{2,1,0:T(8,128)(2,1)S(1)}, u32[]{:S(2)}, u32[]{:S(2)}) collective-permute-start(bf16[4,64,1024]{2,1,0:T(8,128)(2,1)S(1)} %pad_maximum_fusion.1), channel_id=1, source_target_pairs={{0,1},{1,0},{2,3},{3,2},{4,5},{5,4},{6,7},{7,6},{8,9},{9,8},{10,11... | collective-permute-start | bytes 1572872 | tf_op jit(solution)/shard_map/ppermute | solution.py:362
  92.9 4.8 %collective-permute-start.10 = (bf16[8,64,1024]{2,1,0:T(8,128)(2,1)S(1)}, bf16[8,64,1024]{2,1,0:T(8,128)(2,1)}, u32[]{:S(2)}, u32[]{:S(2)}) collective-permute-start(bf16[8,64,1024]{2,1,0:T(8,128)(2,1)S(1)} %all-to-all-done.refs_2_.near_ref), channel_id=1, source_target_pairs={{0,8},{8,0},{1,9},{9,1},{2,10},{10,2},{3,11},{11,3},{4,12},{12,4},... | collective-permute-start | bytes 3145736 | tf_op jit(solution)/shard_map/ppermute | solution.py:403
  93.0 4.8 %collective-permute-start.11 = (bf16[8,64,1024]{2,1,0:T(8,128)(2,1)S(1)}, bf16[8,64,1024]{2,1,0:T(8,128)(2,1)}, u32[]{:S(2)}, u32[]{:S(2)}) collective-permute-start(bf16[8,64,1024]{2,1,0:T(8,128)(2,1)S(1)} %constant_dynamic-update-slice_fusion.refs_4_.refs_9_), channel_id=1, source_target_pairs={{0,8},{8,0},{1,9},{9,1},{2,10},{10,2},{3,11},{11,3},{4,12},{12,4},... | collective-permute-start | bytes 3145736 | tf_op jit(solution)/shard_map/ppermute | solution.py:403
  94.6 27.3 %collective-permute-start.8 = (bf16[4096,128]{1,0:T(8,128)(2,1)}, bf16[4096,128]{1,0:T(8,128)(2,1)}, u32[]{:S(2)}, u32[]{:S(2)}) collective-permute-start(bf16[4096,128]{1,0:T(8,128)(2,1)} %copy-done.24), channel_id=1, source_target_pairs={{0,2},{1,3},{2,4},{3,5},{4,6},{5,7},{6,0},{7,1},{8,10},{9,11},{10,... | collective-permute-start | bytes 3145736 | tf_op jit(solution)/shard_map/ppermute | solution.py:365
  96.1 25.8 %collective-permute-start.9 = (bf16[4096,128]{1,0:T(8,128)(2,1)}, bf16[4096,128]{1,0:T(8,128)(2,1)}, u32[]{:S(2)}, u32[]{:S(2)}) collective-permute-start(bf16[4096,128]{1,0:T(8,128)(2,1)} %copy-done.24), channel_id=1, source_target_pairs={{0,1},{1,0},{2,3},{3,2},{4,5},{5,4},{6,7},{7,6},{8,9},{9,8},{10,11... | collective-permute-start | bytes 3145736 | tf_op jit(solution)/shard_map/ppermute | solution.py:362
  121.9 26.7 %collective-permute-start.13 = (s16[2,2,1040,128]{3,2,1,0:T(8,128)(2,1)}, s16[2,2,1040,128]{3,2,1,0:T(8,128)(2,1)S(1)}, u32[]{:S(2)}, u32[]{:S(2)}) collective-permute-start(s16[2,2,1040,128]{3,2,1,0:T(8,128)(2,1)} %add_parts.13), channel_id=1, source_target_pairs={{0,2},{1,3},{2,4},{3,5},{4,6},{5,7},{6,0},{7,1},{8,10},{9,11},{10,... | collective-permute-start | bytes 3194888 | tf_op jit(solution)/shard_map/ppermute | solution.py:365
  122.6 23.9 %collective-permute-start.12 = (bf16[4096,128]{1,0:T(8,128)(2,1)}, bf16[4096,128]{1,0:T(8,128)(2,1)S(1)}, u32[]{:S(2)}, u32[]{:S(2)}) collective-permute-start(bf16[4096,128]{1,0:T(8,128)(2,1)} %collective-permute-done.8.refs_6_), channel_id=1, source_target_pairs={{0,1},{1,0},{2,3},{3,2},{4,5},{5,4},{6,7},{7,6},{8,9},{9,8},{10,11... | collective-permute-start | bytes 3145736 | tf_op jit(solution)/shard_map/ppermute | solution.py:362
  150.9 15.2 %collective-permute-start.15 = (f32[32,4096]{1,0:T(8,128)}, f32[32,4096]{1,0:T(8,128)}, u32[]{:S(2)}, u32[]{:S(2)}) collective-permute-start(f32[32,4096]{1,0:T(8,128)} %constant_dynamic-slice_fusion.4), channel_id=1, source_target_pairs={{0,1},{1,0},{2,3},{3,2},{4,5},{5,4},{6,7},{7,6},{8,9},{9,8},{10,11... | collective-permute-start | bytes 1572872 | tf_op jit(solution)/shard_map/ppermute | solution.py:362
  157.1 33.9 %collective-permute-start.16 = (s16[2,2,1040,128]{3,2,1,0:T(8,128)(2,1)}, s16[2,2,1040,128]{3,2,1,0:T(8,128)(2,1)S(1)}, u32[]{:S(2)}, u32[]{:S(2)}) collective-permute-start(s16[2,2,1040,128]{3,2,1,0:T(8,128)(2,1)} %add_parts.14), channel_id=1, source_target_pairs={{0,2},{1,3},{2,4},{3,5},{4,6},{5,7},{6,0},{7,1},{8,10},{9,11},{10,... | collective-permute-start | bytes 3194888 | tf_op jit(solution)/shard_map/ppermute | solution.py:365
  157.1 34.0 %collective-permute-start.14 = (s16[4,1,1040,128]{3,2,1,0:T(8,128)(2,1)}, s16[4,1,1040,128]{3,2,1,0:T(8,128)(2,1)S(1)}, u32[]{:S(2)}, u32[]{:S(2)}) collective-permute-start(s16[4,1,1040,128]{3,2,1,0:T(8,128)(2,1)} %get-tuple-element.82), channel_id=1, source_target_pairs={{0,1},{1,0},{2,3},{3,2},{4,5},{5,4},{6,7},{7,6},{8,9},{9,8},{10,11... | collective-permute-start | bytes 3194888 | tf_op jit(solution)/shard_map/ppermute | solution.py:362
  167.2 22.5 %collective-permute-start.17 = (f32[8,4096]{1,0:T(8,128)S(1)}, f32[8,4096]{1,0:T(8,128)S(1)}, u32[]{:S(2)}, u32[]{:S(2)}) collective-permute-start(f32[8,4096]{1,0:T(8,128)S(1)} %get-tuple-element.130), channel_id=1, source_target_pairs={{0,2},{1,3},{2,4},{3,5},{4,6},{5,7},{6,0},{7,1},{8,10},{9,11},{10,... | collective-permute-start | bytes 393224 | tf_op jit(solution)/shard_map/ppermute | solution.py:441
  167.4 23.7 %collective-permute-start.18 = (f32[8,4096]{1,0:T(8,128)S(1)}, f32[8,4096]{1,0:T(8,128)S(1)}, u32[]{:S(2)}, u32[]{:S(2)}) collective-permute-start(f32[8,4096]{1,0:T(8,128)S(1)} %get-tuple-element.129), channel_id=1, source_target_pairs={{0,4},{1,5},{2,6},{3,7},{4,0},{5,1},{6,2},{7,3},{8,12},{9,13},{10,... | collective-permute-start | bytes 393224 | tf_op jit(solution)/shard_map/ppermute | solution.py:441
  169.9 21.2 %collective-permute-start.19 = (f32[8,4096]{1,0:T(8,128)S(1)}, f32[8,4096]{1,0:T(8,128)S(1)}, u32[]{:S(2)}, u32[]{:S(2)}) collective-permute-start(f32[8,4096]{1,0:T(8,128)S(1)} %get-tuple-element.128), channel_id=1, source_target_pairs={{0,6},{1,7},{2,0},{3,1},{4,2},{5,3},{6,4},{7,5},{8,14},{9,15},{10,... | collective-permute-start | bytes 393224 | tf_op jit(solution)/shard_map/ppermute | solution.py:441
  192.1 20.1 %collective-permute-start.21 = (f32[8,64,1024]{2,1,0:T(8,128)}, f32[8,64,1024]{2,1,0:T(8,128)}, u32[]{:S(2)}, u32[]{:S(2)}) collective-permute-start(f32[8,64,1024]{2,1,0:T(8,128)} %get-tuple-element.98), channel_id=1, source_target_pairs={{0,8},{8,0},{1,9},{9,1},{2,10},{10,2},{3,11},{11,3},{4,12},{12,4},... | collective-permute-start | bytes 6291464 | tf_op jit(solution)/shard_map/ppermute | solution.py:505
  192.1 26.9 %collective-permute-start.20 = (s16[4,1,1040,128]{3,2,1,0:T(8,128)(2,1)}, s16[4,1,1040,128]{3,2,1,0:T(8,128)(2,1)S(1)}, u32[]{:S(2)}, u32[]{:S(2)}) collective-permute-start(s16[4,1,1040,128]{3,2,1,0:T(8,128)(2,1)} %get-tuple-element.96), channel_id=1, source_target_pairs={{0,1},{1,0},{2,3},{3,2},{4,5},{5,4},{6,7},{7,6},{8,9},{9,8},{10,11... | collective-permute-start | bytes 3194888 | tf_op jit(solution)/shard_map/ppermute | solution.py:362
  198.1 34.1 %collective-permute-start.25 = (s16[2,2,1040,128]{3,2,1,0:T(8,128)(2,1)}, s16[2,2,1040,128]{3,2,1,0:T(8,128)(2,1)S(1)}, u32[]{:S(2)}, u32[]{:S(2)}) collective-permute-start(s16[2,2,1040,128]{3,2,1,0:T(8,128)(2,1)} %add_parts.17), channel_id=1, source_target_pairs={{0,2},{1,3},{2,4},{3,5},{4,6},{5,7},{6,0},{7,1},{8,10},{9,11},{10,... | collective-permute-start | bytes 3194888 | tf_op jit(solution)/shard_map/ppermute | solution.py:365
  212.0 20.2 %collective-permute-start.23 = (s16[1,1,1040,128]{3,2,1,0:T(8,128)(2,1)}, s16[1,1,1040,128]{3,2,1,0:T(8,128)(2,1)S(1)}, u32[]{:S(2)}, u32[]{:S(2)}) collective-permute-start(s16[1,1,1040,128]{3,2,1,0:T(8,128)(2,1)} %add_parts.15), channel_id=1, source_target_pairs={{0,2},{1,3},{2,4},{3,5},{4,6},{5,7},{6,0},{7,1},{8,10},{9,11},{10,... | collective-permute-start | bytes 798728 | tf_op jit(solution)/shard_map/ppermute | solution.py:365
  222.7 14.5 %collective-permute-start.24 = (s16[1,1,1040,128]{3,2,1,0:T(8,128)(2,1)}, s16[1,1,1040,128]{3,2,1,0:T(8,128)(2,1)S(1)}, u32[]{:S(2)}, u32[]{:S(2)}) collective-permute-start(s16[1,1,1040,128]{3,2,1,0:T(8,128)(2,1)} %add_parts.16), channel_id=1, source_target_pairs={{0,2},{1,3},{2,4},{3,5},{4,6},{5,7},{6,0},{7,1},{8,10},{9,11},{10,... | collective-permute-start | bytes 798728 | tf_op jit(solution)/shard_map/ppermute | solution.py:365
  237.1 46.9 %all-to-all-start.1 = ((s16[8,80,1024]{2,1,0:T(8,128)(2,1)}), s16[8,80,1024]{2,1,0:T(8,128)(2,1)S(1)}, u32[]{:S(2)}, u32[]{:S(2)}) async-start(s16[8,80,1024]{2,1,0:T(8,128)(2,1)} %pack_gradients.1), calls=%async_computation.1 | async-start | bytes 2621440 | tf_op jit(solution)/shard_map/all_to_all | solution.py:525
  243.6 24.6 %collective-permute-start.27 = (s16[1,2,1040,128]{3,2,1,0:T(8,128)(2,1)}, s16[1,2,1040,128]{3,2,1,0:T(8,128)(2,1)S(1)}, u32[]{:S(2)}, u32[]{:S(2)}) collective-permute-start(s16[1,2,1040,128]{3,2,1,0:T(8,128)(2,1)} %add_parts.19), channel_id=1, source_target_pairs={{0,1},{1,0},{2,3},{3,2},{4,5},{5,4},{6,7},{7,6},{8,9},{9,8},{10,11... | collective-permute-start | bytes 1597448 | tf_op jit(solution)/shard_map/ppermute | solution.py:362
  248.4 23.6 %collective-permute-start.26 = (s16[1,1,1040,128]{3,2,1,0:T(8,128)(2,1)}, s16[1,1,1040,128]{3,2,1,0:T(8,128)(2,1)S(1)}, u32[]{:S(2)}, u32[]{:S(2)}) collective-permute-start(s16[1,1,1040,128]{3,2,1,0:T(8,128)(2,1)} %add_parts.18), channel_id=1, source_target_pairs={{0,2},{1,3},{2,4},{3,5},{4,6},{5,7},{6,0},{7,1},{8,10},{9,11},{10,... | collective-permute-start | bytes 798728 | tf_op jit(solution)/shard_map/ppermute | solution.py:365
  274.8 15.9 %collective-permute-start.29 = (s16[1,1,1040,128]{3,2,1,0:T(8,128)(2,1)}, s16[1,1,1040,128]{3,2,1,0:T(8,128)(2,1)S(1)}, u32[]{:S(2)}, u32[]{:S(2)}) collective-permute-start(s16[1,1,1040,128]{3,2,1,0:T(8,128)(2,1)} %add_parts.22), channel_id=1, source_target_pairs={{0,2},{1,3},{2,4},{3,5},{4,6},{5,7},{6,0},{7,1},{8,10},{9,11},{10,... | collective-permute-start | bytes 798728 | tf_op jit(solution)/shard_map/ppermute | solution.py:365
  281.7 10.0 %collective-permute-start.28 = (s16[1,1,1040,128]{3,2,1,0:T(8,128)(2,1)}, s16[1,1,1040,128]{3,2,1,0:T(8,128)(2,1)S(1)}, u32[]{:S(2)}, u32[]{:S(2)}) collective-permute-start(s16[1,1,1040,128]{3,2,1,0:T(8,128)(2,1)} %add_parts.21), channel_id=1, source_target_pairs={{0,2},{1,3},{2,4},{3,5},{4,6},{5,7},{6,0},{7,1},{8,10},{9,11},{10,... | collective-permute-start | bytes 798728 | tf_op jit(solution)/shard_map/ppermute | solution.py:365
  294.5 9.5 %collective-permute-start.30 = (s16[1,1,1040,128]{3,2,1,0:T(8,128)(2,1)}, s16[1,1,1040,128]{3,2,1,0:T(8,128)(2,1)S(1)}, u32[]{:S(2)}, u32[]{:S(2)}) collective-permute-start(s16[1,1,1040,128]{3,2,1,0:T(8,128)(2,1)} %add_parts.24), channel_id=1, source_target_pairs={{0,2},{1,3},{2,4},{3,5},{4,6},{5,7},{6,0},{7,1},{8,10},{9,11},{10,... | collective-permute-start | bytes 798728 | tf_op jit(solution)/shard_map/ppermute | solution.py:365
  (29 other events, 297.0 us)

commit v5 on v4

--- a/solution.py
+++ b/solution.py
@@ -181,11 +181,14 @@
     ref[rows:, :] = jnp.broadcast_to(code, (PAD, code.shape[1])).astype(jnp.int32).astype(jnp.int16)
 
 
-def sum_kernel(coded, place_ref, *refs):
+def sum_kernel(coded, each, place_ref, *refs):
     total = refs[0][0]
     rows = total.shape[0]
-    for ref in refs[1 : 1 + coded]:
-        total = total + decode(ref[0, 0, :rows, :], ref[0, 0, rows : rows + 1, :])
+    refs = list(refs[1:])
+    for count in coded:
+        values = [decode(ref[0, 0, :rows, :], ref[0, 0, rows : rows + 1, :]) for ref in refs[:count]]
+        total = total + (jnp.where(pl.program_id(1) < each, *values) if count == 2 else values[0])
+        refs = refs[count:]
     out_ref = refs[-1]
     if out_ref.dtype == BF16:
         out_ref[...] = total.astype(BF16)
@@ -193,63 +196,79 @@
         put(out_ref.at[0, 0], *encode(total))
 
 
-def add_parts(place, block_rows, count, kept, coded, first=0, blocks=None, last=False):
+def add_parts(place, block_rows, count, kept, coded, first=0, blocks=None, last=None, beside=()):
     part, pick = kept
     rows, cols = part.shape[1:]
     blocks, held = blocks or rows // block_rows, block_rows + PAD
     rows = blocks * block_rows
 
-    def coded_spec(pick):
-        return pl.BlockSpec((1, 1, held, cols), lambda i, b, p: (pick(i, p), b, 0, 0))
+    def coded_spec(pick, start=0, size=blocks):
+        return pl.BlockSpec(
+            (1, 1, held, cols), lambda i, b, p: (pick(i, p), jnp.clip(b - start, 0, size - 1) if size < blocks else b, 0, 0)
+        )
 
     in_specs = [pl.BlockSpec((1, block_rows, cols), lambda i, b, p: (pick(i, p), first + b, 0))]
-    in_specs += [coded_spec(q) for _, q in coded]
-    if last:
-        out_shape = jax.ShapeDtypeStruct((rows, cols), BF16)
-        out_spec = pl.BlockSpec((block_rows, cols), lambda i, b, p: (b, 0))
+    arrays, counts = [], []
+    for held_in, q in coded:
+        held_in = held_in if isinstance(held_in, tuple) else (held_in,)
+        size = blocks // len(held_in)
+        in_specs += [coded_spec(q, k * size, size) for k in range(len(held_in))]
+        arrays += held_in
+        counts.append(len(held_in))
+    if last is not None:
+        out_shape = jax.ShapeDtypeStruct((2 * rows, cols), BF16)
+        out_spec = pl.BlockSpec((block_rows, cols), lambda i, b, p: (last + b, 0))
     else:
         out_shape = jax.ShapeDtypeStruct((count, blocks, held, cols), jnp.int16)
         out_spec = coded_spec(lambda i, p: i)
     return pl.pallas_call(
-        functools.partial(sum_kernel, len(coded)),
+        functools.partial(sum_kernel, tuple(counts), blocks // 2),
         grid_spec=pltpu.PrefetchScalarGridSpec(
-            num_scalar_prefetch=1, grid=(count, blocks), in_specs=in_specs, out_specs=out_spec
+            num_scalar_prefetch=1,
+            grid=(count, blocks),
+            in_specs=in_specs + [pl.BlockSpec(memory_space=pl.ANY)] * len(beside),
+            out_specs=out_spec,
         ),
         out_shape=out_shape,
+        input_output_aliases={2 + len(arrays): 0} if beside else {},
         cost_estimate=pl.CostEstimate(flops=0, bytes_accessed=count * rows * cols * 8, transcendentals=0),
         name="add_parts",
-    )(place, part, *[a for a, _ in coded])
+    )(place, part, *arrays, *beside)
 
 
 def pack_kernel(gdown_ref, rdown_ref, gup_ref, rup_ref, out_ref):
-    rank, width = gdown_ref.shape[1:]
+    count, rank, width = gdown_ref.shape
     own = gup_ref.shape[1]
     groups = gup_ref.shape[2] // width
-    q, code = encode(gdown_ref[0] + rdown_ref[0])
-    out_ref[0, :rank, :] = q
-    tail, codes = [], [code]
-    up = gup_ref[0] + rup_ref[0]
-    for g in range(groups):
-        q, code = encode(up[:, g * width : (g + 1) * width])
-        tail.append(q.astype(jnp.int32))
-        codes.append(code)
     row = lax.broadcasted_iota(jnp.int32, (PAD - groups * own, width), 0)
-    last = jnp.zeros(row.shape, F32)
-    for g, code in enumerate(codes):
-        last = jnp.where(row == g, code, last)
-    out_ref[0, rank:, :] = jnp.concatenate([*tail, last.astype(jnp.int32)], axis=0).astype(jnp.int16)
-
-
-def unpack_kernel(in_ref, down_ref, up_ref):
-    width = in_ref.shape[2]
-    own = up_ref.shape[1]
-    groups = up_ref.shape[2] // width
+    for s in range(count):
+        q, code = encode(gdown_ref[s] + rdown_ref[s])
+        out_ref[s, :rank, :] = q
+        tail, codes = [], [code]
+        up = gup_ref[s] + rup_ref[s]
+        for g in range(groups):
+            q, code = encode(up[:, g * width : (g + 1) * width])
+            tail.append(q.astype(jnp.int32))
+            codes.append(code)
+        last = jnp.zeros(row.shape, F32)
+        for g, code in enumerate(codes):
+            last = jnp.where(row == g, code, last)
+        out_ref[s, rank:, :] = jnp.concatenate([*tail, last.astype(jnp.int32)], axis=0).astype(jnp.int16)
+
+
+def unpack_kernel(outer, in_ref, down_ref, up_ref):
+    count, _, width = in_ref.shape
+    n, own, out_width = up_ref.shape
+    groups = out_width // width
     rank = down_ref.shape[1]
-    tail = in_ref[0, rank:, :].astype(jnp.int32).astype(F32)
-    steps = jnp.exp2(tail[groups * own :] * (1.0 / STEPS)) * (ADAPTER_SCALE / TOP)
-    down_ref[0] = in_ref[0, :rank, :].astype(jnp.int32).astype(F32) * steps[:1]
-    for g in range(groups):
-        up_ref[0, :, g * width : (g + 1) * width] = tail[g * own : (g + 1) * own] * steps[g + 1 : g + 2]
+    for s in range(count):
+        source = pl.program_id(0) * count + s
+        tail = in_ref[s, rank:, :].astype(jnp.int32).astype(F32)
+        steps = jnp.exp2(tail[groups * own :] * (1.0 / STEPS)) * (ADAPTER_SCALE / TOP)
+        down_ref[0, :, s * width : (s + 1) * width] = in_ref[s, :rank, :].astype(jnp.int32).astype(F32) * steps[:1]
+        place = (source % (n // outer)) * outer + source // (n // outer)
+        for g in range(groups):
+            up_ref[place, :, g * width : (g + 1) * width] = tail[g * own : (g + 1) * own] * steps[g + 1 : g + 2]
 
 
 def body(
@@ -373,7 +392,11 @@
     def ring_step(s, kept, near, run, c):
         at = behind(s % outer)
         coded = [(near, at)] + [(r, first) for r in run]
-        return add_parts(place, block_rows, 1, (kept, at), coded, c * each, each, last=s == outer)
+        return add_parts(place, block_rows, 1, (kept, at), coded, c * each, each)
+
+    def both_step(s, kept, near, run, beside=()):
+        at = behind(s % outer)
+        return add_parts(place, block_rows, 1, (kept, at), [(near, at), (run, first)], 0, 2 * each, 0 if beside else None, beside)
 
     def pair_step(s, kept, run):
         at = behind(s)
@@ -385,7 +408,7 @@
             return p[1] if got else 1 - p[1]
 
         coded = [(run, whose)] + [(g, first) for g in got]
-        return add_parts(place, block_rows, 1, (kept, lambda i, p: p[0] * inner + whose(i, p)), coded, last=bool(got))
+        return add_parts(place, block_rows, 1, (kept, lambda i, p: p[0] * inner + whose(i, p)), coded, last=2 * each if got else None)
 
     order = []
     for s in range(outer):
@@ -427,12 +450,14 @@
             add(last)
             block, cots[-1], sums[last] = tie((block, cots[-1], sums[last]))
     send(last)
-    cots[-1], kept, sents, runs, shrink = tie((cots[-1], kept, sents, runs, shrink))
 
     shrink = jnp.concatenate([shrink, late_shrink], axis=1)
-    theirs = swapped(lax.dynamic_slice_in_dim(shrink, other * half, half, 0))
+    theirs = lax.dynamic_slice_in_dim(shrink, other * half, half, 0)
+    mine = lax.dynamic_slice_in_dim(shrink, my_inner * half, half, 0)
+    cots[-1], kept, sents, runs, mine, theirs = tie((cots[-1], kept, sents, runs, mine, theirs))
+    theirs = swapped(theirs)
     add(last)
-    mine = lax.dynamic_slice_in_dim(shrink, my_inner * half, half, 0) + theirs
+    mine += theirs
     send(last)
     cots[-1], mine = tie((cots[-1], mine))
     shrink = [lax.dynamic_slice_in_dim(mine, my_outer * own, own, 0)]
@@ -507,15 +532,16 @@
     packed_rows = rank + PAD
     packed = pl.pallas_call(
         pack_kernel,
-        grid=(n,),
+        grid=(2,),
         in_specs=[
-            pl.BlockSpec((1, rank, width), lambda i: (i, 0, 0)),
-            pl.BlockSpec((1, rank, width), lambda i: (i, 0, 0)),
-            pl.BlockSpec((1, own, out_width), lambda i: (i, 0, 0)),
-            pl.BlockSpec((1, own, out_width), lambda i: (i, 0, 0)),
+            pl.BlockSpec((n // 2, rank, width), lambda i: (i, 0, 0)),
+            pl.BlockSpec((n // 2, rank, width), lambda i: (i, 0, 0)),
+            pl.BlockSpec((n // 2, own, out_width), lambda i: (i, 0, 0)),
+            pl.BlockSpec((n // 2, own, out_width), lambda i: (i, 0, 0)),
         ],
-        out_specs=pl.BlockSpec((1, packed_rows, width), lambda i: (i, 0, 0)),
+        out_specs=pl.BlockSpec((n // 2, packed_rows, width), lambda i: (i, 0, 0)),
         out_shape=jax.ShapeDtypeStruct((n, packed_rows, width), jnp.int16),
+        compiler_params=params,
         name="pack_gradients",
     )(gdown, rdown, gup, rup)
     near, packed = tie((near, packed))
@@ -524,17 +550,18 @@
     runs, packed = tie((runs, packed))
     landed = lax.all_to_all(packed, "mp", split_axis=0, concat_axis=0, tiled=True)
     down_gradient, up_gradient = pl.pallas_call(
-        unpack_kernel,
-        grid=(n,),
-        in_specs=[pl.BlockSpec((1, packed_rows, width), lambda i: (i, 0, 0))],
+        functools.partial(unpack_kernel, outer),
+        grid=(2,),
+        in_specs=[pl.BlockSpec((n // 2, packed_rows, width), lambda i: (i, 0, 0))],
         out_specs=[
-            pl.BlockSpec((1, rank, width), lambda i: (0, 0, i)),
-            pl.BlockSpec((1, own, out_width), lambda i: ((i % inner) * outer + i // inner, 0, 0)),
+            pl.BlockSpec((1, rank, entire_width // 2), lambda i: (0, 0, i)),
+            pl.BlockSpec((n, own, out_width), lambda i: (0, 0, 0)),
         ],
         out_shape=[
             jax.ShapeDtypeStruct((1, rank, entire_width), F32),
             jax.ShapeDtypeStruct((n, own, out_width), F32),
         ],
+        compiler_params=params,
         name="unpack_gradients",
     )(landed)
 
@@ -561,21 +588,16 @@
         name="token_gradient",
     )(tile_slot, cot_all, frozen_weight, near_down, far_down, back)
     run = runs[last][0]
-    outs[last] = pair_end(pair, run, [swapped(pair_end(pair, run, []))])
-    add(0)
-    send(0)
-    runs, outs, token_gradient = tie((runs, outs, token_gradient))
-    for c in (1, 0):
-        add(c)
-        send(c)
-    runs, down_gradient, up_gradient = tie((runs, down_gradient, up_gradient))
-    while done[1] < outer:
-        for c in (1, 0):
-            if done[c] < outer:
-                add(c)
-                if done[c] < outer:
-                    send(c)
-    output = jnp.concatenate([sums[0], sums[1], outs[last]], axis=0)
+    got = swapped(pair_end(pair, run, []))
+    both = (near[0], near[1])
+    run = (runs[0][0], runs[1][0])
+    for s in range(2, outer):
+        run = shifted(both_step(s, kept, both, run))
+        if s == 2:
+            got, run, token_gradient = tie((got, run, token_gradient))
+            outs[last] = pair_end(pair, runs[last][0], [got])
+    run, down_gradient, up_gradient, outs = tie((run, down_gradient, up_gradient, outs))
+    output = both_step(outer, kept, both, run, (outs[last],))
 
     up_gradient = up_gradient.reshape(1, rank, out_width)
     return output, token_gradient, jnp.swapaxes(down_gradient, 1, 2), up_gradient

time: 311 us -> 301 us (0.968)
  Pallas kernels: 130 us -> 117 us
  waiting for transfers between devices: 109 us -> 116 us
    pallas_call x15 -> x12, Pallas kernels: 53.5 us -> 41.2 us  [the longest x10 35.2 us: add_parts(): pl.pallas_call(functools.partial(sum_kernel, tuple(counts), blocks // 2),...]
    ppermute x12 -> x10, waiting for transfers between devices: 26.1 us -> 34.3 us  [shifted(): return lax.ppermute(x, 'mp', ring)]
    ppermute x12 -> x10, starting transfers between devices: 22.4 us -> 20.9 us  [shifted(): return lax.ppermute(x, 'mp', ring)]
    unnamed x61 -> x53, local copies, waits for them, and re-layouts: 8.85 us -> 9.43 us
  transfers between devices with their start and end apart: 33 -> 31, of which waited for: 13 -> 13; matrix products, arithmetic and copies ran while one was open for 2% -> 2% of each run, Pallas kernels for 40% -> 38%
where the time goes in v5:
time: 301 us; the launch traced here: 300 us
  Pallas kernels  117 us (39%)
  waiting for transfers between devices  116 us (39%)
  starting transfers between devices  50.3 us (17%)
  local copies, waits for them, and re-layouts  11.1 us (4%)
  other arithmetic  3.99 us (1%)
    ppermute x9, waiting for transfers between devices, swapped(): return lax.ppermute(x, 'mp', swap)  57.9 us
    pallas_call x10, Pallas kernels, add_parts(): pl.pallas_call(functools.partial(sum_kernel, tuple(counts), blocks // 2),...  35.2 us
    ppermute x10, waiting for transfers between devices, shifted(): return lax.ppermute(x, 'mp', ring)  34.3 us
    pallas_call x2, Pallas kernels, forward(): pl.pallas_call(functools.partial(forward_kernel, start * (block_rows // T...  29.2 us
    ppermute x3, waiting for transfers between devices, body(): lax.ppermute(adapter_up, 'mp', [(i, (i + s * inner) % n) for i in range(n)])  21.8 us
    ppermute x10, starting transfers between devices, shifted(): return lax.ppermute(x, 'mp', ring)  20.9 us
    pallas_call x1, Pallas kernels, body(): pl.pallas_call(functools.partial(gradient_kernel, len(cots)), grid_spec=p...  18.6 us
    pallas_call x1, Pallas kernels, body(): pl.pallas_call(token_kernel, grid_spec=pltpu.PrefetchScalarGridSpec(num_s...  16.9 us
  transfers between devices with their start and end apart: 31, of which 13 were waited for; matrix products, arithmetic and copies ran while one was open for 2% of the time, Pallas kernels for 38%

profile of v5, /device:TPU:0, one launch (start us, length us, event | category | flops | bytes accessed | tf_op | source)
XLA Modules:
  0.0 300.2 jit_solution(7401834718807607947)
XLA Ops:
  0.6 3.1 %collective-permute-start = (bf16[4096,128]{1,0:T(8,128)(2,1)}, bf16[4096,128]{1,0:T(8,128)(2,1)}, u32[]{:S(2)}, u32[]{:S(2)}) collective-permute-start(bf16[4096,128]{1,0:T(8,128)(2,1)} %refs_0_.5), channel_id=1, source_target_pairs={{0,2},{1,3},{2,4},{3,5},{4,6},{5,7},{6,0},{7,1},{8,10},{9,11},{10,... | collective-permute-start | bytes 3145736 | tf_op jit(solution)/shard_map/ppermute | solution.py:384
  8.0 2.7 collective-permute-start.4
  10.7 5.2 %cut_down.1 = bf16[8,64,1024]{2,1,0:T(8,128)(2,1)} custom-call(bf16[1,64,8192]{2,1,0:T(8,128)(2,1)} %bitcast.15), custom_call_target="tpu_custom_call" | custom-call | tf_op jit(solution)/shard_map/cut_down/pallas_call | solution.py:309
  15.9 17.0 %collective-permute-done.2 = bf16[1,64,1024]{2,1,0:T(8,128)(2,1)S(1)} collective-permute-done((bf16[1,64,1024]{2,1,0:T(8,128)(2,1)}, bf16[1,64,1024]{2,1,0:T(8,128)(2,1)S(1)}, u32[]{:S(2)}, u32[]{:S(2)}) %collective-permute-start.2) | collective-permute-done | bytes 131104 | tf_op jit(solution)/shard_map/ppermute | solution.py:308
  32.9 4.8 %collective-permute-done.3 = bf16[1,64,1024]{2,1,0:T(8,128)(2,1)S(1)} collective-permute-done((bf16[1,64,1024]{2,1,0:T(8,128)(2,1)}, bf16[1,64,1024]{2,1,0:T(8,128)(2,1)S(1)}, u32[]{:S(2)}, u32[]{:S(2)}) %collective-permute-start.3) | collective-permute-done | bytes 131104 | tf_op jit(solution)/shard_map/ppermute | solution.py:308
  38.6 6.5 %all-to-all-start = ((bf16[8,64,1024]{2,1,0:T(8,128)(2,1)}), bf16[8,64,1024]{2,1,0:T(8,128)(2,1)S(1)}, u32[]{:S(2)}, u32[]{:S(2)}) async-start(bf16[8,64,1024]{2,1,0:T(8,128)(2,1)} %cut_down.1), calls=%async_computation | async-start | bytes 2097152 | tf_op jit(solution)/shard_map/all_to_all | solution.py:421
  49.5 42.2 %collective-permute-done.7 = bf16[4,64,1024]{2,1,0:T(8,128)(2,1)S(1)} collective-permute-done((bf16[4,64,1024]{2,1,0:T(8,128)(2,1)S(1)}, bf16[4,64,1024]{2,1,0:T(8,128)(2,1)S(1)}, u32[]{:S(2)}, u32[]{:S(2)}) %collective-permute-start.7) | collective-permute-done | bytes 524320 | tf_op jit(solution)/shard_map/ppermute | solution.py:381
  97.7 14.0 %forward.2 = (f32[64,2048]{1,0:T(8,128)}, f32[8,2048,128]{2,1,0:T(8,128)}) custom-call(s32[32]{0:T(128)} %fusion.7.slot_ref, s32[32]{0:T(128)} %get-tuple-element.126.upslot_ref, s32[2]{0:T(128)} %pad_add_fusion.place_ref, bf16[4096,1024]{1,0:T(8,128)(2,1)} %refs_8_.1, bf16[1024,1024]{1,0:T(8,128)(2,1)} %w_ref.1, bf16[8,64,1024]{2,1,0:T(8,128)(2,1)} %copy-done.6, ...), custom_call_target="tpu_custom_call" | custom-call | flops 8589934592 | bytes 12582912 | tf_op jit(solution)/shard_map/forward/pallas_call | solution.py:342
  111.7 4.5 %add_parts.10 = s16[2,2,1040,128]{3,2,1,0:T(8,128)(2,1)} custom-call(s32[2]{0:T(128)} %pad_add_fusion.place_ref, f32[8,2048,128]{2,1,0:T(8,128)} %get-tuple-element.74.refs_0_), custom_call_target="tpu_custom_call" | custom-call | bytes 4194304 | tf_op jit(solution)/shard_map/add_parts/pallas_call | solution.py:224
  116.2 5.6 %collective-permute-done.8.refs_6_ = bf16[4096,128]{1,0:T(8,128)(2,1)} collective-permute-done((bf16[4096,128]{1,0:T(8,128)(2,1)}, bf16[4096,128]{1,0:T(8,128)(2,1)}, u32[]{:S(2)}, u32[]{:S(2)}) %collective-permute-start.8) | collective-permute-done | bytes 1048608 | tf_op jit(solution)/shard_map/ppermute | solution.py:384
  123.1 15.2 %forward.3 = (f32[64,2048]{1,0:T(8,128)}, f32[4,2048,128]{2,1,0:T(8,128)}, s16[4,1,1040,128]{3,2,1,0:T(8,128)(2,1)}, s16[4,1,1040,128]{3,2,1,0:T(8,128)(2,1)}) custom-call(s32[32]{0:T(128)} %fusion.7.slot_ref, s32[32]{0:T(128)} %get-tuple-element.126.upslot_ref, s32[2]{0:T(128)} %pad_add_fusion.place_ref, bf16[4096,1024]{1,0:T(8,128)(2,1)} %refs_8_.1, ...), custom_call_target="tpu_custom_call" | custom-call | flops 8589934592 | bytes 12582912 | tf_op jit(solution)/shard_map/forward/pallas_call | solution.py:342
  140.4 6.0 %collective-permute-done.12.refs_7_ = bf16[4096,128]{1,0:T(8,128)(2,1)S(1)} collective-permute-done((bf16[4096,128]{1,0:T(8,128)(2,1)}, bf16[4096,128]{1,0:T(8,128)(2,1)S(1)}, u32[]{:S(2)}, u32[]{:S(2)}) %collective-permute-start.12) | collective-permute-done | bytes 1048608 | tf_op jit(solution)/shard_map/ppermute | solution.py:381
  150.0 4.7 %add_parts.11 = s16[2,2,1040,128]{3,2,1,0:T(8,128)(2,1)} custom-call(s32[2]{0:T(128)} %pad_add_fusion.place_ref, f32[8,2048,128]{2,1,0:T(8,128)} %get-tuple-element.74.refs_0_, s16[2,2,1040,128]{3,2,1,0:T(8,128)(2,1)} %copy-done.4), custom_call_target="tpu_custom_call" | custom-call | bytes 4194304 | tf_op jit(solution)/shard_map/add_parts/pallas_call | solution.py:224
  155.8 7.7 %collective-permute-done.15 = f32[32,4096]{1,0:T(8,128)S(1)} collective-permute-done((f32[32,4096]{1,0:T(8,128)}, f32[32,4096]{1,0:T(8,128)S(1)}, u32[]{:S(2)}, u32[]{:S(2)}) %collective-permute-start.15) | collective-permute-done | bytes 524320 | tf_op jit(solution)/shard_map/ppermute | solution.py:381
  167.5 18.6 %gradients.1 = (bf16[4096,1024]{1,0:T(8,128)(2,1)}, bf16[4096,128]{1,0:T(8,128)(2,1)}, f32[8,64,1024]{2,1,0:T(8,128)}, f32[8,64,1024]{2,1,0:T(8,128)}) custom-call(s32[32]{0:T(128)} %fusion.7.slot_ref, s32[32]{0:T(128)} %get-tuple-element.126.upslot_ref, s32[8]{0:T(128)} %stack.47.order_ref, bf16[4096,128]{1,0:T(8,128)(2,1)} %refs_0_.5, ...), custom_call_target="tpu_custom_call" | custom-call | flops 8589934592 | bytes 25165824 | tf_op jit(solution)/shard_map/gradients/pallas_call | solution.py:472
  190.9 4.7 %add_parts.14 = s16[2,2,1040,128]{3,2,1,0:T(8,128)(2,1)} custom-call(s32[2]{0:T(128)} %pad_add_fusion.place_ref, f32[8,2048,128]{2,1,0:T(8,128)} %get-tuple-element.74.refs_0_, s16[2,2,1040,128]{3,2,1,0:T(8,128)(2,1)} %copy-done.5), custom_call_target="tpu_custom_call" | custom-call | bytes 4194304 | tf_op jit(solution)/shard_map/add_parts/pallas_call | solution.py:224
  195.6 3.3 %collective-permute-start.25 = (s16[2,2,1040,128]{3,2,1,0:T(8,128)(2,1)}, s16[2,2,1040,128]{3,2,1,0:T(8,128)(2,1)S(1)}, u32[]{:S(2)}, u32[]{:S(2)}) collective-permute-start(s16[2,2,1040,128]{3,2,1,0:T(8,128)(2,1)} %add_parts.14), channel_id=1, source_target_pairs={{0,2},{1,3},{2,4},{3,5},{4,6},{5,7},{6,0},{7,1},{8,10},{9,11},{10,... | collective-permute-start | bytes 3194888 | tf_op jit(solution)/shard_map/ppermute | solution.py:384
  200.5 6.3 %up_gradient.1 = (f32[8,8,1024]{2,1,0:T(8,128)}, f32[8,8,1024]{2,1,0:T(8,128)}) custom-call(s32[32]{0:T(128)} %fusion.7.slot_ref, f32[8,4096]{1,0:T(8,128)} %add_add_fusion.shrink_ref, bf16[4096,1024]{1,0:T(8,128)(2,1)} %get-tuple-element.104.cot_ref), custom_call_target="tpu_custom_call" | custom-call | bytes 8388608 | tf_op jit(solution)/shard_map/up_gradient/pallas_call | solution.py:513
  210.4 3.4 %pack_gradients.1 = s16[8,80,1024]{2,1,0:T(8,128)(2,1)} custom-call(f32[8,64,1024]{2,1,0:T(8,128)} %get-tuple-element.98.gdown_ref, f32[8,64,1024]{2,1,0:T(8,128)} %collective-permute-done.21.rdown_ref, f32[8,8,1024]{2,1,0:T(8,128)} %get-tuple-element.105.gup_ref, f32[8,8,1024]{2,1,0:T(8,128)} %copy-done.14), custom_call_target="tpu_custom_call" | custom-call | tf_op jit(solution)/shard_map/pack_gradients/pallas_call | solution.py:533
  219.4 3.3 %collective-permute-start.24 = (s16[1,1,1040,128]{3,2,1,0:T(8,128)(2,1)}, s16[1,1,1040,128]{3,2,1,0:T(8,128)(2,1)S(1)}, u32[]{:S(2)}, u32[]{:S(2)}) collective-permute-start(s16[1,1,1040,128]{3,2,1,0:T(8,128)(2,1)} %add_parts.13), channel_id=1, source_target_pairs={{0,2},{1,3},{2,4},{3,5},{4,6},{5,7},{6,0},{7,1},{8,10},{9,11},{10,... | collective-permute-start | bytes 798728 | tf_op jit(solution)/shard_map/ppermute | solution.py:384
  222.7 7.0 %collective-permute-done.23.refs_3_ = s16[1,1,1040,128]{3,2,1,0:T(8,128)(2,1)S(1)} collective-permute-done((s16[1,1,1040,128]{3,2,1,0:T(8,128)(2,1)}, s16[1,1,1040,128]{3,2,1,0:T(8,128)(2,1)S(1)}, u32[]{:S(2)}, u32[]{:S(2)}) %collective-permute-start.23) | collective-permute-done | bytes 266272 | tf_op jit(solution)/shard_map/ppermute | solution.py:384
  229.6 5.0 %collective-permute-done.24.refs_4_ = s16[1,1,1040,128]{3,2,1,0:T(8,128)(2,1)S(1)} collective-permute-done((s16[1,1,1040,128]{3,2,1,0:T(8,128)(2,1)}, s16[1,1,1040,128]{3,2,1,0:T(8,128)(2,1)S(1)}, u32[]{:S(2)}, u32[]{:S(2)}) %collective-permute-start.24) | collective-permute-done | bytes 266272 | tf_op jit(solution)/shard_map/ppermute | solution.py:384
  235.3 3.6 %all-to-all-start.1 = ((s16[8,80,1024]{2,1,0:T(8,128)(2,1)}), s16[8,80,1024]{2,1,0:T(8,128)(2,1)S(1)}, u32[]{:S(2)}, u32[]{:S(2)}) async-start(s16[8,80,1024]{2,1,0:T(8,128)(2,1)} %pack_gradients.1), calls=%async_computation.1 | async-start | bytes 2621440 | tf_op jit(solution)/shard_map/all_to_all | solution.py:551
  238.9 3.5 %add_parts.16 = s16[1,2,1040,128]{3,2,1,0:T(8,128)(2,1)} custom-call(s32[2]{0:T(128)} %pad_add_fusion.place_ref, f32[4,2048,128]{2,1,0:T(8,128)} %get-tuple-element.82.refs_0_, s16[4,1,1040,128]{3,2,1,0:T(8,128)(2,1)} %copy-done, s16[4,1,1040,128]{3,2,1,0:T(8,128)(2,1)} %copy-done.1, s16[1,1,1040,128]{3,2,1,0:T(8,128)(2,1)} %copy-done.12, ...), custom_call_target="tpu_custom_call" | custom-call | bytes 2097152 | tf_op jit(solution)/shard_map/add_parts/pallas_call | solution.py:224
  244.4 2.9 add_parts.15
  248.8 16.9 %token_gradient.1 = bf16[4096,1024]{1,0:T(8,128)(2,1)} custom-call(s32[32]{0:T(128)} %fusion.7.slot_ref, bf16[4096,1024]{1,0:T(8,128)(2,1)} %get-tuple-element.104.cot_ref, bf16[1024,1024]{1,0:T(8,128)(2,1)} %w_ref.1, bf16[8,64,1024]{2,1,0:T(8,128)(2,1)} %copy-done.6, bf16[8,64,1024]{2,1,0:T(8,128)(2,1)} %collective-permute-done.10.refs_3_.far_ref, ...), custom_call_target="tpu_custom_call" | custom-call | flops 12884901888 | bytes 16777216 | tf_op jit(solution)/shard_map/token_gradient/pallas_call | solution.py:568
  265.7 9.7 %collective-permute-done.27.refs_3_ = s16[1,2,1040,128]{3,2,1,0:T(8,128)(2,1)S(1)} collective-permute-done((s16[1,2,1040,128]{3,2,1,0:T(8,128)(2,1)}, s16[1,2,1040,128]{3,2,1,0:T(8,128)(2,1)S(1)}, u32[]{:S(2)}, u32[]{:S(2)}) %collective-permute-start.27) | collective-permute-done | bytes 532512 | tf_op jit(solution)/shard_map/ppermute | solution.py:384
  276.2 3.3 %add_parts.17 = s16[1,2,1040,128]{3,2,1,0:T(8,128)(2,1)} custom-call(s32[2]{0:T(128)} %pad_add_fusion.place_ref, f32[4,2048,128]{2,1,0:T(8,128)} %get-tuple-element.82.refs_0_, s16[4,1,1040,128]{3,2,1,0:T(8,128)(2,1)} %copy-done, s16[4,1,1040,128]{3,2,1,0:T(8,128)(2,1)} %copy-done.1, s16[1,2,1040,128]{3,2,1,0:T(8,128)(2,1)} %copy-done.9), custom_call_target="tpu_custom_call" | custom-call | bytes 2097152 | tf_op jit(solution)/shard_map/add_parts/pallas_call | solution.py:224
  279.5 4.9 %collective-permute-start.28 = (s16[1,2,1040,128]{3,2,1,0:T(8,128)(2,1)}, s16[1,2,1040,128]{3,2,1,0:T(8,128)(2,1)S(1)}, u32[]{:S(2)}, u32[]{:S(2)}) collective-permute-start(s16[1,2,1040,128]{3,2,1,0:T(8,128)(2,1)} %add_parts.17), channel_id=1, source_target_pairs={{0,2},{1,3},{2,4},{3,5},{4,6},{5,7},{6,0},{7,1},{8,10},{9,11},{10,... | collective-permute-start | bytes 1597448 | tf_op jit(solution)/shard_map/ppermute | solution.py:384
  284.4 3.1 %add_parts.18.refs_4_ = bf16[4096,128]{1,0:T(8,128)(2,1)} custom-call(s32[2]{0:T(128)} %pad_add_fusion.place_ref, f32[8,2048,128]{2,1,0:T(8,128)} %get-tuple-element.74.refs_0_, s16[2,2,1040,128]{3,2,1,0:T(8,128)(2,1)} %copy-done.3, s16[1,2,1040,128]{3,2,1,0:T(8,128)(2,1)} %copy-done.7), custom_call_target="tpu_custom_call" | custom-call | bytes 2097152 | tf_op jit(solution)/shard_map/add_parts/pallas_call | solution.py:224
  291.2 5.0 %collective-permute-done.28.refs_3_ = s16[1,2,1040,128]{3,2,1,0:T(8,128)(2,1)S(1)} collective-permute-done((s16[1,2,1040,128]{3,2,1,0:T(8,128)(2,1)}, s16[1,2,1040,128]{3,2,1,0:T(8,128)(2,1)S(1)}, u32[]{:S(2)}, u32[]{:S(2)}) %collective-permute-start.28) | collective-permute-done | bytes 532512 | tf_op jit(solution)/shard_map/ppermute | solution.py:384
  297.0 3.1 %add_parts.19 = bf16[4096,128]{1,0:T(8,128)(2,1)} custom-call(s32[2]{0:T(128)} %pad_add_fusion.place_ref, f32[4,2048,128]{2,1,0:T(8,128)} %get-tuple-element.82.refs_0_, s16[4,1,1040,128]{3,2,1,0:T(8,128)(2,1)} %copy-done, s16[4,1,1040,128]{3,2,1,0:T(8,128)(2,1)} %copy-done.1, s16[1,2,1040,128]{3,2,1,0:T(8,128)(2,1)} %copy-done.8, ...), custom_call_target="tpu_custom_call", output_to_operand_aliasing={{}: (5, {})} | custom-call | bytes 2097152 | tf_op jit(solution)/shard_map/add_parts/pallas_call | solution.py:224
  (118 shorter events, 52.4 us)
Async XLA Ops:
  0.6 37.0 %collective-permute-start = (bf16[4096,128]{1,0:T(8,128)(2,1)}, bf16[4096,128]{1,0:T(8,128)(2,1)}, u32[]{:S(2)}, u32[]{:S(2)}) collective-permute-start(bf16[4096,128]{1,0:T(8,128)(2,1)} %refs_0_.5), channel_id=1, source_target_pairs={{0,2},{1,3},{2,4},{3,5},{4,6},{5,7},{6,0},{7,1},{8,10},{9,11},{10,... | collective-permute-start | bytes 3145736 | tf_op jit(solution)/shard_map/ppermute | solution.py:384
  3.7 34.0 %collective-permute-start.1 = (bf16[4096,128]{1,0:T(8,128)(2,1)}, bf16[4096,128]{1,0:T(8,128)(2,1)S(1)}, u32[]{:S(2)}, u32[]{:S(2)}) collective-permute-start(bf16[4096,128]{1,0:T(8,128)(2,1)} %refs_0_.5), channel_id=1, source_target_pairs={{0,1},{1,0},{2,3},{3,2},{4,5},{5,4},{6,7},{7,6},{8,9},{9,8},{10,11... | collective-permute-start | bytes 3145736 | tf_op jit(solution)/shard_map/ppermute | solution.py:381
  5.2 27.7 %collective-permute-start.2 = (bf16[1,64,1024]{2,1,0:T(8,128)(2,1)}, bf16[1,64,1024]{2,1,0:T(8,128)(2,1)S(1)}, u32[]{:S(2)}, u32[]{:S(2)}) collective-permute-start(bf16[1,64,1024]{2,1,0:T(8,128)(2,1)} %param.12), channel_id=1, source_target_pairs={{0,2},{1,3},{2,4},{3,5},{4,6},{5,7},{6,0},{7,1},{8,10},{9,11},{10,... | collective-permute-start | bytes 393224 | tf_op jit(solution)/shard_map/ppermute | solution.py:308
  6.8 30.9 %collective-permute-start.3 = (bf16[1,64,1024]{2,1,0:T(8,128)(2,1)}, bf16[1,64,1024]{2,1,0:T(8,128)(2,1)S(1)}, u32[]{:S(2)}, u32[]{:S(2)}) collective-permute-start(bf16[1,64,1024]{2,1,0:T(8,128)(2,1)} %param.12), channel_id=1, source_target_pairs={{0,4},{1,5},{2,6},{3,7},{4,0},{5,1},{6,2},{7,3},{8,12},{9,13},{10,... | collective-permute-start | bytes 393224 | tf_op jit(solution)/shard_map/ppermute | solution.py:308
  8.0 29.6 %collective-permute-start.4 = (bf16[1,64,1024]{2,1,0:T(8,128)(2,1)}, bf16[1,64,1024]{2,1,0:T(8,128)(2,1)S(1)}, u32[]{:S(2)}, u32[]{:S(2)}) collective-permute-start(bf16[1,64,1024]{2,1,0:T(8,128)(2,1)} %param.12), channel_id=1, source_target_pairs={{0,6},{1,7},{2,0},{3,1},{4,2},{5,3},{6,4},{7,5},{8,14},{9,15},{10,... | collective-permute-start | bytes 393224 | tf_op jit(solution)/shard_map/ppermute | solution.py:308
  38.6 54.2 %all-to-all-start = ((bf16[8,64,1024]{2,1,0:T(8,128)(2,1)}), bf16[8,64,1024]{2,1,0:T(8,128)(2,1)S(1)}, u32[]{:S(2)}, u32[]{:S(2)}) async-start(bf16[8,64,1024]{2,1,0:T(8,128)(2,1)} %cut_down.1), calls=%async_computation | async-start | bytes 2097152 | tf_op jit(solution)/shard_map/all_to_all | solution.py:421
  45.2 46.6 %collective-permute-start.5 = (bf16[4096,128]{1,0:T(8,128)(2,1)}, bf16[4096,128]{1,0:T(8,128)(2,1)S(1)}, u32[]{:S(2)}, u32[]{:S(2)}) collective-permute-start(bf16[4096,128]{1,0:T(8,128)(2,1)} %collective-permute-done.refs_2_), channel_id=1, source_target_pairs={{0,2},{1,3},{2,4},{3,5},{4,6},{5,7},{6,0},{7,1},{8,10},{9,11},{10,... | collective-permute-start | bytes 3145736 | tf_op jit(solution)/shard_map/ppermute | solution.py:384
  47.2 45.7 %collective-permute-start.6 = (bf16[4096,128]{1,0:T(8,128)(2,1)}, bf16[4096,128]{1,0:T(8,128)(2,1)}, u32[]{:S(2)}, u32[]{:S(2)}) collective-permute-start(bf16[4096,128]{1,0:T(8,128)(2,1)} %collective-permute-done.refs_2_), channel_id=1, source_target_pairs={{0,1},{1,0},{2,3},{3,2},{4,5},{5,4},{6,7},{7,6},{8,9},{9,8},{10,11... | collective-permute-start | bytes 3145736 | tf_op jit(solution)/shard_map/ppermute | solution.py:381
  48.8 45.1 %copy-start.23 = (s32[16]{0:T(128)S(1)}, s32[16]{0:T(128)}, u32[]{:S(2)}) copy-start(s32[16]{0:T(128)} %param.15) | copy-start | bytes 196
  48.8 42.9 %collective-permute-start.7 = (bf16[4,64,1024]{2,1,0:T(8,128)(2,1)S(1)}, bf16[4,64,1024]{2,1,0:T(8,128)(2,1)S(1)}, u32[]{:S(2)}, u32[]{:S(2)}) collective-permute-start(bf16[4,64,1024]{2,1,0:T(8,128)(2,1)S(1)} %pad_maximum_fusion), channel_id=1, source_target_pairs={{0,1},{1,0},{2,3},{3,2},{4,5},{5,4},{6,7},{7,6},{8,9},{9,8},{10,11... | collective-permute-start | bytes 1572872 | tf_op jit(solution)/shard_map/ppermute | solution.py:381
  92.9 4.9 %collective-permute-start.10 = (bf16[8,64,1024]{2,1,0:T(8,128)(2,1)S(1)}, bf16[8,64,1024]{2,1,0:T(8,128)(2,1)}, u32[]{:S(2)}, u32[]{:S(2)}) collective-permute-start(bf16[8,64,1024]{2,1,0:T(8,128)(2,1)S(1)} %all-to-all-done.refs_2_.near_ref), channel_id=1, source_target_pairs={{0,8},{8,0},{1,9},{9,1},{2,10},{10,2},{3,11},{11,3},{4,12},{12,4},... | collective-permute-start | bytes 3145736 | tf_op jit(solution)/shard_map/ppermute | solution.py:426
  92.9 4.8 %collective-permute-start.11 = (bf16[8,64,1024]{2,1,0:T(8,128)(2,1)S(1)}, bf16[8,64,1024]{2,1,0:T(8,128)(2,1)}, u32[]{:S(2)}, u32[]{:S(2)}) collective-permute-start(bf16[8,64,1024]{2,1,0:T(8,128)(2,1)S(1)} %constant_dynamic-update-slice_fusion.refs_4_.refs_9_), channel_id=1, source_target_pairs={{0,8},{8,0},{1,9},{9,1},{2,10},{10,2},{3,11},{11,3},{4,12},{12,4},... | collective-permute-start | bytes 3145736 | tf_op jit(solution)/shard_map/ppermute | solution.py:426
  94.5 27.3 %collective-permute-start.8 = (bf16[4096,128]{1,0:T(8,128)(2,1)}, bf16[4096,128]{1,0:T(8,128)(2,1)}, u32[]{:S(2)}, u32[]{:S(2)}) collective-permute-start(bf16[4096,128]{1,0:T(8,128)(2,1)} %copy-done.20), channel_id=1, source_target_pairs={{0,2},{1,3},{2,4},{3,5},{4,6},{5,7},{6,0},{7,1},{8,10},{9,11},{10,... | collective-permute-start | bytes 3145736 | tf_op jit(solution)/shard_map/ppermute | solution.py:384
  96.0 25.8 %collective-permute-start.9 = (bf16[4096,128]{1,0:T(8,128)(2,1)}, bf16[4096,128]{1,0:T(8,128)(2,1)}, u32[]{:S(2)}, u32[]{:S(2)}) collective-permute-start(bf16[4096,128]{1,0:T(8,128)(2,1)} %copy-done.20), channel_id=1, source_target_pairs={{0,1},{1,0},{2,3},{3,2},{4,5},{5,4},{6,7},{7,6},{8,9},{9,8},{10,11... | collective-permute-start | bytes 3145736 | tf_op jit(solution)/shard_map/ppermute | solution.py:381
  121.8 26.7 %collective-permute-start.13 = (s16[2,2,1040,128]{3,2,1,0:T(8,128)(2,1)}, s16[2,2,1040,128]{3,2,1,0:T(8,128)(2,1)S(1)}, u32[]{:S(2)}, u32[]{:S(2)}) collective-permute-start(s16[2,2,1040,128]{3,2,1,0:T(8,128)(2,1)} %add_parts.10), channel_id=1, source_target_pairs={{0,2},{1,3},{2,4},{3,5},{4,6},{5,7},{6,0},{7,1},{8,10},{9,11},{10,... | collective-permute-start | bytes 3194888 | tf_op jit(solution)/shard_map/ppermute | solution.py:384
  122.6 23.9 %collective-permute-start.12 = (bf16[4096,128]{1,0:T(8,128)(2,1)}, bf16[4096,128]{1,0:T(8,128)(2,1)S(1)}, u32[]{:S(2)}, u32[]{:S(2)}) collective-permute-start(bf16[4096,128]{1,0:T(8,128)(2,1)} %collective-permute-done.8.refs_6_), channel_id=1, source_target_pairs={{0,1},{1,0},{2,3},{3,2},{4,5},{5,4},{6,7},{7,6},{8,9},{9,8},{10,11... | collective-permute-start | bytes 3145736 | tf_op jit(solution)/shard_map/ppermute | solution.py:381
  148.5 15.1 %collective-permute-start.15 = (f32[32,4096]{1,0:T(8,128)}, f32[32,4096]{1,0:T(8,128)S(1)}, u32[]{:S(2)}, u32[]{:S(2)}) collective-permute-start(f32[32,4096]{1,0:T(8,128)} %get-tuple-element.89), channel_id=1, source_target_pairs={{0,1},{1,0},{2,3},{3,2},{4,5},{5,4},{6,7},{7,6},{8,9},{9,8},{10,11... | collective-permute-start | bytes 1572872 | tf_op jit(solution)/shard_map/ppermute | solution.py:381
  154.7 33.9 %collective-permute-start.16 = (s16[2,2,1040,128]{3,2,1,0:T(8,128)(2,1)}, s16[2,2,1040,128]{3,2,1,0:T(8,128)(2,1)S(1)}, u32[]{:S(2)}, u32[]{:S(2)}) collective-permute-start(s16[2,2,1040,128]{3,2,1,0:T(8,128)(2,1)} %add_parts.11), channel_id=1, source_target_pairs={{0,2},{1,3},{2,4},{3,5},{4,6},{5,7},{6,0},{7,1},{8,10},{9,11},{10,... | collective-permute-start | bytes 3194888 | tf_op jit(solution)/shard_map/ppermute | solution.py:384
  154.7 34.0 %collective-permute-start.14 = (s16[4,1,1040,128]{3,2,1,0:T(8,128)(2,1)}, s16[4,1,1040,128]{3,2,1,0:T(8,128)(2,1)S(1)}, u32[]{:S(2)}, u32[]{:S(2)}) collective-permute-start(s16[4,1,1040,128]{3,2,1,0:T(8,128)(2,1)} %get-tuple-element.83), channel_id=1, source_target_pairs={{0,1},{1,0},{2,3},{3,2},{4,5},{5,4},{6,7},{7,6},{8,9},{9,8},{10,11... | collective-permute-start | bytes 3194888 | tf_op jit(solution)/shard_map/ppermute | solution.py:381
  163.6 22.5 %collective-permute-start.17 = (f32[8,4096]{1,0:T(8,128)S(1)}, f32[8,4096]{1,0:T(8,128)S(1)}, u32[]{:S(2)}, u32[]{:S(2)}) collective-permute-start(f32[8,4096]{1,0:T(8,128)S(1)} %get-tuple-element.132), channel_id=1, source_target_pairs={{0,2},{1,3},{2,4},{3,5},{4,6},{5,7},{6,0},{7,1},{8,10},{9,11},{10,... | collective-permute-start | bytes 393224 | tf_op jit(solution)/shard_map/ppermute | solution.py:466
  163.7 24.9 %collective-permute-start.18 = (f32[8,4096]{1,0:T(8,128)S(1)}, f32[8,4096]{1,0:T(8,128)S(1)}, u32[]{:S(2)}, u32[]{:S(2)}) collective-permute-start(f32[8,4096]{1,0:T(8,128)S(1)} %get-tuple-element.131), channel_id=1, source_target_pairs={{0,4},{1,5},{2,6},{3,7},{4,0},{5,1},{6,2},{7,3},{8,12},{9,13},{10,... | collective-permute-start | bytes 393224 | tf_op jit(solution)/shard_map/ppermute | solution.py:466
  165.7 22.9 %collective-permute-start.19 = (f32[8,4096]{1,0:T(8,128)S(1)}, f32[8,4096]{1,0:T(8,128)S(1)}, u32[]{:S(2)}, u32[]{:S(2)}) collective-permute-start(f32[8,4096]{1,0:T(8,128)S(1)} %get-tuple-element.130), channel_id=1, source_target_pairs={{0,6},{1,7},{2,0},{3,1},{4,2},{5,3},{6,4},{7,5},{8,14},{9,15},{10,... | collective-permute-start | bytes 393224 | tf_op jit(solution)/shard_map/ppermute | solution.py:466
  189.6 20.1 %collective-permute-start.21 = (f32[8,64,1024]{2,1,0:T(8,128)}, f32[8,64,1024]{2,1,0:T(8,128)}, u32[]{:S(2)}, u32[]{:S(2)}) collective-permute-start(f32[8,64,1024]{2,1,0:T(8,128)} %get-tuple-element.99), channel_id=1, source_target_pairs={{0,8},{8,0},{1,9},{9,1},{2,10},{10,2},{3,11},{11,3},{4,12},{12,4},... | collective-permute-start | bytes 6291464 | tf_op jit(solution)/shard_map/ppermute | solution.py:530
  189.6 26.1 %collective-permute-start.20 = (s16[4,1,1040,128]{3,2,1,0:T(8,128)(2,1)}, s16[4,1,1040,128]{3,2,1,0:T(8,128)(2,1)S(1)}, u32[]{:S(2)}, u32[]{:S(2)}) collective-permute-start(s16[4,1,1040,128]{3,2,1,0:T(8,128)(2,1)} %get-tuple-element.97), channel_id=1, source_target_pairs={{0,1},{1,0},{2,3},{3,2},{4,5},{5,4},{6,7},{7,6},{8,9},{9,8},{10,11... | collective-permute-start | bytes 3194888 | tf_op jit(solution)/shard_map/ppermute | solution.py:381
  195.6 34.1 %collective-permute-start.25 = (s16[2,2,1040,128]{3,2,1,0:T(8,128)(2,1)}, s16[2,2,1040,128]{3,2,1,0:T(8,128)(2,1)S(1)}, u32[]{:S(2)}, u32[]{:S(2)}) collective-permute-start(s16[2,2,1040,128]{3,2,1,0:T(8,128)(2,1)} %add_parts.14), channel_id=1, source_target_pairs={{0,2},{1,3},{2,4},{3,5},{4,6},{5,7},{6,0},{7,1},{8,10},{9,11},{10,... | collective-permute-start | bytes 3194888 | tf_op jit(solution)/shard_map/ppermute | solution.py:384
  206.9 2.9 collective-permute-start.22
  209.5 20.1 %collective-permute-start.23 = (s16[1,1,1040,128]{3,2,1,0:T(8,128)(2,1)}, s16[1,1,1040,128]{3,2,1,0:T(8,128)(2,1)S(1)}, u32[]{:S(2)}, u32[]{:S(2)}) collective-permute-start(s16[1,1,1040,128]{3,2,1,0:T(8,128)(2,1)} %add_parts.12), channel_id=1, source_target_pairs={{0,2},{1,3},{2,4},{3,5},{4,6},{5,7},{6,0},{7,1},{8,10},{9,11},{10,... | collective-permute-start | bytes 798728 | tf_op jit(solution)/shard_map/ppermute | solution.py:384
  219.4 15.2 %collective-permute-start.24 = (s16[1,1,1040,128]{3,2,1,0:T(8,128)(2,1)}, s16[1,1,1040,128]{3,2,1,0:T(8,128)(2,1)S(1)}, u32[]{:S(2)}, u32[]{:S(2)}) collective-permute-start(s16[1,1,1040,128]{3,2,1,0:T(8,128)(2,1)} %add_parts.13), channel_id=1, source_target_pairs={{0,2},{1,3},{2,4},{3,5},{4,6},{5,7},{6,0},{7,1},{8,10},{9,11},{10,... | collective-permute-start | bytes 798728 | tf_op jit(solution)/shard_map/ppermute | solution.py:384
  235.3 52.1 %all-to-all-start.1 = ((s16[8,80,1024]{2,1,0:T(8,128)(2,1)}), s16[8,80,1024]{2,1,0:T(8,128)(2,1)S(1)}, u32[]{:S(2)}, u32[]{:S(2)}) async-start(s16[8,80,1024]{2,1,0:T(8,128)(2,1)} %pack_gradients.1), calls=%async_computation.1 | async-start | bytes 2621440 | tf_op jit(solution)/shard_map/all_to_all | solution.py:551
  242.5 32.9 %collective-permute-start.27 = (s16[1,2,1040,128]{3,2,1,0:T(8,128)(2,1)}, s16[1,2,1040,128]{3,2,1,0:T(8,128)(2,1)S(1)}, u32[]{:S(2)}, u32[]{:S(2)}) collective-permute-start(s16[1,2,1040,128]{3,2,1,0:T(8,128)(2,1)} %add_parts.16), channel_id=1, source_target_pairs={{0,2},{1,3},{2,4},{3,5},{4,6},{5,7},{6,0},{7,1},{8,10},{9,11},{10,... | collective-permute-start | bytes 1597448 | tf_op jit(solution)/shard_map/ppermute | solution.py:384
  247.3 28.1 %collective-permute-start.26 = (s16[1,2,1040,128]{3,2,1,0:T(8,128)(2,1)}, s16[1,2,1040,128]{3,2,1,0:T(8,128)(2,1)S(1)}, u32[]{:S(2)}, u32[]{:S(2)}) collective-permute-start(s16[1,2,1040,128]{3,2,1,0:T(8,128)(2,1)} %add_parts.15), channel_id=1, source_target_pairs={{0,1},{1,0},{2,3},{3,2},{4,5},{5,4},{6,7},{7,6},{8,9},{9,8},{10,11... | collective-permute-start | bytes 1597448 | tf_op jit(solution)/shard_map/ppermute | solution.py:381
  279.5 16.7 %collective-permute-start.28 = (s16[1,2,1040,128]{3,2,1,0:T(8,128)(2,1)}, s16[1,2,1040,128]{3,2,1,0:T(8,128)(2,1)S(1)}, u32[]{:S(2)}, u32[]{:S(2)}) collective-permute-start(s16[1,2,1040,128]{3,2,1,0:T(8,128)(2,1)} %add_parts.17), channel_id=1, source_target_pairs={{0,2},{1,3},{2,4},{3,5},{4,6},{5,7},{6,0},{7,1},{8,10},{9,11},{10,... | collective-permute-start | bytes 1597448 | tf_op jit(solution)/shard_map/ppermute | solution.py:384
  (23 other events, 172.5 us)
